TPU v7x, 512 devices: a whole 4x8x8 slice. The times are simulated.
512 devices in a mesh: row: 16 (over z_lo, y), col: 32 (over z_hi, x, core).
Axes of the slice: x: 4, y: 8, z: 8 (z_hi: 4, z_lo: 2; z = z_hi * 2 + z_lo), core: 2. Of those that a mesh axis runs over, the one named last changes fastest.
Arguments:
- tokens: bfloat16 [256, 8192], P('col', 'row'), may hold values from -500 to 500
- norm_gain: float32 [8192], P('row'), may hold values from 0.5 to 1.5
- cotangent: bfloat16 [256, 8192], P('col', 'row'), may hold values from -6 to 6
- gate_frozen_weight: bfloat16 [8192, 28672], P('row', 'col'), may hold values from -0.0625 to 0.0625
- up_frozen_weight: bfloat16 [8192, 28672], P('row', 'col'), may hold values from -0.0625 to 0.0625
- down_frozen_weight: bfloat16 [28672, 8192], P('col', 'row'), may hold values from -0.03125 to 0.03125
- gate_input_factor: bfloat16 [8192, 64], P('row'), may hold values from -0.0625 to 0.0625
- gate_output_factor: bfloat16 [64, 28672], P(None, 'col'), may hold values from -0.75 to 0.75
- up_input_factor: bfloat16 [8192, 64], P('row'), may hold values from -0.0625 to 0.0625
- up_output_factor: bfloat16 [64, 28672], P(None, 'col'), may hold values from -0.75 to 0.75
- down_input_factor: bfloat16 [28672, 64], P('col'), may hold values from -0.03125 to 0.03125
- down_b: bfloat16 [64, 8192], P(None, 'row'), may hold values from -0.75 to 0.75
- gate_input_factor_direction: bfloat16 [8192, 64], P('row'), may hold values from -0.0625 to 0.0625
- gate_output_factor_direction: bfloat16 [64, 28672], P(None, 'col'), may hold values from -0.75 to 0.75
- up_input_factor_direction: bfloat16 [8192, 64], P('row'), may hold values from -0.0625 to 0.0625
- up_output_factor_direction: bfloat16 [64, 28672], P(None, 'col'), may hold values from -0.75 to 0.75
- down_input_factor_direction: bfloat16 [28672, 64], P('col'), may hold values from -0.03125 to 0.03125
- down_b_dir: bfloat16 [64, 8192], P(None, 'row'), may hold values from -0.75 to 0.75
Outputs:
- normed_feature_adjoint: float32 [256, 8192], P('col', 'row')
- normed_feature_adjoint_direction: float32 [256, 8192], P('col', 'row')
- curvature_gate_input: float32 [8192, 64], P('row')
- curvature_gate_output: float32 [64, 28672], P(None, 'col')
- curvature_up_input: float32 [8192, 64], P('row')
- curvature_up_output: float32 [64, 28672], P(None, 'col')
- curvature_down_input: float32 [28672, 64], P('col')
- curvature_down_output: float32 [64, 8192], P(None, 'row')
All inputs are finite; a program needn't handle non-finite values.
Results may differ from a plain program's by a relative error of at most 0.024.
Values may be sent and summed in bfloat16 or wider, within the bound.
No kernel may reach another device: no remote copies, remote signals or barrier semaphores. Data moves between devices by JAX's collectives and lax.ppermute only.
A program may use at most 64 MiB of HBM per device.

v0:
```python
import jax
import jax.numpy as jnp
from jax import lax
from jax.sharding import Mesh
from jax.sharding import PartitionSpec as P

D = 8192
ROW = ("row_0", "row_1")


adapter_scale = 0.5
epsilon = 1e-05


def copy_for_each(array, axis):
    copies = jnp.broadcast_to(array, (lax.axis_size(axis), *array.shape))
    return lax.all_to_all(copies, axis, split_axis=0, concat_axis=0, tiled=True)


def taken_together(array, axis):
    everything = copy_for_each(array, axis)
    return jnp.sum(everything, axis=0)


def in_one_piece(arrays, axis, dim, along):
    widths = [a.shape[along] for a in arrays]
    both = jnp.concatenate(arrays, axis=along)
    filled = lax.all_gather(both, axis, axis=dim, tiled=True)
    return tuple(jnp.split(filled, [sum(widths[:k]) for k in range(1, len(widths))], axis=along))


def filled_up(lines, peers):
    spare = -len(lines) % peers
    return jnp.pad(lines, [(0, spare)] + [(0, 0)] * (lines.ndim - 1))


def joined_along(tiles, dim):
    tiles = jnp.moveaxis(tiles, 0, dim)
    lengths = tiles.shape
    return tiles.reshape(*lengths[:dim], lengths[dim] * lengths[dim + 1], *lengths[dim + 2 :])


def collect(array, axis, dim):
    tiles = copy_for_each(array, axis)
    return joined_along(tiles, dim)


def split_up(array, dim, peers):
    lengths = array.shape
    tiles = array.reshape(*lengths[:dim], peers, lengths[dim] // peers, *lengths[dim + 1 :])
    return jnp.moveaxis(tiles, dim, 0)


def sent_and_summed(array, axis, dim):
    tiles = split_up(array, dim, lax.axis_size(axis))
    arrived = lax.all_to_all(tiles, axis, split_axis=0, concat_axis=0, tiled=True)
    return arrived.sum(axis=0)


def total_of(array, axes):
    lines = array.reshape(-1, array.shape[-1])
    padded = filled_up(lines, lax.axis_size(axes))
    whole = collect(sent_and_summed(padded, axes, 0), axes, 0)
    return lax.slice_in_dim(whole, 0, len(lines)).reshape(array.shape)


def own_block(tiles, axes, order):
    lengths = [lax.axis_size(a) for a in axes]
    tiles = tiles.reshape(*lengths, *tiles.shape[1:])
    tiles = tiles.transpose(*order, *range(len(axes), tiles.ndim))
    tiles = tiles.reshape(-1, *tiles.shape[len(axes) :])
    for k in order:
        tiles = lax.psum_scatter(tiles, axes[k], scatter_dimension=0, tiled=True)
    return tiles[0]


def summed_rows(array, axes, order, dim):
    peers = lax.axis_size(axes)
    return own_block(split_up(array, dim, peers), axes, order)


def sum_at_owner(array, axis, dim):
    peers = lax.axis_size(axis)
    tiles = lax.all_to_all(split_up(array, dim, peers), axis, 0, 0, tiled=True)
    return jnp.sum(tiles.astype(jnp.float32), axis=0)


def nested_sum(array, axes):
    lines = array.reshape(-1, array.shape[-1])
    own = sum_at_owner(filled_up(lines, lax.axis_size(axes)), axes, 0)
    whole = collect(own.astype(jnp.bfloat16), axes, 0)
    return whole[: len(lines)].reshape(array.shape).astype(jnp.float32)


def curvature_product(left, right):
    return jnp.dot(left, right, preferred_element_type=jnp.float32)


def cross_shard_total(left, right):
    return lax.dot_general(
        left, right, (((1,), (1,)), ((), ())), preferred_element_type=jnp.float32
    )


def summed_over_rows(left, right):
    return lax.dot_general(
        left, right, (((0,), (0,)), ((), ())), preferred_element_type=jnp.float32
    )


def lowered(factor, panel):
    return lax.dot_general(
        factor, panel, (((0,), (1,)), ((), ())), preferred_element_type=jnp.float32
    )


def lifted(adjoint, factor):
    return lax.dot_general(
        adjoint, factor, (((0,), (1,)), ((), ())), precision=lax.Precision.HIGHEST
    )


def second_order(
    gate_preactivation,
    up_preactivation,
    hidden_adjoint,
    gate_tangent_rows,
    up_tangent_rows,
    adjoint_tangent_rows,
):
    sigma = jax.nn.sigmoid(gate_preactivation)
    silu_value = gate_preactivation * sigma
    slope = sigma * (1.0 + gate_preactivation * (1.0 - sigma))
    bend = sigma * (1.0 - sigma) * (2.0 + gate_preactivation * (1.0 - 2.0 * sigma))
    hidden_activation = (silu_value * up_preactivation).astype(jnp.bfloat16)
    hidden_direction = (
        slope * gate_tangent_rows * up_preactivation + silu_value * up_tangent_rows
    ).astype(jnp.bfloat16)
    gate_derivative = (hidden_adjoint * up_preactivation * slope).astype(jnp.bfloat16)
    up_derivative = (hidden_adjoint * silu_value).astype(jnp.bfloat16)
    gate_derivative_direction = (
        adjoint_tangent_rows * up_preactivation * slope
        + hidden_adjoint * (up_tangent_rows * slope + up_preactivation * bend * gate_tangent_rows)
    ).astype(jnp.bfloat16)
    up_derivative_direction = (
        adjoint_tangent_rows * silu_value + hidden_adjoint * slope * gate_tangent_rows
    ).astype(jnp.bfloat16)
    return (
        hidden_activation,
        hidden_direction,
        gate_derivative,
        up_derivative,
        gate_derivative_direction,
        up_derivative_direction,
    )


def on_device(
    tokens,
    norm_gain,
    cotangent,
    gate_frozen_weight,
    up_frozen_weight,
    down_frozen_weight,
    gate_input_factor,
    gate_output_factor,
    up_input_factor,
    up_output_factor,
    down_input_factor,
    down_b,
    gate_input_factor_direction,
    gate_output_factor_direction,
    up_input_factor_direction,
    up_output_factor_direction,
    down_input_factor_direction,
    down_b_dir,
):
    rank_size = gate_input_factor.shape[1]
    width_rows = gate_frozen_weight.shape[0]
    width_columns = gate_frozen_weight.shape[1]
    own_count = tokens.shape[0]
    tokens_f = tokens.astype(jnp.float32)
    squares = taken_together(jnp.sum(tokens_f * tokens_f, axis=1), ROW)
    own_normed = (tokens_f * lax.rsqrt(squares[:, None] / D + epsilon) * norm_gain).astype(
        jnp.bfloat16
    )
    normed_tokens, cot_panel = in_one_piece((own_normed, cotangent), "col", 0, 1)
    all_tokens = normed_tokens.shape[0]
    in_factors = jnp.concatenate(
        [
            gate_input_factor,
            up_input_factor,
            gate_input_factor_direction,
            up_input_factor_direction,
        ],
        axis=1,
    )
    out_factors = jnp.concatenate([down_b, down_b_dir], axis=0)
    projected = jnp.concatenate(
        [curvature_product(normed_tokens, in_factors), cross_shard_total(cot_panel, out_factors)],
        axis=1,
    )
    ranks = total_of(projected, ROW).astype(jnp.bfloat16)
    share = all_tokens // lax.axis_size(ROW)
    swiglu_block = summed_rows(
        jnp.concatenate(
            [
                curvature_product(normed_tokens, gate_frozen_weight),
                curvature_product(normed_tokens, up_frozen_weight),
                cross_shard_total(cot_panel, down_frozen_weight),
            ],
            axis=1,
        ),
        ROW,
        (1, 0),
        0,
    )
    local_ranks = lax.dynamic_slice_in_dim(ranks, lax.axis_index(ROW) * share, share, 0)

    def column(array, index):
        return array[:, index * rank_size : (index + 1) * rank_size]

    (
        gate_rank_rows,
        up_rank_rows,
        gate_rank_rows_direction,
        up_rank_rows_direction,
        adjoint_rank_rows,
        adjoint_rank_rows_direction,
    ) = [column(local_ranks, index) for index in range(6)]
    gate_preactivation = swiglu_block[:, :width_columns] + adapter_scale * curvature_product(
        gate_rank_rows, gate_output_factor
    )
    up_preactivation = swiglu_block[
        :, width_columns : 2 * width_columns
    ] + adapter_scale * curvature_product(up_rank_rows, up_output_factor)
    hidden_adjoint = swiglu_block[:, 2 * width_columns :] + adapter_scale * cross_shard_total(
        adjoint_rank_rows, down_input_factor
    )
    gate_tangent_rows = adapter_scale * (
        curvature_product(gate_rank_rows_direction, gate_output_factor)
        + curvature_product(gate_rank_rows, gate_output_factor_direction)
    )
    up_tangent_rows = adapter_scale * (
        curvature_product(up_rank_rows_direction, up_output_factor)
        + curvature_product(up_rank_rows, up_output_factor_direction)
    )
    adjoint_tangent_rows = adapter_scale * (
        cross_shard_total(adjoint_rank_rows_direction, down_input_factor)
        + cross_shard_total(adjoint_rank_rows, down_input_factor_direction)
    )
    (
        hidden_activation,
        hidden_direction,
        gate_derivative,
        up_derivative,
        gate_derivative_direction,
        up_derivative_direction,
    ) = second_order(
        gate_preactivation,
        up_preactivation,
        hidden_adjoint,
        gate_tangent_rows,
        up_tangent_rows,
        adjoint_tangent_rows,
    )
    (
        hidden_activation,
        hidden_direction,
        gate_derivative,
        up_derivative,
        gate_derivative_direction,
        up_derivative_direction,
    ) = in_one_piece(
        (
            hidden_activation,
            hidden_direction,
            gate_derivative,
            up_derivative,
            gate_derivative_direction,
            up_derivative_direction,
        ),
        ROW,
        0,
        1,
    )
    (
        gate_full_rows,
        up_full_rows,
        gate_full_rows_direction,
        up_full_rows_direction,
        adjoint_full_rows,
        adjoint_full_rows_direction,
    ) = [column(ranks, index) for index in range(6)]
    curvature_gate_output = adapter_scale * (
        summed_over_rows(gate_full_rows_direction, gate_derivative)
        + summed_over_rows(gate_full_rows, gate_derivative_direction)
    )
    curvature_up_output = adapter_scale * (
        summed_over_rows(up_full_rows_direction, up_derivative)
        + summed_over_rows(up_full_rows, up_derivative_direction)
    )
    curvature_down_input = adapter_scale * (
        summed_over_rows(hidden_direction, adjoint_full_rows)
        + summed_over_rows(hidden_activation, adjoint_full_rows_direction)
    )
    rank_adjoints = jnp.concatenate(
        [
            cross_shard_total(gate_output_factor, gate_derivative),
            cross_shard_total(up_output_factor, up_derivative),
            cross_shard_total(gate_output_factor, gate_derivative_direction)
            + cross_shard_total(gate_output_factor_direction, gate_derivative),
            cross_shard_total(up_output_factor, up_derivative_direction)
            + cross_shard_total(up_output_factor_direction, up_derivative),
            lowered(down_input_factor, hidden_direction)
            + lowered(down_input_factor_direction, hidden_activation),
        ],
        axis=0,
    )
    factors_f = [
        factor.astype(jnp.float32)
        for factor in (
            gate_input_factor,
            up_input_factor,
            gate_input_factor_direction,
            up_input_factor_direction,
        )
    ]
    normed_f = normed_tokens.astype(jnp.float32)
    cotangent_float = cot_panel.astype(jnp.float32)
    adjoints = nested_sum(rank_adjoints.astype(jnp.bfloat16), "col")
    adjoint_contribution = cross_shard_total(
        gate_derivative, gate_frozen_weight
    ) + cross_shard_total(up_derivative, up_frozen_weight)
    tangent_contribution = cross_shard_total(
        gate_derivative_direction, gate_frozen_weight
    ) + cross_shard_total(up_derivative_direction, up_frozen_weight)
    adjoint_contribution, tangent_contribution = (adjoint_contribution, tangent_contribution)
    summed = sum_at_owner(
        jnp.concatenate([adjoint_contribution, tangent_contribution], axis=1).astype(jnp.bfloat16),
        "col",
        0,
    )
    normed_feature_adjoint = summed[:, :width_rows]
    normed_feature_adjoint_direction = summed[:, width_rows:]
    piece = lax.dynamic_slice_in_dim(adjoints, lax.axis_index("col") * own_count, own_count, 1)
    parts = [piece[index * rank_size : (index + 1) * rank_size] for index in range(5)]
    adjoint_contribution = lifted(parts[0], factors_f[0]) + lifted(parts[1], factors_f[1])
    tangent_contribution = (
        lifted(parts[2], factors_f[0])
        + lifted(parts[0], factors_f[2])
        + lifted(parts[3], factors_f[1])
        + lifted(parts[1], factors_f[3])
    )
    normed_feature_adjoint = normed_feature_adjoint + adapter_scale * adjoint_contribution
    normed_feature_adjoint_direction = (
        normed_feature_adjoint_direction + adapter_scale * tangent_contribution
    )
    spread = (((0,), (1,)), ((), ()))
    gate_dir_rows = adjoints[2 * rank_size : 3 * rank_size]
    up_dir_rows = adjoints[3 * rank_size : 4 * rank_size]
    rank_row_values = adjoints[4 * rank_size : 5 * rank_size]
    gate_contribution = adapter_scale * lax.dot_general(
        normed_f, gate_dir_rows, spread, precision=lax.Precision.HIGHEST
    )
    up_contribution = adapter_scale * lax.dot_general(
        normed_f, up_dir_rows, spread, precision=lax.Precision.HIGHEST
    )
    down_contribution = adapter_scale * jnp.dot(
        rank_row_values, cotangent_float, precision=lax.Precision.HIGHEST
    )
    return (
        normed_feature_adjoint,
        normed_feature_adjoint_direction,
        gate_contribution,
        curvature_gate_output,
        up_contribution,
        curvature_up_output,
        curvature_down_input,
        down_contribution,
    )


def solution(mesh):
    split = Mesh(mesh.devices.reshape(2, 8, mesh.shape["col"]), ("row_0", "row_1", "col"))
    return jax.shard_map(
        on_device,
        mesh=split,
        in_specs=(
            P("col", ROW),
            P(ROW),
            P("col", ROW),
            P(ROW, "col"),
            P(ROW, "col"),
            P("col", ROW),
            P(ROW, None),
            P(None, "col"),
            P(ROW, None),
            P(None, "col"),
            P("col", None),
            P(None, ROW),
            P(ROW, None),
            P(None, "col"),
            P(ROW, None),
            P(None, "col"),
            P("col", None),
            P(None, ROW),
        ),
        out_specs=(
            P("col", ROW),
            P("col", ROW),
            P(ROW, None),
            P(None, "col"),
            P(ROW, None),
            P(None, "col"),
            P("col", None),
            P(None, ROW),
        ),
        check_vma=False,
    )
```

profile of v0, /device:TPU:1, one launch (start us, length us, event | category | flops | bytes accessed | tf_op | source)
XLA Modules:
  0.0 310.4 jit_solution(14303357313274765809)
XLA Ops:
  8.2 16.7 %all_to_all.31 = f32[16,1,8]{2,1,0:T(1,128)S(1)} all-to-all(f32[16,1,8]{2,1,0:T(1,128)S(1)} %broadcast_in_dim.11), channel_id=1, replica_groups=mesh['row_0'=2,'row_1'=8,'col'=32] {'row_0','row_1'}, dimensions={0} | all-to-all | bytes 1024 | tf_op jit(solution)/shard_map/all_to_all | solution.py:17
  26.4 52.8 %all_gather.6 = bf16[256,1024]{1,0:T(8,128)(2,1)S(1)} all-gather(bf16[8,1024]{1,0:T(8,128)(2,1)S(1)} %pad_maximum_fusion.3), channel_id=1, replica_groups=mesh['row_0'=2,'row_1'=8,'col'=32] {'col'}, dimensions={0}, use_global_device_ids=true | all-gather | bytes 540672 | tf_op jit(solution)/shard_map/all_gather | solution.py:28
  79.1 1.6 fusion.67
  81.9 1.8 copy.32
  85.3 20.4 %all_to_all.32 = f32[16,16,384]{2,1,0:T(8,128)S(1)} all-to-all(f32[16,16,384]{2,1,0:T(8,128)S(1)} %bitcast.78), channel_id=1, replica_groups=mesh['row_0'=2,'row_1'=8,'col'=32] {'row_0','row_1'}, dimensions={0} | all-to-all | bytes 786432 | tf_op jit(solution)/shard_map/all_to_all | solution.py:56
  106.5 4.2 %all-to-all-start.2 = ((bf16[16,16,384]{2,1,0:T(8,128)(2,1)}), bf16[16,16,384]{2,1,0:T(8,128)(2,1)S(1)}, u32[]{:S(2)}, u32[]{:S(2)}) async-start(bf16[16,16,384]{2,1,0:T(8,128)(2,1)} %broadcast_in_dim.12), calls=%async_computation.4 | async-start | bytes 393216 | tf_op jit(solution)/shard_map/all_to_all | solution.py:17
  110.7 17.5 %reduce-scatter.3.cloned.1.call-done = f32[2,16,2688]{2,1,0:T(8,128)} async-done(((f32[16,16,2688]{2,1,0:T(8,128)}), f32[2,16,2688]{2,1,0:T(8,128)}) %reduce-scatter.3.cloned.1.call-update) | async-done | bytes 344080 | tf_op jit(solution)/shard_map/reduce_scatter | solution.py:73
  128.4 1.7 fusion.117
  130.1 1.7 fusion.115
  132.9 15.4 %reduce-scatter.5.cloned.1.call-done = f32[1,16,2688]{2,1,0:T(8,128)} async-done(((f32[2,16,2688]{2,1,0:T(8,128)}), f32[1,16,2688]{2,1,0:T(8,128)}) %reduce-scatter.5.cloned.1.call-update) | async-done | bytes 172048 | tf_op jit(solution)/shard_map/reduce_scatter | solution.py:73
  154.4 67.2 %all-gather.2.cloned.1.call-done = bf16[256,5376]{1,0:T(8,128)(2,1)} async-done(((bf16[16,5376]{1,0:T(8,128)(2,1)}), bf16[256,5376]{1,0:T(8,128)(2,1)}) %all-gather.2.cloned.1.call-update) | async-done | bytes 2752528 | tf_op jit(solution)/shard_map/all_gather | solution.py:28
  221.6 1.4 fusion.23
  223.0 1.3 fusion.41
  224.3 1.3 fusion.37
  225.6 1.3 fusion.34
  230.7 19.5 %all-to-all-start.4 = ((bf16[32,10,256]{2,1,0:T(8,128)(2,1)}), bf16[32,10,256]{2,1,0:T(8,128)(2,1)S(1)}, u32[]{:S(2)}, u32[]{:S(2)}) async-start(bf16[32,10,256]{2,1,0:T(8,128)(2,1)} %convert_element_type.60), calls=%async_computation.6 | async-start | bytes 524288 | tf_op jit(solution)/shard_map/all_to_all | solution.py:84
  250.2 1.6 fusion.43
  251.9 1.5 fusion.54
  257.7 6.2 %all-to-all-done.4 = bf16[32,10,256]{2,1,0:T(8,128)(2,1)S(1)} async-done(((bf16[32,10,256]{2,1,0:T(8,128)(2,1)}), bf16[32,10,256]{2,1,0:T(8,128)(2,1)S(1)}, u32[]{:S(2)}, u32[]{:S(2)}) %all-to-all-start.4) | async-done | bytes 163872 | tf_op jit(solution)/shard_map/all_to_all | solution.py:84
  264.6 3.7 %all-to-all-start.5 = ((bf16[32,10,256]{2,1,0:T(8,128)(2,1)}), bf16[32,10,256]{2,1,0:T(8,128)(2,1)S(1)}, u32[]{:S(2)}, u32[]{:S(2)}) async-start(bf16[32,10,256]{2,1,0:T(8,128)(2,1)} %broadcast_in_dim.13), calls=%async_computation.7 | async-start | bytes 524288 | tf_op jit(solution)/shard_map/all_to_all | solution.py:17
  269.2 2.0 fusion.4
  271.2 10.7 %all-to-all-done.5 = bf16[32,10,256]{2,1,0:T(8,128)(2,1)S(1)} async-done(((bf16[32,10,256]{2,1,0:T(8,128)(2,1)}), bf16[32,10,256]{2,1,0:T(8,128)(2,1)S(1)}, u32[]{:S(2)}, u32[]{:S(2)}) %all-to-all-start.5) | async-done | bytes 163872 | tf_op jit(solution)/shard_map/all_to_all | solution.py:17
  281.9 3.7 %all-to-all-start.3 = ((bf16[32,8,1024]{2,1,0:T(8,128)(2,1)}), bf16[32,8,1024]{2,1,0:T(8,128)(2,1)S(1)}, u32[]{:S(2)}, u32[]{:S(2)}) async-start(bf16[32,8,1024]{2,1,0:T(8,128)(2,1)} %pad_maximum_fusion.1), calls=%async_computation.5 | async-start | bytes 1048576 | tf_op jit(solution)/shard_map/all_to_all | solution.py:84
  289.2 12.9 %all-to-all-done.3 = bf16[32,8,1024]{2,1,0:T(8,128)(2,1)S(1)} async-done(((bf16[32,8,1024]{2,1,0:T(8,128)(2,1)}), bf16[32,8,1024]{2,1,0:T(8,128)(2,1)S(1)}, u32[]{:S(2)}, u32[]{:S(2)}) %all-to-all-start.3) | async-done | bytes 524320 | tf_op jit(solution)/shard_map/all_to_all | solution.py:84
  (91 shorter events, 28.2 us)
Async XLA Ops:
  7.2 74.1 %copy-start = (bf16[512,896]{1,0:T(8,128)(2,1)S(1)}, bf16[512,896]{1,0:T(8,128)(2,1)}, u32[]{:S(2)}) copy-start(bf16[512,896]{1,0:T(8,128)(2,1)} %param.21) | copy-start | bytes 2752516
  7.2 73.6 %copy-start.1 = (bf16[512,896]{1,0:T(8,128)(2,1)S(1)}, bf16[512,896]{1,0:T(8,128)(2,1)}, u32[]{:S(2)}) copy-start(bf16[512,896]{1,0:T(8,128)(2,1)} %param.22) | copy-start | bytes 2752516
  7.2 121.0 %reduce-scatter.3.cloned.1.call-start = ((), (), s32[]{:S(2)}) async-start(), calls=%async_computation.8 | async-start | bytes 3096576 | tf_op jit(solution)/shard_map/reduce_scatter | solution.py:73
  83.7 0.8 copy-start.15
  83.7 0.9 copy-start.16
  83.7 1.1 copy-start.6
  83.7 1.1 copy-start.7
  83.7 1.1 copy-start.12
  83.7 1.1 copy-start.13
  84.5 43.7 %copy-start.5 = (bf16[64,896]{1,0:T(8,128)(2,1)S(1)}, bf16[64,896]{1,0:T(8,128)(2,1)}, u32[]{:S(2)}) copy-start(bf16[64,896]{1,0:T(8,128)(2,1)} %param.25) | copy-start | bytes 344068
  106.5 117.9 %copy-start.11 = (bf16[64,896]{1,0:T(8,128)(2,1)S(1)}, bf16[64,896]{1,0:T(8,128)(2,1)}, u32[]{:S(2)}) copy-start(bf16[64,896]{1,0:T(8,128)(2,1)} %param.27) | copy-start | bytes 344068
  106.5 21.8 %all-to-all-start.2 = ((bf16[16,16,384]{2,1,0:T(8,128)(2,1)}), bf16[16,16,384]{2,1,0:T(8,128)(2,1)S(1)}, u32[]{:S(2)}, u32[]{:S(2)}) async-start(bf16[16,16,384]{2,1,0:T(8,128)(2,1)} %broadcast_in_dim.12), calls=%async_computation.4 | async-start | bytes 393216 | tf_op jit(solution)/shard_map/all_to_all | solution.py:17
  110.7 37.6 %reduce-scatter.5.cloned.1.call-start = ((), (), s32[]{:S(2)}) async-start(), calls=%async_computation.9 | async-start | bytes 516096 | tf_op jit(solution)/shard_map/reduce_scatter | solution.py:73
  128.2 93.4 %all-gather.2.cloned.1.call-start = ((), (), s32[]{:S(2)}) async-start(), calls=%async_computation.10 | async-start | bytes 2924544 | tf_op jit(solution)/shard_map/all_gather | solution.py:28
  128.3 97.4 %copy-start.10 = (bf16[896,64]{0,1:T(8,128)(2,1)S(1)}, bf16[896,64]{0,1:T(8,128)(2,1)}, u32[]{:S(2)}) copy-start(bf16[896,64]{0,1:T(8,128)(2,1)} %param.28) | copy-start | bytes 344068
  150.3 76.9 %copy-start.9 = (bf16[64,896]{1,0:T(8,128)(2,1)S(1)}, bf16[64,896]{1,0:T(8,128)(2,1)}, u32[]{:S(2)}) copy-start(bf16[64,896]{1,0:T(8,128)(2,1)} %param.31) | copy-start | bytes 344068
  153.7 0.7 copy-start.8
  221.6 5.4 %copy-start.2 = (bf16[256,5376]{1,0:T(8,128)(2,1)S(1)}, bf16[256,5376]{1,0:T(8,128)(2,1)}, u32[]{:S(2)}) copy-start(bf16[256,5376]{1,0:T(8,128)(2,1)} %all-gather.2.cloned.1.call-done) | copy-start | bytes 8257540
  230.7 33.2 %all-to-all-start.4 = ((bf16[32,10,256]{2,1,0:T(8,128)(2,1)}), bf16[32,10,256]{2,1,0:T(8,128)(2,1)S(1)}, u32[]{:S(2)}, u32[]{:S(2)}) async-start(bf16[32,10,256]{2,1,0:T(8,128)(2,1)} %convert_element_type.60), calls=%async_computation.6 | async-start | bytes 524288 | tf_op jit(solution)/shard_map/all_to_all | solution.py:84
  250.2 3.1 %copy-start.3 = (bf16[256,5376]{1,0:T(8,128)(2,1)S(1)}, bf16[256,5376]{1,0:T(8,128)(2,1)}, u32[]{:S(2)}) copy-start(bf16[256,5376]{1,0:T(8,128)(2,1)} %all-gather.2.cloned.1.call-done) | copy-start | bytes 8257540
  256.7 12.5 %copy-start.4 = (f32[896,64]{0,1:T(8,128)S(1)}, f32[896,64]{0,1:T(8,128)}, u32[]{:S(2)}) copy-start(f32[896,64]{0,1:T(8,128)} %fusion.32) | copy-start | bytes 688132
  264.6 17.3 %all-to-all-start.5 = ((bf16[32,10,256]{2,1,0:T(8,128)(2,1)}), bf16[32,10,256]{2,1,0:T(8,128)(2,1)S(1)}, u32[]{:S(2)}, u32[]{:S(2)}) async-start(bf16[32,10,256]{2,1,0:T(8,128)(2,1)} %broadcast_in_dim.13), calls=%async_computation.7 | async-start | bytes 524288 | tf_op jit(solution)/shard_map/all_to_all | solution.py:17
  268.3 34.7 %copy-start.14 = (bf16[512,64]{0,1:T(8,128)(2,1)S(1)}, bf16[512,64]{0,1:T(8,128)(2,1)}, u32[]{:S(2)}) copy-start(bf16[512,64]{0,1:T(8,128)(2,1)} %param.32) | copy-start | bytes 196612
  281.9 20.1 %all-to-all-start.3 = ((bf16[32,8,1024]{2,1,0:T(8,128)(2,1)}), bf16[32,8,1024]{2,1,0:T(8,128)(2,1)S(1)}, u32[]{:S(2)}, u32[]{:S(2)}) async-start(bf16[32,8,1024]{2,1,0:T(8,128)(2,1)} %pad_maximum_fusion.1), calls=%async_computation.5 | async-start | bytes 1048576 | tf_op jit(solution)/shard_map/all_to_all | solution.py:84
Sparse Core Ops, SparseCore 0:
  83.8 44.2 reduce-scatter.2
  131.2 17.0 reduce-scatter.4
  154.5 67.0 all-gather.1
where the time goes:
time: 312 us; the launch traced here: 310 us
  waiting for transfers between devices  130 us (42%)
  blocking collectives  89.9 us (29%)
  matrix products  35.8 us (11%)
  starting transfers between devices  31.2 us (10%)
  between operations  14.2 us (5%)
  local copies, waits for them, and re-layouts  5.75 us (2%)
  other arithmetic  3.79 us (1%)
    all_gather x1, waiting for transfers between devices, in_one_piece(): filled = lax.all_gather(both, axis, axis=dim, tiled=True)  67.2 us
    all_gather x1, blocking collectives, in_one_piece(): filled = lax.all_gather(both, axis, axis=dim, tiled=True)  52.8 us
    reduce_scatter x2, waiting for transfers between devices, own_block(): tiles = lax.psum_scatter(tiles, axes[k], scatter_dimension=0, tiled=True)  32.8 us
    all_to_all x2, starting transfers between devices, sum_at_owner(): tiles = lax.all_to_all(split_up(array, dim, peers), axis, 0, 0, tiled=True)  23.2 us
    all_to_all x1, blocking collectives, sent_and_summed(): lax.all_to_all(tiles, axis, split_axis=0, concat_axis=0, tiled=True)  20.4 us
    all_to_all x2, waiting for transfers between devices, sum_at_owner(): tiles = lax.all_to_all(split_up(array, dim, peers), axis, 0, 0, tiled=True)  19 us
    all_to_all x1, blocking collectives, copy_for_each(): return lax.all_to_all(copies, axis, split_axis=0, concat_axis=0, tiled=True)  16.7 us
    dot_general x15, matrix products, cross_shard_total(): lax.dot_general(left, right, (((1,), (1,)), ((), ())), preferred_element_...  15.5 us
  transfers between devices with their start and end apart: 7, of which 6 were waited for; matrix products, arithmetic and copies ran while one was open for 6% of the time, Pallas kernels for 0%

commit v1 on v0

v1 whole, which is shorter than its diff:
```python
import jax
import jax.numpy as jnp
from jax import lax
from jax.sharding import Mesh
from jax.sharding import PartitionSpec as P

D = 8192
ROW = ("zl", "y")
CHIPS = ("zh", "x")
COL = ("zh", "x", "core")
SCALE = 0.5
EPSILON = 1e-05
BF = jnp.bfloat16
F32 = jnp.float32


def nn(left, right):
    return lax.dot_general(left, right, (((1,), (0,)), ((), ())), preferred_element_type=F32)


def nt(left, right):
    return lax.dot_general(left, right, (((1,), (1,)), ((), ())), preferred_element_type=F32)


def tn(left, right):
    return lax.dot_general(left, right, (((0,), (0,)), ((), ())), preferred_element_type=F32)


def spread(array, axis):
    peers = lax.axis_size(axis)
    copies = jnp.broadcast_to(array, (peers, *array.shape))
    return lax.all_to_all(copies, axis, 0, 0, tiled=True).reshape(-1, *array.shape[1:])


def reduced(array, axis):
    peers = lax.axis_size(axis)
    tiles = array.reshape(peers, array.shape[0] // peers, *array.shape[1:])
    return jnp.sum(lax.all_to_all(tiles, axis, 0, 0, tiled=True).astype(F32), axis=0)


def halves(value):
    high = value.astype(BF)
    low = (value - high.astype(F32)).astype(BF)
    return jnp.pad(jnp.concatenate([high, low], axis=1), ((0, 0), (0, 126)))


def on_device(
    tokens,
    norm_gain,
    cotangent,
    gate_w,
    up_w,
    down_w,
    gate_in,
    gate_out,
    up_in,
    up_out,
    down_in,
    down_b,
    gate_in_dir,
    gate_out_dir,
    up_in_dir,
    up_out_dir,
    down_in_dir,
    down_b_dir,
):
    rank = gate_in.shape[1]
    rows = gate_w.shape[0]
    cols = gate_w.shape[1]
    own = jnp.concatenate([tokens, cotangent], axis=1)
    panel = spread(spread(own, CHIPS), "core")
    tokens_all, cot = panel[:, :rows], panel[:, rows:]
    tokens_f = tokens_all.astype(F32)
    squares = jnp.sum(tokens_f * tokens_f, axis=1, keepdims=True)
    scaled = (tokens_f * norm_gain).astype(BF)
    in_factors = jnp.concatenate([gate_in, up_in, gate_in_dir, up_in_dir], axis=1)
    b_factors = jnp.concatenate([down_b, down_b_dir], axis=0)
    partial = jnp.concatenate(
        [
            nn(scaled, gate_w).astype(BF),
            nn(scaled, up_w).astype(BF),
            nt(cot, down_w).astype(BF),
            nn(scaled, in_factors).astype(BF),
            nt(cot, b_factors).astype(BF),
            halves(squares),
        ],
        axis=1,
    )
    mine = reduced(partial, ROW)
    at = 3 * cols + 6 * rank
    inv_rms = lax.rsqrt((mine[:, at : at + 1] + mine[:, at + 1 : at + 2]) / D + EPSILON)
    mine = jnp.concatenate(
        [
            (mine[:, : 2 * cols] * inv_rms).astype(BF),
            mine[:, 2 * cols : 3 * cols].astype(BF),
            (mine[:, 3 * cols : 3 * cols + 4 * rank] * inv_rms).astype(BF),
            mine[:, 3 * cols + 4 * rank : at].astype(BF),
            halves(inv_rms),
        ],
        axis=1,
    )
    full = spread(spread(mine, "y"), "zl")
    inv_all = full[:, at : at + 1].astype(F32) + full[:, at + 1 : at + 2].astype(F32)
    low = full[:, 3 * cols : at]
    gate_low, up_low, gate_low_dir, up_low_dir, adj_low, adj_low_dir = [
        low[:, k * rank : (k + 1) * rank] for k in range(6)
    ]
    gate_pre = full[:, :cols].astype(F32) + SCALE * nn(gate_low, gate_out)
    up_pre = full[:, cols : 2 * cols].astype(F32) + SCALE * nn(up_low, up_out)
    hidden_adj = full[:, 2 * cols : 3 * cols].astype(F32) + SCALE * nt(adj_low, down_in)
    gate_tan = SCALE * (nn(gate_low_dir, gate_out) + nn(gate_low, gate_out_dir))
    up_tan = SCALE * (nn(up_low_dir, up_out) + nn(up_low, up_out_dir))
    adj_tan = SCALE * (nt(adj_low_dir, down_in) + nt(adj_low, down_in_dir))
    sig = jax.nn.sigmoid(gate_pre)
    act = gate_pre * sig
    slope = sig * (1.0 + gate_pre * (1.0 - sig))
    bend = sig * (1.0 - sig) * (2.0 + gate_pre * (1.0 - 2.0 * sig))
    hidden = (act * up_pre).astype(BF)
    hidden_dir = (slope * gate_tan * up_pre + act * up_tan).astype(BF)
    d_gate = (hidden_adj * up_pre * slope).astype(BF)
    d_up = (hidden_adj * act).astype(BF)
    d_gate_dir = (
        adj_tan * up_pre * slope + hidden_adj * (up_tan * slope + up_pre * bend * gate_tan)
    ).astype(BF)
    d_up_dir = (adj_tan * act + hidden_adj * slope * gate_tan).astype(BF)

    quotients = jnp.concatenate(
        [
            nt(d_gate, gate_out),
            nt(d_up, up_out),
            nt(d_gate_dir, gate_out) + nt(d_gate, gate_out_dir),
            nt(d_up_dir, up_out) + nt(d_up, up_out_dir),
            nn(hidden_dir, down_in) + nn(hidden, down_in_dir),
        ],
        axis=1,
    )
    back = jnp.concatenate(
        [
            (nt(d_gate, gate_w) + nt(d_up, up_w)).astype(BF),
            (nt(d_gate_dir, gate_w) + nt(d_up_dir, up_w)).astype(BF),
            jnp.pad(quotients.astype(BF), ((0, 0), (0, rank))),
        ],
        axis=1,
    )
    got = reduced(reduced(back, "core").astype(BF), CHIPS)
    q = got[:, 2 * rows : 2 * rows + 5 * rank]
    q_all = spread(spread(q[:, 2 * rank :].astype(BF), CHIPS), "core").astype(F32)

    curv_gate_out = SCALE * (tn(gate_low_dir, d_gate) + tn(gate_low, d_gate_dir))
    curv_up_out = SCALE * (tn(up_low_dir, d_up) + tn(up_low, d_up_dir))
    curv_down_in = SCALE * (tn(hidden_dir, adj_low) + tn(hidden, adj_low_dir))

    q_gate, q_up, q_gate_dir, q_up_dir = [
        q[:, k * rank : (k + 1) * rank].astype(BF) for k in range(4)
    ]
    adjoint = got[:, :rows] + SCALE * (nt(q_gate, gate_in) + nt(q_up, up_in))
    adjoint_dir = got[:, rows : 2 * rows] + SCALE * (
        nt(q_gate_dir, gate_in)
        + nt(q_gate, gate_in_dir)
        + nt(q_up_dir, up_in)
        + nt(q_up, up_in_dir)
    )
    curv_in = SCALE * tn(scaled, (q_all[:, : 2 * rank] * inv_all).astype(BF))
    curv_down_out = SCALE * tn(q_all[:, 2 * rank :].astype(BF), cot)
    return (
        adjoint,
        adjoint_dir,
        curv_in[:, :rank],
        curv_gate_out,
        curv_in[:, rank:],
        curv_up_out,
        curv_down_in,
        curv_down_out,
    )


def solution(mesh):
    split = Mesh(mesh.devices.reshape(2, 8, 4, 4, 2), ("zl", "y", "zh", "x", "core"))
    features = P(ROW, None)
    hidden = P(None, COL)
    return jax.shard_map(
        on_device,
        mesh=split,
        in_specs=(
            P(COL, ROW),
            P(ROW),
            P(COL, ROW),
            P(ROW, COL),
            P(ROW, COL),
            P(COL, ROW),
            features,
            hidden,
            features,
            hidden,
            P(COL, None),
            P(None, ROW),
            features,
            hidden,
            features,
            hidden,
            P(COL, None),
            P(None, ROW),
        ),
        out_specs=(
            P(COL, ROW),
            P(COL, ROW),
            features,
            hidden,
            features,
            hidden,
            P(COL, None),
            P(None, ROW),
        ),
        check_vma=False,
    )
```

time: 312 us -> 199 us (0.64)
  waiting for transfers between devices: 130 us -> 17.5 us
  blocking collectives: 89.9 us -> 137 us
  starting transfers between devices: 31.2 us -> 9.31 us
  matrix products: 35.8 us -> 22.5 us
  between operations: 14.2 us -> 1.19 us
    all_to_all x2 -> x7, blocking collectives: 37.1 us -> 137 us  [the longest x5 81.1 us: spread(): lax.all_to_all(copies, axis, 0, 0, tiled=True).reshape(-1, *array.shape[1:])]
    all_gather x1 -> x0, waiting for transfers between devices: 67.2 us -> none  [in_one_piece(): filled = lax.all_gather(both, axis, axis=dim, tiled=True)]
    all_gather x1 -> x0, blocking collectives: 52.8 us -> none  [in_one_piece(): filled = lax.all_gather(both, axis, axis=dim, tiled=True)]
    reduce_scatter x2 -> x0, waiting for transfers between devices: 32.8 us -> none  [own_block(): tiles = lax.psum_scatter(tiles, axes[k], scatter_dimension=0, tiled=True)]
    all_to_all x4 -> x2, starting transfers between devices: 31 us -> 9.31 us  [the longest x1 5.1 us: spread(): lax.all_to_all(copies, axis, 0, 0, tiled=True).reshape(-1, *array.shape[1:])]
    dot_general x41 -> x40, matrix products: 35.8 us -> 22.5 us  [the longest x21 11 us: nt(): lax.dot_general(left, right, (((1,), (1,)), ((), ())), preferred_element_...]
    all_to_all x4 -> x2, waiting for transfers between devices: 29.8 us -> 17.5 us  [the longest x1 10.3 us: reduced(): lax.all_to_all(tiles, axis, 0, 0, tiled=True).astype(F32)]
  transfers between devices with their start and end apart: 7 -> 2, of which waited for: 6 -> 2; matrix products, arithmetic and copies ran while one was open for 6% -> 3% of each run, Pallas kernels for 0% -> 0%
where the time goes in v1:
time: 199 us
  blocking collectives  137 us (69%)
  matrix products  22.5 us (11%)
  waiting for transfers between devices  17.5 us (9%)
  starting transfers between devices  9.31 us (5%)
  other arithmetic  5.86 us (3%)
  local copies, waits for them, and re-layouts  5.12 us (3%)
    all_to_all x5, blocking collectives, spread(): lax.all_to_all(copies, axis, 0, 0, tiled=True).reshape(-1, *array.shape[1:])  81.1 us
    all_to_all x2, blocking collectives, reduced(): lax.all_to_all(tiles, axis, 0, 0, tiled=True).astype(F32)  56.1 us
    dot_general x21, matrix products, nt(): lax.dot_general(left, right, (((1,), (1,)), ((), ())), preferred_element_...  11 us
    all_to_all x1, waiting for transfers between devices, reduced(): lax.all_to_all(tiles, axis, 0, 0, tiled=True).astype(F32)  10.3 us
    all_to_all x1, waiting for transfers between devices, spread(): lax.all_to_all(copies, axis, 0, 0, tiled=True).reshape(-1, *array.shape[1:])  7.17 us
    dot_general x8, matrix products, tn(): lax.dot_general(left, right, (((0,), (0,)), ((), ())), preferred_element_...  6.35 us
    dot_general x11, matrix products, nn(): lax.dot_general(left, right, (((1,), (0,)), ((), ())), preferred_element_...  5.13 us
    all_to_all x1, starting transfers between devices, spread(): lax.all_to_all(copies, axis, 0, 0, tiled=True).reshape(-1, *array.shape[1:])  5.1 us
  transfers between devices with their start and end apart: 2, of which 2 were waited for; matrix products, arithmetic and copies ran while one was open for 3% of the time, Pallas kernels for 0%

profile of v1, /device:TPU:1, one launch (start us, length us, event | category | flops | bytes accessed | tf_op | source)
XLA Modules:
  0.0 198.6 jit_solution(13365904978124400874)
XLA Ops:
  1.5 23.3 %all_to_all.45 = bf16[16,8,1024]{2,1,0:T(8,128)(2,1)S(1)} all-to-all(bf16[16,8,1024]{2,1,0:T(8,128)(2,1)S(1)} %broadcast_in_dim.20), channel_id=1, replica_groups=mesh['zl'=2,'y'=8,'zh'=4,'x'=4,'core'=2] {'zh','x'}, dimensions={0} | all-to-all | bytes 524288 | tf_op jit(solution)/shard_map/all_to_all | solution.py:32
  24.9 7.4 %all_to_all.46 = bf16[2,128,1024]{2,1,0:T(8,128)(2,1)S(1)} all-to-all(bf16[2,128,1024]{2,1,0:T(8,128)(2,1)S(1)} %broadcast_in_dim.21), channel_id=1, replica_groups=mesh['zl'=2,'y'=8,'zh'=4,'x'=4,'core'=2] {'core'}, dimensions={0} | all-to-all | bytes 1048576 | tf_op jit(solution)/shard_map/all_to_all | solution.py:32
  34.9 47.5 %all_to_all.47 = bf16[16,16,3200]{2,1,0:T(8,128)(2,1)S(1)} all-to-all(bf16[16,16,3200]{2,1,0:T(8,128)(2,1)S(1)} %bitcast.89), channel_id=1, replica_groups=mesh['zl'=2,'y'=8,'zh'=4,'x'=4,'core'=2] {'zl','y'}, dimensions={0} | all-to-all | bytes 3276800 | tf_op jit(solution)/shard_map/all_to_all | solution.py:38
  83.3 25.5 %all_to_all.48 = bf16[8,16,3200]{2,1,0:T(8,128)(2,1)S(1)} all-to-all(bf16[8,16,3200]{2,1,0:T(8,128)(2,1)S(1)} %broadcast_in_dim.22), channel_id=1, replica_groups=mesh['zl'=2,'y'=8,'zh'=4,'x'=4,'core'=2] {'y'}, dimensions={0} | all-to-all | bytes 1638400 | tf_op jit(solution)/shard_map/all_to_all | solution.py:32
  108.9 19.6 %all_to_all.49 = bf16[2,128,3200]{2,1,0:T(8,128)(2,1)S(1)} all-to-all(bf16[2,128,3200]{2,1,0:T(8,128)(2,1)S(1)} %broadcast_in_dim.23), channel_id=1, replica_groups=mesh['zl'=2,'y'=8,'zh'=4,'x'=4,'core'=2] {'zl'}, dimensions={0} | all-to-all | bytes 3276800 | tf_op jit(solution)/shard_map/all_to_all | solution.py:32
  131.6 1.4 add_convert_fusion
  133.5 0.9 fusion.24
  135.7 1.0 fusion.66
  136.7 1.2 fusion.10
  138.1 1.2 fusion.11
  140.2 1.0 fusion.12
  141.2 0.9 fusion.18
  143.8 1.7 copy.121
  145.5 1.2 fusion.39
  146.7 8.6 %all_to_all.50 = bf16[2,128,1408]{2,1,0:T(8,128)(2,1)} all-to-all(bf16[2,128,1408]{2,1,0:T(8,128)(2,1)S(1)} %bitcast.80), channel_id=1, replica_groups=mesh['zl'=2,'y'=8,'zh'=4,'x'=4,'core'=2] {'core'}, dimensions={0} | all-to-all | bytes 1441792 | tf_op jit(solution)/shard_map/all_to_all | solution.py:38
  155.4 2.1 %reduce_sum.44 = bf16[128,1408]{1,0:T(8,128)(2,1)} reduce(bf16[2,128,1408]{2,1,0:T(8,128)(2,1)} %all_to_all.50, bf16[]{:T(256)} %constant.8.clone.1), dimensions={0}, to_apply=%region_2.3 | reduce | flops 180224 | bytes 1081346 | tf_op jit(solution)/shard_map/reduce_sum | solution.py:38
  157.4 4.2 %all-to-all-start.6 = ((bf16[16,8,1408]{2,1,0:T(8,128)(2,1)}), bf16[16,8,1408]{2,1,0:T(8,128)(2,1)}, u32[]{:S(2)}, u32[]{:S(2)}) async-start(bf16[16,8,1408]{2,1,0:T(8,128)(2,1)} %bitcast.90), calls=%async_computation.6 | async-start | bytes 720896 | tf_op jit(solution)/shard_map/all_to_all | solution.py:38
  162.1 1.9 fusion.13
  164.1 0.9 fusion.14
  165.0 10.3 %all-to-all-done.6 = bf16[16,8,1408]{2,1,0:T(8,128)(2,1)} async-done(((bf16[16,8,1408]{2,1,0:T(8,128)(2,1)}), bf16[16,8,1408]{2,1,0:T(8,128)(2,1)}, u32[]{:S(2)}, u32[]{:S(2)}) %all-to-all-start.6) | async-done | bytes 360480 | tf_op jit(solution)/shard_map/all_to_all | solution.py:38
  175.3 1.0 convert_reduce_fusion.1
  177.2 5.1 %all-to-all-start.7 = ((bf16[16,8,192]{2,1,0:T(8,128)(2,1)}), bf16[16,8,192]{2,1,0:T(8,128)(2,1)S(1)}, u32[]{:S(2)}, u32[]{:S(2)}) async-start(bf16[16,8,192]{2,1,0:T(8,128)(2,1)} %broadcast_in_dim.24), calls=%async_computation.7 | async-start | bytes 131072 | tf_op jit(solution)/shard_map/all_to_all | solution.py:32
  184.2 7.2 %all-to-all-done.7 = bf16[16,8,192]{2,1,0:T(8,128)(2,1)S(1)} async-done(((bf16[16,8,192]{2,1,0:T(8,128)(2,1)}), bf16[16,8,192]{2,1,0:T(8,128)(2,1)S(1)}, u32[]{:S(2)}, u32[]{:S(2)}) %all-to-all-start.7) | async-done | bytes 49184 | tf_op jit(solution)/shard_map/all_to_all | solution.py:32
  191.5 5.3 %all_to_all.51 = bf16[2,128,192]{1,2,0:T(8,128)(2,1)S(1)} all-to-all(bf16[2,128,192]{1,2,0:T(8,128)(2,1)S(1)} %broadcast_in_dim.25), channel_id=1, replica_groups=mesh['zl'=2,'y'=8,'zh'=4,'x'=4,'core'=2] {'core'}, dimensions={0} | all-to-all | bytes 196608 | tf_op jit(solution)/shard_map/all_to_all | solution.py:32
  (112 shorter events, 17.1 us)
Async XLA Ops:
  0.6 31.9 %copy-start = (bf16[512,896]{1,0:T(8,128)(2,1)S(1)}, bf16[512,896]{1,0:T(8,128)(2,1)}, u32[]{:S(2)}) copy-start(bf16[512,896]{1,0:T(8,128)(2,1)} %param.21) | copy-start | bytes 2752516
  0.6 31.9 %copy-start.23 = (f32[512]{0:T(512)S(1)}, f32[512]{0:T(512)}, u32[]{:S(2)}) copy-start(f32[512]{0:T(512)} %param.19) | copy-start | bytes 6148
  24.8 8.2 %copy-start.3 = (bf16[512,896]{1,0:T(8,128)(2,1)S(1)}, bf16[512,896]{1,0:T(8,128)(2,1)}, u32[]{:S(2)}) copy-start(bf16[512,896]{1,0:T(8,128)(2,1)} %param.22) | copy-start | bytes 2752516
  32.3 2.3 %copy-start.5 = (bf16[2,128,1024]{2,1,0:T(8,128)(2,1)}, bf16[2,128,1024]{2,1,0:T(8,128)(2,1)S(1)}, u32[]{:S(2)}) copy-start(bf16[2,128,1024]{2,1,0:T(8,128)(2,1)S(1)} %all_to_all.46) | copy-start | bytes 1572868
  32.6 1.2 copy-start.20
  33.1 1.2 copy-start.12
  33.1 1.2 copy-start.13
  33.1 1.2 copy-start.16
  33.1 1.2 copy-start.18
  108.9 19.6 %copy-start.7 = (bf16[64,896]{1,0:T(8,128)(2,1)S(1)}, bf16[64,896]{1,0:T(8,128)(2,1)}, u32[]{:S(2)}) copy-start(bf16[64,896]{1,0:T(8,128)(2,1)} %param.25) | copy-start | bytes 344068
  128.5 0.9 copy-start.9
  128.7 1.3 copy-start.8
  129.7 1.0 copy-start.11
  130.3 0.9 copy-start.10
  130.7 0.9 copy-start.15
  133.0 1.8 copy-start.1
  134.8 1.8 copy-start.4
  157.4 17.8 %all-to-all-start.6 = ((bf16[16,8,1408]{2,1,0:T(8,128)(2,1)}), bf16[16,8,1408]{2,1,0:T(8,128)(2,1)}, u32[]{:S(2)}, u32[]{:S(2)}) async-start(bf16[16,8,1408]{2,1,0:T(8,128)(2,1)} %bitcast.90), calls=%async_computation.6 | async-start | bytes 720896 | tf_op jit(solution)/shard_map/all_to_all | solution.py:38
  161.7 2.4 %copy-start.2 = (bf16[256,896]{1,0:T(8,128)(2,1)S(1)}, bf16[256,896]{1,0:T(8,128)(2,1)}, u32[]{:S(2)}) copy-start(bf16[256,896]{1,0:T(8,128)(2,1)} %copy-done.1) | copy-start | bytes 1376260
  161.9 14.4 %copy-start.14 = (bf16[512,64]{0,1:T(8,128)(2,1)S(1)}, bf16[512,64]{0,1:T(8,128)(2,1)}, u32[]{:S(2)}) copy-start(bf16[512,64]{0,1:T(8,128)(2,1)} %param.24) | copy-start | bytes 196612
  161.9 20.4 %copy-start.19 = (bf16[512,64]{0,1:T(8,128)(2,1)S(1)}, bf16[512,64]{0,1:T(8,128)(2,1)}, u32[]{:S(2)}) copy-start(bf16[512,64]{0,1:T(8,128)(2,1)} %param.30) | copy-start | bytes 196612
  161.9 20.7 %copy-start.17 = (bf16[512,64]{0,1:T(8,128)(2,1)S(1)}, bf16[512,64]{0,1:T(8,128)(2,1)}, u32[]{:S(2)}) copy-start(bf16[512,64]{0,1:T(8,128)(2,1)} %param.32) | copy-start | bytes 196612
  164.1 32.8 %copy-start.6 = (bf16[2,128,1024]{2,1,0:T(8,128)(2,1)S(1)}, bf16[2,128,1024]{2,1,0:T(8,128)(2,1)}, u32[]{:S(2)}) copy-start(bf16[2,128,1024]{2,1,0:T(8,128)(2,1)} %copy-done.5) | copy-start | bytes 1572868
  177.2 14.2 %all-to-all-start.7 = ((bf16[16,8,192]{2,1,0:T(8,128)(2,1)}), bf16[16,8,192]{2,1,0:T(8,128)(2,1)S(1)}, u32[]{:S(2)}, u32[]{:S(2)}) async-start(bf16[16,8,192]{2,1,0:T(8,128)(2,1)} %broadcast_in_dim.24), calls=%async_computation.7 | async-start | bytes 131072 | tf_op jit(solution)/shard_map/all_to_all | solution.py:32
  (2 other events, 1.7 us)

commit v2 on v1

--- a/solution.py
+++ b/solution.py
@@ -1,6 +1,8 @@
 import jax
 import jax.numpy as jnp
 from jax import lax
+from jax.experimental import pallas as pl
+from jax.experimental.pallas import tpu as pltpu
 from jax.sharding import Mesh
 from jax.sharding import PartitionSpec as P
 
@@ -42,6 +44,120 @@
     high = value.astype(BF)
     low = (value - high.astype(F32)).astype(BF)
     return jnp.pad(jnp.concatenate([high, low], axis=1), ((0, 0), (0, 126)))
+
+
+LANES = 128
+CHUNK = 32
+
+
+def back_kernel(
+    full,
+    gate_w,
+    up_w,
+    gate_out,
+    gate_out_dir,
+    up_out,
+    up_out_dir,
+    down_in,
+    down_in_dir,
+    back,
+    curv_gate,
+    curv_up,
+    curv_down,
+    terms,
+    d_gate,
+    d_up,
+    d_gate_dir,
+    d_up_dir,
+    hidden,
+    hidden_dir,
+):
+    tokens = full.shape[0]
+    rows, cols = gate_w.shape
+    rank = gate_out.shape[0]
+    at = 3 * cols
+    pairs = [full[:, at + 2 * k * rank : at + 2 * (k + 1) * rank] for k in range(3)]
+    factors = ((gate_out, gate_out_dir), (up_out, up_out_dir), (down_in, down_in_dir))
+
+    def column_block(block, carry):
+        here = pl.ds(pl.multiple_of(block * LANES, LANES), LANES)
+        for k, (plain, direction) in enumerate(factors):
+            f, g = plain[:, here], direction[:, here]
+            terms[2 * k] = SCALE * nn(pairs[k][:, :rank], f)
+            terms[2 * k + 1] = SCALE * nn(pairs[k], jnp.concatenate([g, f], axis=0))
+        for chunk in range(tokens // CHUNK):
+            r = pl.ds(chunk * CHUNK, CHUNK)
+            at_up = pl.ds(pl.multiple_of(cols + block * LANES, LANES), LANES)
+            at_adj = pl.ds(pl.multiple_of(2 * cols + block * LANES, LANES), LANES)
+            gate_pre = full[r, here].astype(F32) + terms[0, r, :]
+            up_pre = full[r, at_up].astype(F32) + terms[2, r, :]
+            adj = full[r, at_adj].astype(F32) + terms[4, r, :]
+            gate_tan, up_tan, adj_tan = terms[1, r, :], terms[3, r, :], terms[5, r, :]
+            sig = 1.0 / (1.0 + jnp.exp(-gate_pre))
+            rest = 1.0 - sig
+            act = gate_pre * sig
+            slope = sig * (1.0 + gate_pre * rest)
+            bend = sig * rest * (2.0 + gate_pre * (1.0 - 2.0 * sig))
+            slope_tan = slope * gate_tan
+            up_slope = up_pre * slope
+            hidden[r, here] = (act * up_pre).astype(BF)
+            hidden_dir[r, here] = (slope_tan * up_pre + act * up_tan).astype(BF)
+            d_gate[r, here] = (adj * up_slope).astype(BF)
+            d_up[r, here] = (adj * act).astype(BF)
+            d_gate_dir[r, here] = (
+                adj_tan * up_slope + adj * (up_tan * slope + up_pre * bend * gate_tan)
+            ).astype(BF)
+            d_up_dir[r, here] = (adj_tan * act + adj * slope_tan).astype(BF)
+        return carry
+
+    lax.fori_loop(0, cols // LANES, column_block, 0)
+    dg, du, dgd, dud = d_gate[...], d_up[...], d_gate_dir[...], d_up_dir[...]
+    h, hd = hidden[...], hidden_dir[...]
+    gw, uw = gate_w[...], up_w[...]
+    back[:, :rows] = (nt(dg, gw) + nt(du, uw)).astype(BF)
+    back[:, rows : 2 * rows] = (nt(dgd, gw) + nt(dud, uw)).astype(BF)
+    go, god, uo, uod = gate_out[...], gate_out_dir[...], up_out[...], up_out_dir[...]
+    di, did = down_in[...], down_in_dir[...]
+    q = jnp.concatenate([nt(dg, go), nt(du, uo)], axis=1)
+    back[:, 2 * rows : 2 * rows + 2 * rank] = q.astype(BF)
+    q = jnp.concatenate([nt(dgd, go) + nt(dg, god), nt(dud, uo) + nt(du, uod)], axis=1)
+    back[:, 2 * rows + 2 * rank : 2 * rows + 4 * rank] = q.astype(BF)
+    q = nt(hd, di) + nt(h, did)
+    q = jnp.concatenate([q, jnp.zeros_like(q)], axis=1)
+    back[:, 2 * rows + 4 * rank :] = q.astype(BF)
+    low, low_dir = pairs[0][:, :rank], pairs[0][:, rank:]
+    curv_gate[...] = SCALE * (tn(low_dir, dg) + tn(low, dgd))
+    low, low_dir = pairs[1][:, :rank], pairs[1][:, rank:]
+    curv_up[...] = SCALE * (tn(low_dir, du) + tn(low, dud))
+    low, low_dir = pairs[2][:, :rank], pairs[2][:, rank:]
+    curv_down[...] = SCALE * (tn(low, hd) + tn(low_dir, h))
+
+
+def backward(full, gate_w, up_w, *factors):
+    tokens = full.shape[0]
+    rows, cols = gate_w.shape
+    rank = factors[0].shape[0]
+    whole = pl.BlockSpec(memory_space=pltpu.VMEM)
+    curvature = jax.ShapeDtypeStruct((rank, cols), F32)
+    panel = pltpu.VMEM((tokens, cols), BF)
+    return pl.pallas_call(
+        back_kernel,
+        out_shape=(
+            jax.ShapeDtypeStruct((tokens, 2 * rows + 6 * rank), BF),
+            curvature,
+            curvature,
+            curvature,
+        ),
+        in_specs=[whole] * (3 + len(factors)),
+        out_specs=[whole] * 4,
+        scratch_shapes=[pltpu.VMEM((6, tokens, LANES), F32)] + [panel] * 6,
+        compiler_params=pltpu.CompilerParams(vmem_limit_bytes=32 * 1024 * 1024),
+        cost_estimate=pl.CostEstimate(
+            flops=2 * tokens * cols * (4 * rows + 20 * rank),
+            bytes_accessed=2 * cols * (2 * rows + 4 * tokens),
+            transcendentals=tokens * cols,
+        ),
+    )(full, gate_w, up_w, *factors)
 
 
 def on_device(
@@ -73,7 +189,7 @@
     tokens_f = tokens_all.astype(F32)
     squares = jnp.sum(tokens_f * tokens_f, axis=1, keepdims=True)
     scaled = (tokens_f * norm_gain).astype(BF)
-    in_factors = jnp.concatenate([gate_in, up_in, gate_in_dir, up_in_dir], axis=1)
+    in_factors = jnp.concatenate([gate_in, gate_in_dir, up_in, up_in_dir], axis=1)
     b_factors = jnp.concatenate([down_b, down_b_dir], axis=0)
     partial = jnp.concatenate(
         [
@@ -86,7 +202,7 @@
         ],
         axis=1,
     )
-    mine = reduced(partial, ROW)
+    mine = reduced(reduced(partial, "zl").astype(BF), "y")
     at = 3 * cols + 6 * rank
     inv_rms = lax.rsqrt((mine[:, at : at + 1] + mine[:, at + 1 : at + 2]) / D + EPSILON)
     mine = jnp.concatenate(
@@ -101,54 +217,20 @@
     )
     full = spread(spread(mine, "y"), "zl")
     inv_all = full[:, at : at + 1].astype(F32) + full[:, at + 1 : at + 2].astype(F32)
-    low = full[:, 3 * cols : at]
-    gate_low, up_low, gate_low_dir, up_low_dir, adj_low, adj_low_dir = [
-        low[:, k * rank : (k + 1) * rank] for k in range(6)
-    ]
-    gate_pre = full[:, :cols].astype(F32) + SCALE * nn(gate_low, gate_out)
-    up_pre = full[:, cols : 2 * cols].astype(F32) + SCALE * nn(up_low, up_out)
-    hidden_adj = full[:, 2 * cols : 3 * cols].astype(F32) + SCALE * nt(adj_low, down_in)
-    gate_tan = SCALE * (nn(gate_low_dir, gate_out) + nn(gate_low, gate_out_dir))
-    up_tan = SCALE * (nn(up_low_dir, up_out) + nn(up_low, up_out_dir))
-    adj_tan = SCALE * (nt(adj_low_dir, down_in) + nt(adj_low, down_in_dir))
-    sig = jax.nn.sigmoid(gate_pre)
-    act = gate_pre * sig
-    slope = sig * (1.0 + gate_pre * (1.0 - sig))
-    bend = sig * (1.0 - sig) * (2.0 + gate_pre * (1.0 - 2.0 * sig))
-    hidden = (act * up_pre).astype(BF)
-    hidden_dir = (slope * gate_tan * up_pre + act * up_tan).astype(BF)
-    d_gate = (hidden_adj * up_pre * slope).astype(BF)
-    d_up = (hidden_adj * act).astype(BF)
-    d_gate_dir = (
-        adj_tan * up_pre * slope + hidden_adj * (up_tan * slope + up_pre * bend * gate_tan)
-    ).astype(BF)
-    d_up_dir = (adj_tan * act + hidden_adj * slope * gate_tan).astype(BF)
-
-    quotients = jnp.concatenate(
-        [
-            nt(d_gate, gate_out),
-            nt(d_up, up_out),
-            nt(d_gate_dir, gate_out) + nt(d_gate, gate_out_dir),
-            nt(d_up_dir, up_out) + nt(d_up, up_out_dir),
-            nn(hidden_dir, down_in) + nn(hidden, down_in_dir),
-        ],
-        axis=1,
-    )
-    back = jnp.concatenate(
-        [
-            (nt(d_gate, gate_w) + nt(d_up, up_w)).astype(BF),
-            (nt(d_gate_dir, gate_w) + nt(d_up_dir, up_w)).astype(BF),
-            jnp.pad(quotients.astype(BF), ((0, 0), (0, rank))),
-        ],
-        axis=1,
+    back, curv_gate_out, curv_up_out, curv_down_in = backward(
+        full,
+        gate_w,
+        up_w,
+        gate_out,
+        gate_out_dir,
+        up_out,
+        up_out_dir,
+        down_in.T,
+        down_in_dir.T,
     )
     got = reduced(reduced(back, "core").astype(BF), CHIPS)
     q = got[:, 2 * rows : 2 * rows + 5 * rank]
     q_all = spread(spread(q[:, 2 * rank :].astype(BF), CHIPS), "core").astype(F32)
-
-    curv_gate_out = SCALE * (tn(gate_low_dir, d_gate) + tn(gate_low, d_gate_dir))
-    curv_up_out = SCALE * (tn(up_low_dir, d_up) + tn(up_low, d_up_dir))
-    curv_down_in = SCALE * (tn(hidden_dir, adj_low) + tn(hidden, adj_low_dir))
 
     q_gate, q_up, q_gate_dir, q_up_dir = [
         q[:, k * rank : (k + 1) * rank].astype(BF) for k in range(4)
@@ -169,7 +251,7 @@
         curv_gate_out,
         curv_in[:, rank:],
         curv_up_out,
-        curv_down_in,
+        curv_down_in.T,
         curv_down_out,
     )
 

time: 199 us -> 191 us (0.960)
  matrix products: 22.5 us -> 8.43 us
  Pallas kernels: 0 us -> 6.06 us
  waiting for transfers between devices: 17.5 us -> 21.6 us
  local copies, waits for them, and re-layouts: 5.12 us -> 2.42 us
  other arithmetic: 5.86 us -> 3.86 us
    pallas_call x0 -> x1, Pallas kernels: none -> 6.06 us  [backward(): pl.pallas_call(back_kernel, out_shape=(jax.ShapeDtypeStruct((tokens, 2 *...]
    dot_general x8 -> x2, matrix products: 6.35 us -> 1.03 us  [tn(): lax.dot_general(left, right, (((0,), (0,)), ((), ())), preferred_element_...]
    dot_general x21 -> x8, matrix products: 11 us -> 6.24 us  [nt(): lax.dot_general(left, right, (((1,), (1,)), ((), ())), preferred_element_...]
    dot_general x11 -> x3, matrix products: 5.13 us -> 1.17 us  [nn(): lax.dot_general(left, right, (((1,), (0,)), ((), ())), preferred_element_...]
    all_to_all x1, waiting for transfers between devices: 10.3 us -> 13.5 us  [reduced(): lax.all_to_all(tiles, axis, 0, 0, tiled=True).astype(F32)]
    all_to_all x2 -> x3, blocking collectives: 56.1 us -> 59 us  [reduced(): lax.all_to_all(tiles, axis, 0, 0, tiled=True).astype(F32)]
    unnamed x54 -> x43, local copies, waits for them, and re-layouts: 3.13 us -> 0.44 us
    all_to_all x5, blocking collectives: 81.1 us -> 78.9 us  [spread(): lax.all_to_all(copies, axis, 0, 0, tiled=True).reshape(-1, *array.shape[1:])]
  transfers between devices with their start and end apart: 2 -> 2, of which waited for: 2 -> 2; matrix products, arithmetic and copies ran while one was open for 3% -> 1% of each run, Pallas kernels for 0% -> 0%
where the time goes in v2:
time: 191 us; the launch traced here: 190 us
  blocking collectives  138 us (72%)
  waiting for transfers between devices  21.6 us (11%)
  starting transfers between devices  8.96 us (5%)
  matrix products  8.43 us (4%)
  Pallas kernels  6.06 us (3%)
  other arithmetic  3.86 us (2%)
  local copies, waits for them, and re-layouts  2.42 us (1%)
    all_to_all x5, blocking collectives, spread(): lax.all_to_all(copies, axis, 0, 0, tiled=True).reshape(-1, *array.shape[1:])  78.9 us
    all_to_all x3, blocking collectives, reduced(): lax.all_to_all(tiles, axis, 0, 0, tiled=True).astype(F32)  59 us
    all_to_all x1, waiting for transfers between devices, reduced(): lax.all_to_all(tiles, axis, 0, 0, tiled=True).astype(F32)  13.5 us
    all_to_all x1, waiting for transfers between devices, spread(): lax.all_to_all(copies, axis, 0, 0, tiled=True).reshape(-1, *array.shape[1:])  8.14 us
    dot_general x8, matrix products, nt(): lax.dot_general(left, right, (((1,), (1,)), ((), ())), preferred_element_...  6.24 us
    pallas_call x1, Pallas kernels, backward(): pl.pallas_call(back_kernel, out_shape=(jax.ShapeDtypeStruct((tokens, 2 *...  6.06 us
    all_to_all x1, starting transfers between devices, spread(): lax.all_to_all(copies, axis, 0, 0, tiled=True).reshape(-1, *array.shape[1:])  5.12 us
    all_to_all x1, starting transfers between devices, reduced(): lax.all_to_all(tiles, axis, 0, 0, tiled=True).astype(F32)  3.84 us
  transfers between devices with their start and end apart: 2, of which 2 were waited for; matrix products, arithmetic and copies ran while one was open for 1% of the time, Pallas kernels for 0%

profile of v2, /device:TPU:1, one launch (start us, length us, event | category | flops | bytes accessed | tf_op | source)
XLA Modules:
  0.0 190.2 jit_solution(9161491724023919076)
XLA Ops:
  0.7 0.8 pad_maximum_fusion
  1.5 23.3 %all_to_all.50 = bf16[16,8,1024]{2,1,0:T(8,128)(2,1)S(1)} all-to-all(bf16[16,8,1024]{2,1,0:T(8,128)(2,1)S(1)} %broadcast_in_dim.20), channel_id=1, replica_groups=mesh['zl'=2,'y'=8,'zh'=4,'x'=4,'core'=2] {'zh','x'}, dimensions={0} | all-to-all | bytes 524288 | tf_op jit(solution)/shard_map/all_to_all | solution.py:34
  24.9 7.4 %all_to_all.51 = bf16[2,128,1024]{2,1,0:T(8,128)(2,1)S(1)} all-to-all(bf16[2,128,1024]{2,1,0:T(8,128)(2,1)S(1)} %broadcast_in_dim.21), channel_id=1, replica_groups=mesh['zl'=2,'y'=8,'zh'=4,'x'=4,'core'=2] {'core'}, dimensions={0} | all-to-all | bytes 1048576 | tf_op jit(solution)/shard_map/all_to_all | solution.py:34
  34.8 22.1 %all_to_all.52 = bf16[2,128,3200]{2,1,0:T(8,128)(2,1)S(1)} all-to-all(bf16[2,128,3200]{2,1,0:T(8,128)(2,1)S(1)} %bitcast.43), channel_id=1, replica_groups=mesh['zl'=2,'y'=8,'zh'=4,'x'=4,'core'=2] {'zl'}, dimensions={0} | all-to-all | bytes 3276800 | tf_op jit(solution)/shard_map/all_to_all | solution.py:40
  56.9 1.4 reduce_sum.55
  58.3 28.2 %all_to_all.53 = bf16[8,16,3200]{2,1,0:T(8,128)(2,1)S(1)} all-to-all(bf16[8,16,3200]{2,1,0:T(8,128)(2,1)} %bitcast.34), channel_id=1, replica_groups=mesh['zl'=2,'y'=8,'zh'=4,'x'=4,'core'=2] {'y'}, dimensions={0} | all-to-all | bytes 1638400 | tf_op jit(solution)/shard_map/all_to_all | solution.py:40
  87.2 24.1 %all_to_all.54 = bf16[8,16,3200]{2,1,0:T(8,128)(2,1)S(1)} all-to-all(bf16[8,16,3200]{2,1,0:T(8,128)(2,1)S(1)} %broadcast_in_dim.22), channel_id=1, replica_groups=mesh['zl'=2,'y'=8,'zh'=4,'x'=4,'core'=2] {'y'}, dimensions={0} | all-to-all | bytes 1638400 | tf_op jit(solution)/shard_map/all_to_all | solution.py:34
  111.5 18.7 %all_to_all.55 = bf16[2,128,3200]{2,1,0:T(8,128)(2,1)S(1)} all-to-all(bf16[2,128,3200]{2,1,0:T(8,128)(2,1)S(1)} %broadcast_in_dim.23), channel_id=1, replica_groups=mesh['zl'=2,'y'=8,'zh'=4,'x'=4,'core'=2] {'zl'}, dimensions={0} | all-to-all | bytes 3276800 | tf_op jit(solution)/shard_map/all_to_all | solution.py:34
  130.2 6.1 %shard_map.233 = (bf16[256,1408]{1,0:T(8,128)(2,1)S(1)}, f32[64,896]{1,0:T(8,128)}, f32[64,896]{1,0:T(8,128)}, f32[64,896]{1,0:T(8,128)}) custom-call(bf16[256,3200]{1,0:T(8,128)(2,1)S(1)} %bitcast.28, bf16[512,896]{1,0:T(8,128)(2,1)S(1)} %copy-done.1, bf16[512,896]{1,0:T(8,128)(2,1)S(1)} %copy-done.3, bf16[64,896]{1,0:T(8,128)(2,1)S(1)} %copy-done.4, ...), custom_call_target="tpu_custom_call" | custom-call | flops 1526726656 | bytes 3670016 | tf_op jit(solution)/shard_map/pallas_call | solution.py:143
  136.3 8.7 %all_to_all.56 = bf16[2,128,1408]{2,1,0:T(8,128)(2,1)S(1)} all-to-all(bf16[2,128,1408]{2,1,0:T(8,128)(2,1)S(1)} %bitcast.30), channel_id=1, replica_groups=mesh['zl'=2,'y'=8,'zh'=4,'x'=4,'core'=2] {'core'}, dimensions={0} | all-to-all | bytes 1441792 | tf_op jit(solution)/shard_map/all_to_all | solution.py:40
  145.0 0.9 reduce_sum.57
  146.0 3.8 %all-to-all-start.7 = ((bf16[16,8,1408]{2,1,0:T(8,128)(2,1)}), bf16[16,8,1408]{2,1,0:T(8,128)(2,1)S(1)}, u32[]{:S(2)}, u32[]{:S(2)}) async-start(bf16[16,8,1408]{2,1,0:T(8,128)(2,1)} %bitcast.44), calls=%async_computation.7 | async-start | bytes 720896 | tf_op jit(solution)/shard_map/all_to_all | solution.py:40
  150.0 13.5 %all-to-all-done.7 = bf16[16,8,1408]{2,1,0:T(8,128)(2,1)S(1)} async-done(((bf16[16,8,1408]{2,1,0:T(8,128)(2,1)}), bf16[16,8,1408]{2,1,0:T(8,128)(2,1)S(1)}, u32[]{:S(2)}, u32[]{:S(2)}) %all-to-all-start.7) | async-done | bytes 360480 | tf_op jit(solution)/shard_map/all_to_all | solution.py:40
  163.5 1.0 fusion.35
  164.5 1.0 fusion.40
  165.4 1.0 convolution_add_fusion.2
  166.6 1.6 fusion.6
  168.2 0.6 broadcast_in_dim.24
  168.9 5.1 %all-to-all-start.8 = ((bf16[16,8,192]{2,1,0:T(8,128)(2,1)}), bf16[16,8,192]{2,1,0:T(8,128)(2,1)S(1)}, u32[]{:S(2)}, u32[]{:S(2)}) async-start(bf16[16,8,192]{2,1,0:T(8,128)(2,1)} %broadcast_in_dim.24), calls=%async_computation.8 | async-start | bytes 131072 | tf_op jit(solution)/shard_map/all_to_all | solution.py:34
  174.0 0.8 fusion.8
  174.8 8.1 %all-to-all-done.8 = bf16[16,8,192]{2,1,0:T(8,128)(2,1)S(1)} async-done(((bf16[16,8,192]{2,1,0:T(8,128)(2,1)}), bf16[16,8,192]{2,1,0:T(8,128)(2,1)S(1)}, u32[]{:S(2)}, u32[]{:S(2)}) %all-to-all-start.8) | async-done | bytes 49184 | tf_op jit(solution)/shard_map/all_to_all | solution.py:34
  183.1 5.4 %all_to_all.57 = bf16[2,128,192]{1,2,0:T(8,128)(2,1)S(1)} all-to-all(bf16[2,128,192]{1,2,0:T(8,128)(2,1)S(1)} %broadcast_in_dim.25), channel_id=1, replica_groups=mesh['zl'=2,'y'=8,'zh'=4,'x'=4,'core'=2] {'core'}, dimensions={0} | all-to-all | bytes 196608 | tf_op jit(solution)/shard_map/all_to_all | solution.py:34
  188.5 0.8 convolution_multiply_fusion.1
  189.5 0.7 fusion.45
  (76 shorter events, 4.1 us)
Async XLA Ops:
  0.6 33.0 %copy-start = (bf16[896,512]{1,0:T(8,128)(2,1)S(1)}, bf16[896,512]{1,0:T(8,128)(2,1)}, u32[]{:S(2)}) copy-start(bf16[896,512]{1,0:T(8,128)(2,1)} %param.23) | copy-start | bytes 2752516
  0.6 32.0 %copy-start.18 = (f32[512]{0:T(512)S(1)}, f32[512]{0:T(512)}, u32[]{:S(2)}) copy-start(f32[512]{0:T(512)} %param.19) | copy-start | bytes 6148
  0.7 32.0 %copy-start.1 = (bf16[512,896]{1,0:T(8,128)(2,1)S(1)}, bf16[512,896]{1,0:T(8,128)(2,1)}, u32[]{:S(2)}) copy-start(bf16[512,896]{1,0:T(8,128)(2,1)} %gate_w.1) | copy-start | bytes 2752516
  24.9 8.2 %copy-start.2 = (bf16[512,896]{1,0:T(8,128)(2,1)S(1)}, bf16[512,896]{1,0:T(8,128)(2,1)}, u32[]{:S(2)}) copy-start(bf16[512,896]{1,0:T(8,128)(2,1)} %up_w.1) | copy-start | bytes 2752516
  32.3 2.2 %copy-start.10 = (bf16[2,128,1024]{2,1,0:T(8,128)(2,1)}, bf16[2,128,1024]{2,1,0:T(8,128)(2,1)S(1)}, u32[]{:S(2)}) copy-start(bf16[2,128,1024]{2,1,0:T(8,128)(2,1)S(1)} %all_to_all.51) | copy-start | bytes 1572868
  33.1 1.1 copy-start.12
  33.1 1.1 copy-start.13
  33.1 1.1 copy-start.14
  33.1 1.1 copy-start.15
  33.6 0.9 copy-start.16
  33.6 0.9 copy-start.17
  111.4 18.8 %copy-start.3 = (bf16[512,896]{1,0:T(8,128)(2,1)S(1)}, bf16[512,896]{1,0:T(8,128)(2,1)}, u32[]{:S(2)}) copy-start(bf16[512,896]{1,0:T(8,128)(2,1)} %up_w.1) | copy-start | bytes 2752516
  111.4 18.8 %copy-start.4 = (bf16[64,896]{1,0:T(8,128)(2,1)S(1)}, bf16[64,896]{1,0:T(8,128)(2,1)}, u32[]{:S(2)}) copy-start(bf16[64,896]{1,0:T(8,128)(2,1)} %gate_out.1) | copy-start | bytes 344068
  111.4 18.8 %copy-start.5 = (bf16[64,896]{1,0:T(8,128)(2,1)S(1)}, bf16[64,896]{1,0:T(8,128)(2,1)}, u32[]{:S(2)}) copy-start(bf16[64,896]{1,0:T(8,128)(2,1)} %gate_out_dir.1) | copy-start | bytes 344068
  111.4 18.8 %copy-start.6 = (bf16[64,896]{1,0:T(8,128)(2,1)S(1)}, bf16[64,896]{1,0:T(8,128)(2,1)}, u32[]{:S(2)}) copy-start(bf16[64,896]{1,0:T(8,128)(2,1)} %up_out.1) | copy-start | bytes 344068
  111.4 18.8 %copy-start.7 = (bf16[64,896]{1,0:T(8,128)(2,1)S(1)}, bf16[64,896]{1,0:T(8,128)(2,1)}, u32[]{:S(2)}) copy-start(bf16[64,896]{1,0:T(8,128)(2,1)} %up_out_dir.1) | copy-start | bytes 344068
  111.4 18.8 %copy-start.8 = (bf16[896,64]{0,1:T(8,128)(2,1)S(1)}, bf16[896,64]{0,1:T(8,128)(2,1)}, u32[]{:S(2)}) copy-start(bf16[896,64]{0,1:T(8,128)(2,1)} %param.28) | copy-start | bytes 344068
  111.5 18.8 %copy-start.9 = (bf16[896,64]{0,1:T(8,128)(2,1)S(1)}, bf16[896,64]{0,1:T(8,128)(2,1)}, u32[]{:S(2)}) copy-start(bf16[896,64]{0,1:T(8,128)(2,1)} %param.34) | copy-start | bytes 344068
  146.0 42.5 %copy-start.11 = (bf16[2,128,1024]{2,1,0:T(8,128)(2,1)S(1)}, bf16[2,128,1024]{2,1,0:T(8,128)(2,1)}, u32[]{:S(2)}) copy-start(bf16[2,128,1024]{2,1,0:T(8,128)(2,1)} %copy-done.10) | copy-start | bytes 1572868
  146.0 17.5 %all-to-all-start.7 = ((bf16[16,8,1408]{2,1,0:T(8,128)(2,1)}), bf16[16,8,1408]{2,1,0:T(8,128)(2,1)S(1)}, u32[]{:S(2)}, u32[]{:S(2)}) async-start(bf16[16,8,1408]{2,1,0:T(8,128)(2,1)} %bitcast.44), calls=%async_computation.7 | async-start | bytes 720896 | tf_op jit(solution)/shard_map/all_to_all | solution.py:40
  168.9 14.1 %all-to-all-start.8 = ((bf16[16,8,192]{2,1,0:T(8,128)(2,1)}), bf16[16,8,192]{2,1,0:T(8,128)(2,1)S(1)}, u32[]{:S(2)}, u32[]{:S(2)}) async-start(bf16[16,8,192]{2,1,0:T(8,128)(2,1)} %broadcast_in_dim.24), calls=%async_computation.8 | async-start | bytes 131072 | tf_op jit(solution)/shard_map/all_to_all | solution.py:34

commit v3 on v2

--- a/solution.py
+++ b/solution.py
@@ -1,3 +1,5 @@
+import functools
+
 import jax
 import jax.numpy as jnp
 from jax import lax
@@ -40,6 +42,23 @@
     return jnp.sum(lax.all_to_all(tiles, axis, 0, 0, tiled=True).astype(F32), axis=0)
 
 
+def swapped(array):
+    return lax.ppermute(array, "zl", [(0, 1), (1, 0)])
+
+
+def pair_sum(array):
+    index = lax.axis_index("zl")
+    kept = lax.dynamic_index_in_dim(array, index, 1, keepdims=False)
+    sent = lax.dynamic_index_in_dim(array, 1 - index, 1, keepdims=False)
+    return kept.astype(F32) + swapped(sent).astype(F32)
+
+
+def pair_join(array):
+    other = swapped(array)
+    first = lax.axis_index("zl") == 0
+    return jnp.stack([jnp.where(first, array, other), jnp.where(first, other, array)], axis=1)
+
+
 def halves(value):
     high = value.astype(BF)
     low = (value - high.astype(F32)).astype(BF)
@@ -52,6 +71,7 @@
 
 def back_kernel(
     full,
+    up_full,
     gate_w,
     up_w,
     gate_out,
@@ -75,7 +95,7 @@
     tokens = full.shape[0]
     rows, cols = gate_w.shape
     rank = gate_out.shape[0]
-    at = 3 * cols
+    at = 2 * cols
     pairs = [full[:, at + 2 * k * rank : at + 2 * (k + 1) * rank] for k in range(3)]
     factors = ((gate_out, gate_out_dir), (up_out, up_out_dir), (down_in, down_in_dir))
 
@@ -87,10 +107,9 @@
             terms[2 * k + 1] = SCALE * nn(pairs[k], jnp.concatenate([g, f], axis=0))
         for chunk in range(tokens // CHUNK):
             r = pl.ds(chunk * CHUNK, CHUNK)
-            at_up = pl.ds(pl.multiple_of(cols + block * LANES, LANES), LANES)
-            at_adj = pl.ds(pl.multiple_of(2 * cols + block * LANES, LANES), LANES)
+            at_adj = pl.ds(pl.multiple_of(cols + block * LANES, LANES), LANES)
             gate_pre = full[r, here].astype(F32) + terms[0, r, :]
-            up_pre = full[r, at_up].astype(F32) + terms[2, r, :]
+            up_pre = up_full[r, here].astype(F32) + terms[2, r, :]
             adj = full[r, at_adj].astype(F32) + terms[4, r, :]
             gate_tan, up_tan, adj_tan = terms[1, r, :], terms[3, r, :], terms[5, r, :]
             sig = 1.0 / (1.0 + jnp.exp(-gate_pre))
@@ -133,7 +152,7 @@
     curv_down[...] = SCALE * (tn(low, hd) + tn(low_dir, h))
 
 
-def backward(full, gate_w, up_w, *factors):
+def backward(full, up_full, gate_w, up_w, *factors):
     tokens = full.shape[0]
     rows, cols = gate_w.shape
     rank = factors[0].shape[0]
@@ -148,7 +167,7 @@
             curvature,
             curvature,
         ),
-        in_specs=[whole] * (3 + len(factors)),
+        in_specs=[whole] * (4 + len(factors)),
         out_specs=[whole] * 4,
         scratch_shapes=[pltpu.VMEM((6, tokens, LANES), F32)] + [panel] * 6,
         compiler_params=pltpu.CompilerParams(vmem_limit_bytes=32 * 1024 * 1024),
@@ -157,7 +176,89 @@
             bytes_accessed=2 * cols * (2 * rows + 4 * tokens),
             transcendentals=tokens * cols,
         ),
-    )(full, gate_w, up_w, *factors)
+    )(full, up_full, gate_w, up_w, *factors)
+
+
+def own_kernel(normed_ranks, left_parts, right_sum, copies, right_own):
+    cols = right_sum.shape[1]
+    total = left_parts[0].astype(F32)
+    for k in range(1, left_parts.shape[0]):
+        total += left_parts[k].astype(F32)
+    at = total.shape[1] - LANES
+    squares = total[:, at : at + 1] + total[:, at + 1 : at + 2]
+    inv_rms = lax.rsqrt(squares / D + EPSILON)
+    high = inv_rms.astype(BF).astype(F32)
+    lane = lax.broadcasted_iota(jnp.int32, (total.shape[0], LANES), 1)
+    scale = jnp.where(lane == 0, high, jnp.where(lane == 1, inv_rms - high, 0.0))
+    low = 2 * cols
+    own = jnp.concatenate(
+        [
+            total[:, :cols] * inv_rms,
+            total[:, cols:low],
+            total[:, low : low + normed_ranks] * inv_rms,
+            total[:, low + normed_ranks : at],
+            scale,
+        ],
+        axis=1,
+    ).astype(BF)
+    for k in range(copies.shape[0]):
+        copies[k] = own
+    right_own[...] = (right_sum[...] * inv_rms).astype(BF)
+
+
+def own_rows_scaled(left_parts, right_sum, normed_ranks):
+    whole = pl.BlockSpec(memory_space=pltpu.VMEM)
+    return pl.pallas_call(
+        functools.partial(own_kernel, normed_ranks),
+        out_shape=(
+            jax.ShapeDtypeStruct(left_parts.shape, BF),
+            jax.ShapeDtypeStruct(right_sum.shape, BF),
+        ),
+        in_specs=[whole] * 2,
+        out_specs=[whole] * 2,
+        compiler_params=pltpu.CompilerParams(vmem_limit_bytes=16 * 1024 * 1024),
+        cost_estimate=pl.CostEstimate(
+            flops=left_parts.size, bytes_accessed=4 * left_parts.size, transcendentals=0
+        ),
+    )(left_parts, right_sum)
+
+
+def tail_kernel(parts, gate_in, up_in, gate_in_dir, up_in_dir, adjoint, adjoint_dir, copies):
+    rank, rows = gate_in.shape
+    total = parts[0].astype(F32)
+    for k in range(1, parts.shape[0]):
+        total += parts[k].astype(F32)
+    q = total[:, 2 * rows :].astype(BF)
+    for k in range(copies.shape[0]):
+        copies[k] = q[:, 2 * rank : 5 * rank]
+    q_gate, q_up, q_gate_dir, q_up_dir = [q[:, k * rank : (k + 1) * rank] for k in range(4)]
+    gi, ui = gate_in[...], up_in[...]
+    adjoint[...] = total[:, :rows] + SCALE * (nn(q_gate, gi) + nn(q_up, ui))
+    adjoint_dir[...] = total[:, rows : 2 * rows] + SCALE * (
+        nn(q_gate_dir, gi)
+        + nn(q_gate, gate_in_dir[...])
+        + nn(q_up_dir, ui)
+        + nn(q_up, up_in_dir[...])
+    )
+
+
+def tail(parts, *factors):
+    peers, tokens, width = parts.shape
+    rank, rows = factors[0].shape
+    whole = pl.BlockSpec(memory_space=pltpu.VMEM)
+    out = jax.ShapeDtypeStruct((tokens, rows), F32)
+    return pl.pallas_call(
+        tail_kernel,
+        out_shape=(out, out, jax.ShapeDtypeStruct((peers, tokens, 3 * rank), BF)),
+        in_specs=[whole] * (1 + len(factors)),
+        out_specs=[whole] * 3,
+        compiler_params=pltpu.CompilerParams(vmem_limit_bytes=16 * 1024 * 1024),
+        cost_estimate=pl.CostEstimate(
+            flops=12 * tokens * rank * rows,
+            bytes_accessed=2 * peers * tokens * width,
+            transcendentals=0,
+        ),
+    )(parts, *factors)
 
 
 def on_device(
@@ -191,10 +292,9 @@
     scaled = (tokens_f * norm_gain).astype(BF)
     in_factors = jnp.concatenate([gate_in, gate_in_dir, up_in, up_in_dir], axis=1)
     b_factors = jnp.concatenate([down_b, down_b_dir], axis=0)
-    partial = jnp.concatenate(
+    left = jnp.concatenate(
         [
             nn(scaled, gate_w).astype(BF),
-            nn(scaled, up_w).astype(BF),
             nt(cot, down_w).astype(BF),
             nn(scaled, in_factors).astype(BF),
             nt(cot, b_factors).astype(BF),
@@ -202,23 +302,26 @@
         ],
         axis=1,
     )
-    mine = reduced(reduced(partial, "zl").astype(BF), "y")
-    at = 3 * cols + 6 * rank
-    inv_rms = lax.rsqrt((mine[:, at : at + 1] + mine[:, at + 1 : at + 2]) / D + EPSILON)
-    mine = jnp.concatenate(
-        [
-            (mine[:, : 2 * cols] * inv_rms).astype(BF),
-            mine[:, 2 * cols : 3 * cols].astype(BF),
-            (mine[:, 3 * cols : 3 * cols + 4 * rank] * inv_rms).astype(BF),
-            mine[:, 3 * cols + 4 * rank : at].astype(BF),
-            halves(inv_rms),
-        ],
-        axis=1,
-    )
-    full = spread(spread(mine, "y"), "zl")
+    right = nn(scaled, up_w).astype(BF)
+    peers = lax.axis_size("y")
+    own_rows = left.shape[0] // (2 * peers)
+    right_half = reduced(right, "y").astype(BF)
+    left_half = pair_sum(left.reshape(peers, 2, own_rows, -1)).astype(BF)
+    left_half, right_half = lax.optimization_barrier((left_half, right_half))
+    left_parts = lax.all_to_all(left_half, "y", 0, 0, tiled=True)
+    right_sum = pair_sum(right_half.reshape(1, 2, own_rows, cols))[0]
+    left_parts, right_sum = lax.optimization_barrier((left_parts, right_sum))
+    copies, right_own = own_rows_scaled(left_parts, right_sum, 4 * rank)
+    right_pair = pair_join(right_own[None]).reshape(2 * own_rows, cols)
+    left_line = lax.all_to_all(copies, "y", 0, 0, tiled=True)
+    left_line, right_pair = lax.optimization_barrier((left_line, right_pair))
+    up_full = spread(right_pair, "y")
+    full = pair_join(left_line).reshape(2 * peers * own_rows, -1)
+    at = 2 * cols + 6 * rank
     inv_all = full[:, at : at + 1].astype(F32) + full[:, at + 1 : at + 2].astype(F32)
     back, curv_gate_out, curv_up_out, curv_down_in = backward(
         full,
+        up_full,
         gate_w,
         up_w,
         gate_out,
@@ -228,20 +331,15 @@
         down_in.T,
         down_in_dir.T,
     )
-    got = reduced(reduced(back, "core").astype(BF), CHIPS)
-    q = got[:, 2 * rows : 2 * rows + 5 * rank]
-    q_all = spread(spread(q[:, 2 * rank :].astype(BF), CHIPS), "core").astype(F32)
-
-    q_gate, q_up, q_gate_dir, q_up_dir = [
-        q[:, k * rank : (k + 1) * rank].astype(BF) for k in range(4)
-    ]
-    adjoint = got[:, :rows] + SCALE * (nt(q_gate, gate_in) + nt(q_up, up_in))
-    adjoint_dir = got[:, rows : 2 * rows] + SCALE * (
-        nt(q_gate_dir, gate_in)
-        + nt(q_gate, gate_in_dir)
-        + nt(q_up_dir, up_in)
-        + nt(q_up, up_in_dir)
-    )
+    halved = reduced(back, "core").astype(BF)
+    peers = lax.axis_size(CHIPS)
+    parts = lax.all_to_all(
+        halved.reshape(peers, -1, halved.shape[1]), CHIPS, 0, 0, tiled=True
+    )
+    adjoint, adjoint_dir, copies = tail(parts, gate_in.T, up_in.T, gate_in_dir.T, up_in_dir.T)
+    q_chips = lax.all_to_all(copies, CHIPS, 0, 0, tiled=True).reshape(-1, 3 * rank)
+    q_all = spread(q_chips, "core").astype(F32)
+
     curv_in = SCALE * tn(scaled, (q_all[:, : 2 * rank] * inv_all).astype(BF))
     curv_down_out = SCALE * tn(q_all[:, 2 * rank :].astype(BF), cot)
     return (

time: 191 us -> 193 us (1.010)
  blocking collectives: 138 us -> 33.4 us
  waiting for transfers between devices: 21.6 us -> 82.3 us
  starting transfers between devices: 8.96 us -> 46.2 us
  local copies, waits for them, and re-layouts: 2.42 us -> 10.4 us
  matrix products: 8.43 us -> 5.59 us
    all_to_all x5 -> x2, blocking collectives: 78.9 us -> 14 us  [spread(): lax.all_to_all(copies, axis, 0, 0, tiled=True).reshape(-1, *array.shape[1:])]
    all_to_all x3 -> x1, blocking collectives: 59 us -> 4.42 us  [reduced(): lax.all_to_all(tiles, axis, 0, 0, tiled=True).astype(F32)]
    all_to_all x0 -> x3, waiting for transfers between devices: none -> 37.5 us  [the longest x1 14.4 us: on_device(): left_line = lax.all_to_all(copies, 'y', 0, 0, tiled=True)]
    ppermute x0 -> x4, waiting for transfers between devices: none -> 20.8 us  [swapped(): return lax.ppermute(array, 'zl', [(0, 1), (1, 0)])]
    all_to_all x0 -> x1, blocking collectives: none -> 15 us  [on_device(): lax.all_to_all(halved.reshape(peers, -1, halved.shape[1]), CHIPS, 0, 0, t...]
    all_to_all x0 -> x3, starting transfers between devices: none -> 12.9 us  [the longest x1 5.81 us: on_device(): lax.all_to_all(copies, CHIPS, 0, 0, tiled=True).reshape(-1, 3 * rank)]
    all_to_all x1 -> x2, starting transfers between devices: 5.12 us -> 16.9 us  [spread(): lax.all_to_all(copies, axis, 0, 0, tiled=True).reshape(-1, *array.shape[1:])]
    ppermute x0 -> x4, starting transfers between devices: none -> 9.54 us  [swapped(): return lax.ppermute(array, 'zl', [(0, 1), (1, 0)])]
  transfers between devices with their start and end apart: 2 -> 10, of which waited for: 2 -> 10; matrix products, arithmetic and copies ran while one was open for 1% -> 3% of each run, Pallas kernels for 0% -> 0%
where the time goes in v3:
time: 193 us; the launch traced here: 192 us
  waiting for transfers between devices  82.3 us (43%)
  starting transfers between devices  46.2 us (24%)
  blocking collectives  33.4 us (17%)
  local copies, waits for them, and re-layouts  10.4 us (5%)
  Pallas kernels  7.97 us (4%)
  matrix products  5.59 us (3%)
  other arithmetic  5 us (3%)
    ppermute x4, waiting for transfers between devices, swapped(): return lax.ppermute(array, 'zl', [(0, 1), (1, 0)])  20.8 us
    all_to_all x2, starting transfers between devices, spread(): lax.all_to_all(copies, axis, 0, 0, tiled=True).reshape(-1, *array.shape[1:])  16.9 us
    all_to_all x2, waiting for transfers between devices, spread(): lax.all_to_all(copies, axis, 0, 0, tiled=True).reshape(-1, *array.shape[1:])  15.1 us
    all_to_all x1, blocking collectives, on_device(): lax.all_to_all(halved.reshape(peers, -1, halved.shape[1]), CHIPS, 0, 0, t...  15 us
    all_to_all x1, waiting for transfers between devices, on_device(): left_line = lax.all_to_all(copies, 'y', 0, 0, tiled=True)  14.4 us
    all_to_all x1, waiting for transfers between devices, on_device(): left_parts = lax.all_to_all(left_half, 'y', 0, 0, tiled=True)  14.3 us
    all_to_all x2, blocking collectives, spread(): lax.all_to_all(copies, axis, 0, 0, tiled=True).reshape(-1, *array.shape[1:])  14 us
    ppermute x4, starting transfers between devices, swapped(): return lax.ppermute(array, 'zl', [(0, 1), (1, 0)])  9.54 us
  transfers between devices with their start and end apart: 10, of which 10 were waited for; matrix products, arithmetic and copies ran while one was open for 3% of the time, Pallas kernels for 0%

profile of v3, /device:TPU:1, one launch (start us, length us, event | category | flops | bytes accessed | tf_op | source)
XLA Modules:
  0.0 191.8 jit_solution(7682347703435828587)
XLA Ops:
  2.2 13.4 %all-to-all-start = ((bf16[16,8,1024]{2,1,0:T(8,128)(2,1)}), bf16[16,8,1024]{2,1,0:T(8,128)(2,1)S(1)}, u32[]{:S(2)}, u32[]{:S(2)}) async-start(bf16[16,8,1024]{2,1,0:T(8,128)(2,1)} %broadcast_in_dim.17), calls=%async_computation | async-start | bytes 524288 | tf_op jit(solution)/shard_map/all_to_all | solution.py:36
  15.6 10.0 %all-to-all-done = bf16[16,8,1024]{2,1,0:T(8,128)(2,1)S(1)} async-done(((bf16[16,8,1024]{2,1,0:T(8,128)(2,1)}), bf16[16,8,1024]{2,1,0:T(8,128)(2,1)S(1)}, u32[]{:S(2)}, u32[]{:S(2)}) %all-to-all-start) | async-done | bytes 262176 | tf_op jit(solution)/shard_map/all_to_all | solution.py:36
  25.7 7.3 %all_to_all.50 = bf16[2,128,1024]{2,1,0:T(8,128)(2,1)S(1)} all-to-all(bf16[2,128,1024]{2,1,0:T(8,128)(2,1)S(1)} %broadcast_in_dim.18), channel_id=1, replica_groups=mesh['zl'=2,'y'=8,'zh'=4,'x'=4,'core'=2] {'core'}, dimensions={0} | all-to-all | bytes 1048576 | tf_op jit(solution)/shard_map/all_to_all | solution.py:36
  36.0 3.1 %collective-permute-start = (bf16[8,16,2304]{2,1,0:T(8,128)(2,1)S(1)}, bf16[8,16,2304]{2,1,0:T(8,128)(2,1)}, u32[]{:S(2)}, u32[]{:S(2)}) collective-permute-start(bf16[8,16,2304]{2,1,0:T(8,128)(2,1)S(1)} %dynamic-slice_bitcast_fusion), channel_id=1, source_target_pairs={{0,256},{256,0},{1,257},{257,1},{2,258},{258,2},{3,259},{259,3},{4... | collective-permute-start | bytes 1769480 | tf_op jit(solution)/shard_map/ppermute | solution.py:46
  40.4 6.8 %all-to-all-start.2 = ((bf16[8,32,896]{2,1,0:T(8,128)(2,1)}), bf16[8,32,896]{2,1,0:T(8,128)(2,1)S(1)}, u32[]{:S(2)}, u32[]{:S(2)}) async-start(bf16[8,32,896]{2,1,0:T(8,128)(2,1)} %bitcast.6), calls=%async_computation.2 | async-start | bytes 917504 | tf_op jit(solution)/shard_map/all_to_all | solution.py:42
  47.2 5.3 %collective-permute-done = bf16[8,16,2304]{2,1,0:T(8,128)(2,1)} collective-permute-done((bf16[8,16,2304]{2,1,0:T(8,128)(2,1)S(1)}, bf16[8,16,2304]{2,1,0:T(8,128)(2,1)}, u32[]{:S(2)}, u32[]{:S(2)}) %collective-permute-start) | collective-permute-done | bytes 589856 | tf_op jit(solution)/shard_map/ppermute | solution.py:46
  52.5 2.2 %fusion.2 = bf16[8,16,2304]{2,1,0:T(8,128)(2,1)} fusion(bf16[8,16,2304]{2,1,0:T(8,128)(2,1)} %collective-permute-done, bf16[8,2,16,2304]{3,2,1,0:T(8,128)(2,1)} %bitcast.73, s32[]{:T(128)S(6)} %select_n.35), kind=kLoop, calls=%fused_computation.7 | loop fusion | flops 1179648 | bytes 1769476 | tf_op jit(solution)/shard_map/convert_element_type | solution.py:309
  54.7 9.0 %all-to-all-done.2 = bf16[8,32,896]{2,1,0:T(8,128)(2,1)S(1)} async-done(((bf16[8,32,896]{2,1,0:T(8,128)(2,1)}), bf16[8,32,896]{2,1,0:T(8,128)(2,1)S(1)}, u32[]{:S(2)}, u32[]{:S(2)}) %all-to-all-start.2) | async-done | bytes 458784 | tf_op jit(solution)/shard_map/all_to_all | solution.py:42
  63.8 3.5 %all-to-all-start.3 = ((bf16[8,16,2304]{2,1,0:T(8,128)(2,1)}), bf16[8,16,2304]{2,1,0:T(8,128)(2,1)S(1)}, u32[]{:S(2)}, u32[]{:S(2)}) async-start(bf16[8,16,2304]{2,1,0:T(8,128)(2,1)} %fusion.2), calls=%async_computation.3 | async-start | bytes 1179648 | tf_op jit(solution)/shard_map/all_to_all | solution.py:311
  67.3 2.1 %collective-permute-start.1 = (bf16[1,16,896]{2,1,0:T(8,128)(2,1)S(1)}, bf16[1,16,896]{2,1,0:T(8,128)(2,1)S(1)}, u32[]{:S(2)}, u32[]{:S(2)}) collective-permute-start(bf16[1,16,896]{2,1,0:T(8,128)(2,1)S(1)} %dynamic-slice_bitcast_fusion.1), channel_id=1, source_target_pairs={{0,256},{256,0},{1,257},{257,1},{2,258},{258,2},{3,259},{259,3},{4... | collective-permute-start | bytes 86024 | tf_op jit(solution)/shard_map/ppermute | solution.py:46
  69.5 2.8 %collective-permute-done.1 = bf16[1,16,896]{2,1,0:T(8,128)(2,1)S(1)} collective-permute-done((bf16[1,16,896]{2,1,0:T(8,128)(2,1)S(1)}, bf16[1,16,896]{2,1,0:T(8,128)(2,1)S(1)}, u32[]{:S(2)}, u32[]{:S(2)}) %collective-permute-start.1) | collective-permute-done | bytes 28704 | tf_op jit(solution)/shard_map/ppermute | solution.py:46
  72.3 14.3 %all-to-all-done.3.left_parts = bf16[8,16,2304]{2,1,0:T(8,128)(2,1)S(1)} async-done(((bf16[8,16,2304]{2,1,0:T(8,128)(2,1)}), bf16[8,16,2304]{2,1,0:T(8,128)(2,1)S(1)}, u32[]{:S(2)}, u32[]{:S(2)}) %all-to-all-start.3) | async-done | bytes 589856 | tf_op jit(solution)/shard_map/all_to_all | solution.py:311
  87.6 3.5 %all-to-all-start.4 = ((bf16[8,16,2304]{2,1,0:T(8,128)(2,1)}), bf16[8,16,2304]{2,1,0:T(8,128)(2,1)S(1)}, u32[]{:S(2)}, u32[]{:S(2)}) async-start(bf16[8,16,2304]{2,1,0:T(8,128)(2,1)} %get-tuple-element.27), calls=%async_computation.4 | async-start | bytes 1179648 | tf_op jit(solution)/shard_map/all_to_all | solution.py:316
  93.3 2.8 %collective-permute-done.2 = bf16[1,16,896]{2,1,0:T(8,128)(2,1)S(1)} collective-permute-done((bf16[1,16,896]{2,1,0:T(8,128)(2,1)S(1)}, bf16[1,16,896]{2,1,0:T(8,128)(2,1)S(1)}, u32[]{:S(2)}, u32[]{:S(2)}) %collective-permute-start.2) | collective-permute-done | bytes 28704 | tf_op jit(solution)/shard_map/ppermute | solution.py:46
  96.1 14.4 %all-to-all-done.4 = bf16[8,16,2304]{2,1,0:T(8,128)(2,1)S(1)} async-done(((bf16[8,16,2304]{2,1,0:T(8,128)(2,1)}), bf16[8,16,2304]{2,1,0:T(8,128)(2,1)S(1)}, u32[]{:S(2)}, u32[]{:S(2)}) %all-to-all-start.4) | async-done | bytes 589856 | tf_op jit(solution)/shard_map/all_to_all | solution.py:316
  113.4 3.5 %all-to-all-start.5 = ((bf16[8,32,896]{2,1,0:T(8,128)(2,1)}), bf16[8,32,896]{2,1,0:T(8,128)(2,1)S(1)}, u32[]{:S(2)}, u32[]{:S(2)}) async-start(bf16[8,32,896]{2,1,0:T(8,128)(2,1)} %broadcast_in_dim.20), calls=%async_computation.5 | async-start | bytes 917504 | tf_op jit(solution)/shard_map/all_to_all | solution.py:36
  116.9 10.0 %collective-permute-done.3 = bf16[8,16,2304]{2,1,0:T(8,128)(2,1)} collective-permute-done((bf16[8,16,2304]{2,1,0:T(8,128)(2,1)S(1)}, bf16[8,16,2304]{2,1,0:T(8,128)(2,1)}, u32[]{:S(2)}, u32[]{:S(2)}) %collective-permute-start.3) | collective-permute-done | bytes 589856 | tf_op jit(solution)/shard_map/ppermute | solution.py:46
  128.3 5.1 %all-to-all-done.5 = bf16[8,32,896]{2,1,0:T(8,128)(2,1)S(1)} async-done(((bf16[8,32,896]{2,1,0:T(8,128)(2,1)}), bf16[8,32,896]{2,1,0:T(8,128)(2,1)S(1)}, u32[]{:S(2)}, u32[]{:S(2)}) %all-to-all-start.5) | async-done | bytes 458784 | tf_op jit(solution)/shard_map/all_to_all | solution.py:36
  139.9 6.1 %shard_map.234 = (bf16[256,1408]{1,0:T(8,128)(2,1)S(1)}, f32[64,896]{1,0:T(8,128)}, f32[64,896]{1,0:T(8,128)}, f32[64,896]{1,0:T(8,128)}) custom-call(bf16[256,2304]{1,0:T(8,128)(2,1)S(1)} %bitcast.52, bf16[256,896]{1,0:T(8,128)(2,1)S(1)} %bitcast.55, bf16[512,896]{1,0:T(8,128)(2,1)S(1)} %copy-done.10, bf16[512,896]{1,0:T(8,128)(2,1)S(1)} %copy-done.1, ...), custom_call_target="tpu_custom_call" | custom-call | flops 1526726656 | bytes 3670016 | tf_op jit(solution)/shard_map/pallas_call | solution.py:162
  146.0 4.4 %all_to_all.51 = bf16[2,128,1408]{2,1,0:T(8,128)(2,1)S(1)} all-to-all(bf16[2,128,1408]{2,1,0:T(8,128)(2,1)S(1)} %bitcast.54), channel_id=1, replica_groups=mesh['zl'=2,'y'=8,'zh'=4,'x'=4,'core'=2] {'core'}, dimensions={0} | all-to-all | bytes 1441792 | tf_op jit(solution)/shard_map/all_to_all | solution.py:42
  150.7 15.0 %all_to_all.52.parts = bf16[16,8,1408]{2,1,0:T(8,128)(2,1)S(1)} all-to-all(bf16[16,8,1408]{2,1,0:T(8,128)(2,1)S(1)} %bitcast.71), channel_id=1, replica_groups=mesh['zl'=2,'y'=8,'zh'=4,'x'=4,'core'=2] {'zh','x'}, dimensions={0} | all-to-all | bytes 720896 | tf_op jit(solution)/shard_map/all_to_all | solution.py:336
  166.6 5.8 %all-to-all-start.8 = ((bf16[16,8,192]{2,1,0:T(8,128)(2,1)}), bf16[16,8,192]{2,1,0:T(8,128)(2,1)S(1)}, u32[]{:S(2)}, u32[]{:S(2)}) async-start(bf16[16,8,192]{2,1,0:T(8,128)(2,1)} %get-tuple-element.34), calls=%async_computation.8 | async-start | bytes 131072 | tf_op jit(solution)/shard_map/all_to_all | solution.py:340
  172.6 8.8 %all-to-all-done.8 = bf16[16,8,192]{2,1,0:T(8,128)(2,1)S(1)} async-done(((bf16[16,8,192]{2,1,0:T(8,128)(2,1)}), bf16[16,8,192]{2,1,0:T(8,128)(2,1)S(1)}, u32[]{:S(2)}, u32[]{:S(2)}) %all-to-all-start.8) | async-done | bytes 49184 | tf_op jit(solution)/shard_map/all_to_all | solution.py:340
  181.4 6.7 %all_to_all.53 = bf16[2,128,192]{1,2,0:T(8,128)(2,1)S(1)} all-to-all(bf16[2,128,192]{1,2,0:T(8,128)(2,1)S(1)} %broadcast_in_dim.21), channel_id=1, replica_groups=mesh['zl'=2,'y'=8,'zh'=4,'x'=4,'core'=2] {'core'}, dimensions={0} | all-to-all | bytes 196608 | tf_op jit(solution)/shard_map/all_to_all | solution.py:36
  (80 shorter events, 24.9 us)
Async XLA Ops:
  0.6 33.2 %copy-start = (bf16[896,512]{1,0:T(8,128)(2,1)S(1)}, bf16[896,512]{1,0:T(8,128)(2,1)}, u32[]{:S(2)}) copy-start(bf16[896,512]{1,0:T(8,128)(2,1)} %param.23) | copy-start | bytes 2752516
  2.2 23.5 %all-to-all-start = ((bf16[16,8,1024]{2,1,0:T(8,128)(2,1)}), bf16[16,8,1024]{2,1,0:T(8,128)(2,1)S(1)}, u32[]{:S(2)}, u32[]{:S(2)}) async-start(bf16[16,8,1024]{2,1,0:T(8,128)(2,1)} %broadcast_in_dim.17), calls=%async_computation | async-start | bytes 524288 | tf_op jit(solution)/shard_map/all_to_all | solution.py:36
  15.6 17.7 %copy-start.9 = (bf16[512,896]{1,0:T(8,128)(2,1)S(1)}, bf16[512,896]{1,0:T(8,128)(2,1)}, u32[]{:S(2)}) copy-start(bf16[512,896]{1,0:T(8,128)(2,1)} %gate_w.1) | copy-start | bytes 2752516
  15.6 17.7 %copy-start.19 = (f32[512]{0:T(512)S(1)}, f32[512]{0:T(512)}, u32[]{:S(2)}) copy-start(f32[512]{0:T(512)} %param.19) | copy-start | bytes 6148
  33.0 6.1 %copy-start.17 = (bf16[2,128,1024]{2,1,0:T(8,128)(2,1)}, bf16[2,128,1024]{2,1,0:T(8,128)(2,1)S(1)}, u32[]{:S(2)}) copy-start(bf16[2,128,1024]{2,1,0:T(8,128)(2,1)S(1)} %all_to_all.50) | copy-start | bytes 1572868
  33.8 0.9 copy-start.7
  35.6 3.5 %copy-start.1 = (bf16[512,896]{1,0:T(8,128)(2,1)S(1)}, bf16[512,896]{1,0:T(8,128)(2,1)}, u32[]{:S(2)}) copy-start(bf16[512,896]{1,0:T(8,128)(2,1)} %up_w.1) | copy-start | bytes 2752516
  35.9 4.5 %copy-start.18 = (bf16[256,2304]{1,0:T(8,128)(2,1)}, bf16[256,2304]{1,0:T(8,128)(2,1)S(1)}, u32[]{:S(2)}) copy-start(bf16[256,2304]{1,0:T(8,128)(2,1)S(1)} %pad_dynamic-update-slice_fusion) | copy-start | bytes 3538948
  36.0 16.5 %collective-permute-start = (bf16[8,16,2304]{2,1,0:T(8,128)(2,1)S(1)}, bf16[8,16,2304]{2,1,0:T(8,128)(2,1)}, u32[]{:S(2)}, u32[]{:S(2)}) collective-permute-start(bf16[8,16,2304]{2,1,0:T(8,128)(2,1)S(1)} %dynamic-slice_bitcast_fusion), channel_id=1, source_target_pairs={{0,256},{256,0},{1,257},{257,1},{2,258},{258,2},{3,259},{259,3},{4... | collective-permute-start | bytes 1769480 | tf_op jit(solution)/shard_map/ppermute | solution.py:46
  40.4 23.3 %all-to-all-start.2 = ((bf16[8,32,896]{2,1,0:T(8,128)(2,1)}), bf16[8,32,896]{2,1,0:T(8,128)(2,1)S(1)}, u32[]{:S(2)}, u32[]{:S(2)}) async-start(bf16[8,32,896]{2,1,0:T(8,128)(2,1)} %bitcast.6), calls=%async_computation.2 | async-start | bytes 917504 | tf_op jit(solution)/shard_map/all_to_all | solution.py:42
  63.8 22.8 %all-to-all-start.3 = ((bf16[8,16,2304]{2,1,0:T(8,128)(2,1)}), bf16[8,16,2304]{2,1,0:T(8,128)(2,1)S(1)}, u32[]{:S(2)}, u32[]{:S(2)}) async-start(bf16[8,16,2304]{2,1,0:T(8,128)(2,1)} %fusion.2), calls=%async_computation.3 | async-start | bytes 1179648 | tf_op jit(solution)/shard_map/all_to_all | solution.py:311
  67.3 4.9 %collective-permute-start.1 = (bf16[1,16,896]{2,1,0:T(8,128)(2,1)S(1)}, bf16[1,16,896]{2,1,0:T(8,128)(2,1)S(1)}, u32[]{:S(2)}, u32[]{:S(2)}) collective-permute-start(bf16[1,16,896]{2,1,0:T(8,128)(2,1)S(1)} %dynamic-slice_bitcast_fusion.1), channel_id=1, source_target_pairs={{0,256},{256,0},{1,257},{257,1},{2,258},{258,2},{3,259},{259,3},{4... | collective-permute-start | bytes 86024 | tf_op jit(solution)/shard_map/ppermute | solution.py:46
  87.6 22.9 %all-to-all-start.4 = ((bf16[8,16,2304]{2,1,0:T(8,128)(2,1)}), bf16[8,16,2304]{2,1,0:T(8,128)(2,1)S(1)}, u32[]{:S(2)}, u32[]{:S(2)}) async-start(bf16[8,16,2304]{2,1,0:T(8,128)(2,1)} %get-tuple-element.27), calls=%async_computation.4 | async-start | bytes 1179648 | tf_op jit(solution)/shard_map/all_to_all | solution.py:316
  91.2 4.9 %collective-permute-start.2 = (bf16[1,16,896]{2,1,0:T(8,128)(2,1)S(1)}, bf16[1,16,896]{2,1,0:T(8,128)(2,1)S(1)}, u32[]{:S(2)}, u32[]{:S(2)}) collective-permute-start(bf16[1,16,896]{2,1,0:T(8,128)(2,1)S(1)} %bitcast.60), channel_id=1, source_target_pairs={{0,256},{256,0},{1,257},{257,1},{2,258},{258,2},{3,259},{259,3},{4... | collective-permute-start | bytes 86024 | tf_op jit(solution)/shard_map/ppermute | solution.py:46
  110.5 16.4 %collective-permute-start.3 = (bf16[8,16,2304]{2,1,0:T(8,128)(2,1)S(1)}, bf16[8,16,2304]{2,1,0:T(8,128)(2,1)}, u32[]{:S(2)}, u32[]{:S(2)}) collective-permute-start(bf16[8,16,2304]{2,1,0:T(8,128)(2,1)S(1)} %all-to-all-done.4), channel_id=1, source_target_pairs={{0,256},{256,0},{1,257},{257,1},{2,258},{258,2},{3,259},{259,3},{4... | collective-permute-start | bytes 1769480 | tf_op jit(solution)/shard_map/ppermute | solution.py:46
  113.4 19.9 %all-to-all-start.5 = ((bf16[8,32,896]{2,1,0:T(8,128)(2,1)}), bf16[8,32,896]{2,1,0:T(8,128)(2,1)S(1)}, u32[]{:S(2)}, u32[]{:S(2)}) async-start(bf16[8,32,896]{2,1,0:T(8,128)(2,1)} %broadcast_in_dim.20), calls=%async_computation.5 | async-start | bytes 917504 | tf_op jit(solution)/shard_map/all_to_all | solution.py:36
  133.4 1.2 copy-start.10
  134.5 0.9 copy-start.11
  135.4 0.9 copy-start.12
  136.3 0.9 copy-start.13
  150.4 15.2 %copy-start.4 = (bf16[512,64]{0,1:T(8,128)(2,1)S(1)}, bf16[512,64]{0,1:T(8,128)(2,1)}, u32[]{:S(2)}) copy-start(bf16[512,64]{0,1:T(8,128)(2,1)} %param.26) | copy-start | bytes 196612
  150.4 15.2 %copy-start.6 = (bf16[512,64]{0,1:T(8,128)(2,1)S(1)}, bf16[512,64]{0,1:T(8,128)(2,1)}, u32[]{:S(2)}) copy-start(bf16[512,64]{0,1:T(8,128)(2,1)} %param.30) | copy-start | bytes 196612
  150.4 15.2 %copy-start.8 = (bf16[512,64]{0,1:T(8,128)(2,1)S(1)}, bf16[512,64]{0,1:T(8,128)(2,1)}, u32[]{:S(2)}) copy-start(bf16[512,64]{0,1:T(8,128)(2,1)} %param.24) | copy-start | bytes 196612
  166.6 14.8 %all-to-all-start.8 = ((bf16[16,8,192]{2,1,0:T(8,128)(2,1)}), bf16[16,8,192]{2,1,0:T(8,128)(2,1)S(1)}, u32[]{:S(2)}, u32[]{:S(2)}) async-start(bf16[16,8,192]{2,1,0:T(8,128)(2,1)} %get-tuple-element.34), calls=%async_computation.8 | async-start | bytes 131072 | tf_op jit(solution)/shard_map/all_to_all | solution.py:340
  (8 other events, 7.0 us)

commit v4 on v3

v4 whole, which is shorter than its diff:
```python
import functools

import jax
import jax.numpy as jnp
from jax import lax
from jax.experimental import pallas as pl
from jax.experimental.pallas import tpu as pltpu
from jax.sharding import Mesh
from jax.sharding import PartitionSpec as P

D = 8192
ROW = ("zl", "y")
CHIPS = ("zh", "x")
COL = ("zh", "x", "core")
SCALE = 0.5
EPSILON = 1e-05
BF = jnp.bfloat16
F32 = jnp.float32


def nn(left, right):
    return lax.dot_general(left, right, (((1,), (0,)), ((), ())), preferred_element_type=F32)


def nt(left, right):
    return lax.dot_general(left, right, (((1,), (1,)), ((), ())), preferred_element_type=F32)


def tn(left, right):
    return lax.dot_general(left, right, (((0,), (0,)), ((), ())), preferred_element_type=F32)


def spread(array, axis):
    peers = lax.axis_size(axis)
    copies = jnp.broadcast_to(array, (peers, *array.shape))
    return lax.all_to_all(copies, axis, 0, 0, tiled=True).reshape(-1, *array.shape[1:])


def reduced(array, axis):
    peers = lax.axis_size(axis)
    tiles = array.reshape(peers, array.shape[0] // peers, *array.shape[1:])
    return jnp.sum(lax.all_to_all(tiles, axis, 0, 0, tiled=True).astype(F32), axis=0)


def swapped(array):
    return lax.ppermute(array, "zl", [(0, 1), (1, 0)])


def pair_sum(array):
    index = lax.axis_index("zl")
    kept = lax.dynamic_index_in_dim(array, index, 1, keepdims=False)
    sent = lax.dynamic_index_in_dim(array, 1 - index, 1, keepdims=False)
    return kept.astype(F32) + swapped(sent).astype(F32)


def pair_join(array):
    other = swapped(array)
    first = lax.axis_index("zl") == 0
    return jnp.stack([jnp.where(first, array, other), jnp.where(first, other, array)], axis=1)


def partner(array, axis, bit):
    return lax.ppermute(array, axis, [(k, k ^ bit) for k in range(lax.axis_size(axis))])


def pair_of(low, first, second):
    return jnp.concatenate([jnp.where(low, first, second), jnp.where(low, second, first)], axis=0)


def doubled(array, axis, bit):
    return pair_of((lax.axis_index(axis) & bit) == 0, array, partner(array, axis, bit))


def quadrupled(array, axis):
    one, two, three = [partner(array, axis, k) for k in (1, 2, 3)]
    index = lax.axis_index(axis)
    low = (index & 1) == 0
    return pair_of((index & 2) == 0, pair_of(low, array, one), pair_of(low, two, three))


def four_sum(array, axis):
    one, two, three = [partner(array, axis, k) for k in (1, 2, 3)]
    return (array + one) + (two + three)


LANES = 128
CHUNK = 32


def second_order(gate_pre, up_pre, adj, gate_tan, up_tan, adj_tan):
    sig = 1.0 / (1.0 + jnp.exp(-gate_pre))
    rest = 1.0 - sig
    act = gate_pre * sig
    slope = sig * (1.0 + gate_pre * rest)
    bend = sig * rest * (2.0 + gate_pre * (1.0 - 2.0 * sig))
    slope_tan = slope * gate_tan
    up_slope = up_pre * slope
    return (
        (act * up_pre).astype(BF),
        (slope_tan * up_pre + act * up_tan).astype(BF),
        (adj * up_slope).astype(BF),
        (adj * act).astype(BF),
        (adj_tan * up_slope + adj * (up_tan * slope + up_pre * bend * gate_tan)).astype(BF),
        (adj_tan * act + adj * slope_tan).astype(BF),
    )


def adapter_terms(pair, plain, direction):
    rank = plain.shape[0]
    term = SCALE * nn(pair[:, :rank], plain)
    return term, SCALE * nn(pair, jnp.concatenate([direction, plain], axis=0))


def own_q_kernel(own, right_own, gate_out, gate_dir, up_out, up_dir, down_in, down_dir, q):
    rank, cols = gate_out.shape
    at = 2 * cols
    pairs = [own[:, at + 2 * k * rank : at + 2 * (k + 1) * rank] for k in range(3)]
    go, god, uo, uod = gate_out[...], gate_dir[...], up_out[...], up_dir[...]
    di, did = down_in[...], down_dir[...]
    gate_term, gate_tan = adapter_terms(pairs[0], go, god)
    up_term, up_tan = adapter_terms(pairs[1], uo, uod)
    adj_term, adj_tan = adapter_terms(pairs[2], di, did)
    h, hd, dg, du, dgd, dud = second_order(
        own[:, :cols].astype(F32) + gate_term,
        right_own[...].astype(F32) + up_term,
        own[:, cols:at].astype(F32) + adj_term,
        gate_tan,
        up_tan,
        adj_tan,
    )
    low_dir = nt(hd, di) + nt(h, did)
    q[...] = jnp.concatenate(
        [
            nt(dg, go),
            nt(du, uo),
            nt(dgd, go) + nt(dg, god),
            nt(dud, uo) + nt(du, uod),
            low_dir,
            jnp.zeros_like(low_dir),
        ],
        axis=1,
    )


def own_q(copies, right_own, *factors):
    rows, rank = right_own.shape[0], factors[0].shape[0]
    cols = factors[0].shape[1]
    whole = pl.BlockSpec(memory_space=pltpu.VMEM)
    return pl.pallas_call(
        own_q_kernel,
        out_shape=jax.ShapeDtypeStruct((rows, 6 * rank), F32),
        in_specs=[whole] * (2 + len(factors)),
        out_specs=whole,
        compiler_params=pltpu.CompilerParams(vmem_limit_bytes=16 * 1024 * 1024),
        cost_estimate=pl.CostEstimate(
            flops=40 * rows * cols * rank,
            bytes_accessed=12 * rank * cols,
            transcendentals=rows * cols,
        ),
    )(copies, right_own, *factors)


def back_kernel(
    full,
    up_full,
    gate_w_hbm,
    up_w_hbm,
    factors_hbm_0,
    factors_hbm_1,
    factors_hbm_2,
    factors_hbm_3,
    factors_hbm_4,
    factors_hbm_5,
    back,
    curv_gate,
    curv_up,
    curv_down,
    terms,
    d_gate,
    d_up,
    d_gate_dir,
    d_up_dir,
    hidden,
    hidden_dir,
    gate_w,
    up_w,
    factors,
    sems,
):
    tokens = full.shape[0]
    rows, cols = gate_w.shape
    rank = factors.shape[1]
    at = 2 * cols
    hbm = (
        factors_hbm_0,
        factors_hbm_1,
        factors_hbm_2,
        factors_hbm_3,
        factors_hbm_4,
        factors_hbm_5,
    )
    loads = [pltpu.make_async_copy(hbm[k], factors.at[k], sems.at[k]) for k in range(6)]
    loads.append(pltpu.make_async_copy(gate_w_hbm, gate_w, sems.at[6]))
    loads.append(pltpu.make_async_copy(up_w_hbm, up_w, sems.at[7]))
    for load in loads:
        load.start()
    pairs = [full[:, at + 2 * k * rank : at + 2 * (k + 1) * rank] for k in range(3)]
    for load in loads[:6]:
        load.wait()

    def column_block(block, carry):
        here = pl.ds(pl.multiple_of(block * LANES, LANES), LANES)
        at_adj = pl.ds(pl.multiple_of(cols + block * LANES, LANES), LANES)
        for k in range(3):
            term, tan = adapter_terms(pairs[k], factors[2 * k, :, here], factors[2 * k + 1, :, here])
            terms[2 * k] = term
            terms[2 * k + 1] = tan
        for chunk in range(tokens // CHUNK):
            r = pl.ds(chunk * CHUNK, CHUNK)
            (
                hidden[r, here],
                hidden_dir[r, here],
                d_gate[r, here],
                d_up[r, here],
                d_gate_dir[r, here],
                d_up_dir[r, here],
            ) = second_order(
                full[r, here].astype(F32) + terms[0, r, :],
                up_full[r, here].astype(F32) + terms[2, r, :],
                full[r, at_adj].astype(F32) + terms[4, r, :],
                terms[1, r, :],
                terms[3, r, :],
                terms[5, r, :],
            )
        return carry

    lax.fori_loop(0, cols // LANES, column_block, 0)
    for load in loads[6:]:
        load.wait()
    dg, du, dgd, dud = d_gate[...], d_up[...], d_gate_dir[...], d_up_dir[...]
    h, hd = hidden[...], hidden_dir[...]
    gw, uw = gate_w[...], up_w[...]
    back[:, :rows] = (nt(dg, gw) + nt(du, uw)).astype(BF)
    back[:, rows:] = (nt(dgd, gw) + nt(dud, uw)).astype(BF)
    low, low_dir = pairs[0][:, :rank], pairs[0][:, rank:]
    curv_gate[...] = SCALE * (tn(low_dir, dg) + tn(low, dgd))
    low, low_dir = pairs[1][:, :rank], pairs[1][:, rank:]
    curv_up[...] = SCALE * (tn(low_dir, du) + tn(low, dud))
    low, low_dir = pairs[2][:, :rank], pairs[2][:, rank:]
    curv_down[...] = SCALE * (tn(low, hd) + tn(low_dir, h))


def backward(full, up_full, gate_w, up_w, *factors):
    tokens = full.shape[0]
    rows, cols = gate_w.shape
    rank = factors[0].shape[0]
    whole = pl.BlockSpec(memory_space=pltpu.VMEM)
    anywhere = pl.BlockSpec(memory_space=pl.ANY)
    curvature = jax.ShapeDtypeStruct((rank, cols), F32)
    panel = pltpu.VMEM((tokens, cols), BF)
    weight = pltpu.VMEM((rows, cols), BF)
    return pl.pallas_call(
        back_kernel,
        out_shape=(
            jax.ShapeDtypeStruct((tokens, 2 * rows), BF),
            curvature,
            curvature,
            curvature,
        ),
        in_specs=[whole] * 2 + [anywhere] * (2 + len(factors)),
        out_specs=[whole] * 4,
        scratch_shapes=[pltpu.VMEM((6, tokens, LANES), F32)]
        + [panel] * 6
        + [weight, weight]
        + [pltpu.VMEM((6, rank, cols), BF), pltpu.SemaphoreType.DMA((8,))],
        compiler_params=pltpu.CompilerParams(vmem_limit_bytes=32 * 1024 * 1024),
        cost_estimate=pl.CostEstimate(
            flops=2 * tokens * cols * (4 * rows + 15 * rank),
            bytes_accessed=2 * cols * (2 * rows + 4 * tokens),
            transcendentals=tokens * cols,
        ),
    )(full, up_full, gate_w, up_w, *factors)


def spread_kernel(flag, scaled, panel, gate_w, down_w, gi, gid, ui, uid, db, dbd, kept, sent):
    rows, cols = gate_w.shape
    peers, own_rows = kept.shape[:2]
    tokens_f = panel[:, :rows].astype(F32)
    squares = jnp.sum(tokens_f * tokens_f, axis=1, keepdims=True)
    high = squares.astype(BF).astype(F32)
    lane = lax.broadcasted_iota(jnp.int32, (tokens_f.shape[0], LANES), 1)
    first = flag[0] == 0

    def put(value, at):
        value = value.astype(F32).reshape(peers, 2, own_rows, value.shape[1])
        here = slice(at, at + value.shape[3])
        zero, one = value[:, 0], value[:, 1]
        kept[:, :, here] = jnp.where(first, zero, one).astype(BF)
        sent[:, :, here] = jnp.where(first, one, zero).astype(BF)

    x, cot = scaled[...], panel[:, rows:]
    put(nn(x, gate_w[...]), 0)
    put(nt(cot, down_w[...]), cols)
    at = 2 * cols
    for left, factors in ((x, (gi, gid)), (x, (ui, uid)), (cot, (db, dbd))):
        both = jnp.concatenate([factors[0][...], factors[1][...]], axis=0)
        put(nt(left, both), at)
        at += both.shape[0]
    put(jnp.where(lane == 0, high, jnp.where(lane == 1, squares - high, 0.0)), at)


def forward(flag, scaled, panel, gate_w, down_w, peers, *factors):
    tokens = scaled.shape[0]
    rows, cols = gate_w.shape
    rank = factors[0].shape[0]
    whole = pl.BlockSpec(memory_space=pltpu.VMEM)
    half = jax.ShapeDtypeStruct(
        (peers, tokens // (2 * peers), 2 * cols + 6 * rank + LANES), BF
    )
    return pl.pallas_call(
        spread_kernel,
        out_shape=(half, half),
        in_specs=[pl.BlockSpec(memory_space=pltpu.SMEM)] + [whole] * (4 + len(factors)),
        out_specs=[whole] * 2,
        compiler_params=pltpu.CompilerParams(vmem_limit_bytes=32 * 1024 * 1024),
        cost_estimate=pl.CostEstimate(
            flops=4 * tokens * rows * (cols + 3 * rank),
            bytes_accessed=4 * rows * cols,
            transcendentals=0,
        ),
    )(flag, scaled, panel, gate_w, down_w, *factors)


def own_kernel(normed_ranks, left_parts, right_sum, copies, right_own):
    cols = right_sum.shape[1]
    total = left_parts[0].astype(F32)
    for k in range(1, left_parts.shape[0]):
        total += left_parts[k].astype(F32)
    at = total.shape[1] - LANES
    squares = total[:, at : at + 1] + total[:, at + 1 : at + 2]
    inv_rms = lax.rsqrt(squares / D + EPSILON)
    high = inv_rms.astype(BF).astype(F32)
    lane = lax.broadcasted_iota(jnp.int32, (total.shape[0], LANES), 1)
    scale = jnp.where(lane == 0, high, jnp.where(lane == 1, inv_rms - high, 0.0))
    low = 2 * cols
    own = jnp.concatenate(
        [
            total[:, :cols] * inv_rms,
            total[:, cols:low],
            total[:, low : low + normed_ranks] * inv_rms,
            total[:, low + normed_ranks : at],
            scale,
        ],
        axis=1,
    ).astype(BF)
    for k in range(copies.shape[0]):
        copies[k] = own
    right_own[...] = (right_sum[...] * inv_rms).astype(BF)


def own_rows_scaled(left_parts, right_sum, normed_ranks):
    whole = pl.BlockSpec(memory_space=pltpu.VMEM)
    return pl.pallas_call(
        functools.partial(own_kernel, normed_ranks),
        out_shape=(
            jax.ShapeDtypeStruct(left_parts.shape, BF),
            jax.ShapeDtypeStruct(right_sum.shape, BF),
        ),
        in_specs=[whole] * 2,
        out_specs=[whole] * 2,
        compiler_params=pltpu.CompilerParams(vmem_limit_bytes=16 * 1024 * 1024),
        cost_estimate=pl.CostEstimate(
            flops=left_parts.size, bytes_accessed=4 * left_parts.size, transcendentals=0
        ),
    )(left_parts, right_sum)


def curvature_kernel(q_all, scaled, cot, block, gate, up, down):
    rank = gate.shape[0]
    q = q_all[...].astype(F32)
    last = block[...].astype(F32)
    inv_rms = last[:, :1] + last[:, 1:2]
    x, c = scaled[...], cot[...]
    gate[...] = tn((q[:, 2 * rank : 3 * rank] * inv_rms).astype(BF), x)
    up[...] = tn((q[:, 3 * rank : 4 * rank] * inv_rms).astype(BF), x)
    down[...] = tn(q[:, 4 * rank : 5 * rank].astype(BF), c)


def curvatures(q_all, scaled, cot, block, rank):
    tokens, rows = scaled.shape
    whole = pl.BlockSpec(memory_space=pltpu.VMEM)
    out = jax.ShapeDtypeStruct((rank, rows), F32)
    return pl.pallas_call(
        curvature_kernel,
        out_shape=(out, out, out),
        in_specs=[whole] * 4,
        out_specs=[whole] * 3,
        compiler_params=pltpu.CompilerParams(vmem_limit_bytes=16 * 1024 * 1024),
        cost_estimate=pl.CostEstimate(
            flops=6 * tokens * rank * rows,
            bytes_accessed=4 * tokens * rows,
            transcendentals=0,
        ),
    )(q_all, scaled, cot, block)


def tail_kernel(parts, q_own, gate_in, up_in, gate_in_dir, up_in_dir, adjoint, adjoint_dir):
    rank, rows = gate_in.shape
    total = parts[0].astype(F32)
    for k in range(1, parts.shape[0]):
        total += parts[k].astype(F32)
    q = q_own[...]
    q_gate, q_up, q_gate_dir, q_up_dir = [q[:, k * rank : (k + 1) * rank] for k in range(4)]
    gi, ui = gate_in[...], up_in[...]
    adjoint[...] = total[:, :rows] + nn(q_gate, gi) + nn(q_up, ui)
    adjoint_dir[...] = total[:, rows:] + (
        nn(q_gate_dir, gi)
        + nn(q_gate, gate_in_dir[...])
        + nn(q_up_dir, ui)
        + nn(q_up, up_in_dir[...])
    )


def tail(parts, q_own, *factors):
    peers, tokens, width = parts.shape
    rank, rows = factors[0].shape
    whole = pl.BlockSpec(memory_space=pltpu.VMEM)
    out = jax.ShapeDtypeStruct((tokens, rows), F32)
    return pl.pallas_call(
        tail_kernel,
        out_shape=(out, out),
        in_specs=[whole] * (2 + len(factors)),
        out_specs=[whole] * 2,
        compiler_params=pltpu.CompilerParams(vmem_limit_bytes=16 * 1024 * 1024),
        cost_estimate=pl.CostEstimate(
            flops=12 * tokens * rank * rows,
            bytes_accessed=2 * peers * tokens * width,
            transcendentals=0,
        ),
    )(parts, q_own, *factors)


def on_device(
    tokens,
    norm_gain,
    cotangent,
    gate_w,
    up_w,
    down_w,
    gate_in,
    gate_out,
    up_in,
    up_out,
    down_in,
    down_b,
    gate_in_dir,
    gate_out_dir,
    up_in_dir,
    up_out_dir,
    down_in_dir,
    down_b_dir,
):
    rank = gate_in.shape[1]
    rows = gate_w.shape[0]
    cols = gate_w.shape[1]
    own = jnp.concatenate([tokens, cotangent], axis=1)
    panel = spread(spread(own, CHIPS), "core")
    cot = panel[:, rows:]
    scaled = (panel[:, :rows].astype(F32) * norm_gain).astype(BF)
    right = nn(scaled, up_w).astype(BF)
    scaled, right = lax.optimization_barrier((scaled, right))
    peers = lax.axis_size("y")
    own_rows = right.shape[0] // (2 * peers)
    flag = jnp.full((1,), lax.axis_index("zl"), jnp.int32)
    kept, sent = forward(
        flag,
        scaled,
        panel,
        gate_w,
        down_w,
        peers,
        gate_in.T,
        gate_in_dir.T,
        up_in.T,
        up_in_dir.T,
        down_b,
        down_b_dir,
    )
    right_half = reduced(right, "y").astype(BF)
    left_half = (kept.astype(F32) + swapped(sent).astype(F32)).astype(BF)
    left_half, right_half = lax.optimization_barrier((left_half, right_half))
    left_parts = lax.all_to_all(left_half, "y", 0, 0, tiled=True)
    right_sum = pair_sum(right_half.reshape(1, 2, own_rows, cols))[0]
    left_parts, right_sum = lax.optimization_barrier((left_parts, right_sum))
    copies, right_own = own_rows_scaled(left_parts, right_sum, 4 * rank)
    out_factors = (gate_out, gate_out_dir, up_out, up_out_dir, down_in.T, down_in_dir.T)

    q = own_q(copies[0], right_own, *out_factors)
    q = q + partner(q, "core", 1)
    q = four_sum(four_sum(q, "x"), "zh")
    q = (q * SCALE).astype(BF)

    right_pair = pair_join(right_own[None]).reshape(2 * own_rows, cols)
    left_line = lax.all_to_all(copies, "y", 0, 0, tiled=True)
    left_line, right_pair, q = lax.optimization_barrier((left_line, right_pair, q))
    up_full = spread(right_pair, "y")
    q = doubled(q, "zl", 1)
    full = pair_join(left_line).reshape(2 * peers * own_rows, -1)
    full, up_full, q = lax.optimization_barrier((full, up_full, q))
    q = doubled(q, "y", 1)
    back, curv_gate_out, curv_up_out, curv_down_in = backward(
        full, up_full, gate_w, up_w, *out_factors
    )
    back, q = lax.optimization_barrier((back, q))
    q = doubled(q, "y", 2)
    halved = reduced(back, "core").astype(BF)
    halved, q = lax.optimization_barrier((halved, q))
    chips = lax.axis_size(CHIPS)
    parts = lax.all_to_all(
        halved.reshape(chips, -1, halved.shape[1]), CHIPS, 0, 0, tiled=True
    )
    q_all = doubled(q, "y", 4)
    curv_gate_in, curv_up_in, curv_down_out = curvatures(
        q_all, scaled, cot, full[:, 2 * cols + 6 * rank :], rank
    )
    count = tokens.shape[0]
    place = lax.axis_index("core") * chips + lax.axis_index(CHIPS)
    q_own = lax.dynamic_slice_in_dim(q_all, place * count, count, 0)
    adjoint, adjoint_dir = tail(parts, q_own, gate_in.T, up_in.T, gate_in_dir.T, up_in_dir.T)
    return (
        adjoint,
        adjoint_dir,
        curv_gate_in.T,
        curv_gate_out,
        curv_up_in.T,
        curv_up_out,
        curv_down_in.T,
        curv_down_out,
    )


def solution(mesh):
    split = Mesh(mesh.devices.reshape(2, 8, 4, 4, 2), ("zl", "y", "zh", "x", "core"))
    features = P(ROW, None)
    hidden = P(None, COL)
    return jax.shard_map(
        on_device,
        mesh=split,
        in_specs=(
            P(COL, ROW),
            P(ROW),
            P(COL, ROW),
            P(ROW, COL),
            P(ROW, COL),
            P(COL, ROW),
            features,
            hidden,
            features,
            hidden,
            P(COL, None),
            P(None, ROW),
            features,
            hidden,
            features,
            hidden,
            P(COL, None),
            P(None, ROW),
        ),
        out_specs=(
            P(COL, ROW),
            P(COL, ROW),
            features,
            hidden,
            features,
            hidden,
            P(COL, None),
            P(None, ROW),
        ),
        check_vma=False,
    )
```

time: 193 us -> 201 us (1.041)
  starting transfers between devices: 46.2 us -> 85.5 us
  waiting for transfers between devices: 82.3 us -> 65.4 us
  blocking collectives: 33.4 us -> 17.8 us
  matrix products: 5.59 us -> 1.21 us
  Pallas kernels: 7.97 us -> 11.9 us
    ppermute x0 -> x11, starting transfers between devices: none -> 33.9 us  [partner(): lax.ppermute(array, axis, [(k, k ^ bit) for k in range(lax.axis_size(axis...]
    all_to_all x1 -> x0, blocking collectives: 15 us -> none  [on_device(): lax.all_to_all(halved.reshape(peers, -1, halved.shape[1]), CHIPS, 0, 0, t...]
    all_to_all x1, waiting for transfers between devices: 14.4 us -> 0.01 us  [on_device(): left_line = lax.all_to_all(copies, 'y', 0, 0, tiled=True)]
    ppermute x4, waiting for transfers between devices: 20.8 us -> 9.43 us  [swapped(): return lax.ppermute(array, 'zl', [(0, 1), (1, 0)])]
    ppermute x0 -> x11, waiting for transfers between devices: none -> 6.69 us  [partner(): lax.ppermute(array, axis, [(k, k ^ bit) for k in range(lax.axis_size(axis...]
    all_to_all x2 -> x1, blocking collectives: 14 us -> 7.41 us  [spread(): lax.all_to_all(copies, axis, 0, 0, tiled=True).reshape(-1, *array.shape[1:])]
    all_to_all x1, blocking collectives: 4.42 us -> 10.4 us  [reduced(): lax.all_to_all(tiles, axis, 0, 0, tiled=True).astype(F32)]
    dot_general x4 -> x0, matrix products: 3.65 us -> none  [the longest x2 2.92 us: tn(): lax.dot_general(left, right, (((0,), (0,)), ((), ())), preferred_element_...]
  transfers between devices with their start and end apart: 10 -> 21, of which waited for: 10 -> 14; matrix products, arithmetic and copies ran while one was open for 3% -> 3% of each run, Pallas kernels for 0% -> 4%
where the time goes in v4:
time: 201 us; the launch traced here: 198 us
  starting transfers between devices  85.5 us (43%)
  waiting for transfers between devices  65.4 us (33%)
  blocking collectives  17.8 us (9%)
  Pallas kernels  11.9 us (6%)
  local copies, waits for them, and re-layouts  11.4 us (6%)
  other arithmetic  4.1 us (2%)
    ppermute x11, starting transfers between devices, partner(): lax.ppermute(array, axis, [(k, k ^ bit) for k in range(lax.axis_size(axis...  33.9 us
    all_to_all x2, starting transfers between devices, spread(): lax.all_to_all(copies, axis, 0, 0, tiled=True).reshape(-1, *array.shape[1:])  19.9 us
    all_to_all x2, waiting for transfers between devices, spread(): lax.all_to_all(copies, axis, 0, 0, tiled=True).reshape(-1, *array.shape[1:])  18.5 us
    all_to_all x1, waiting for transfers between devices, on_device(): left_parts = lax.all_to_all(left_half, 'y', 0, 0, tiled=True)  14.1 us
    ppermute x4, starting transfers between devices, swapped(): return lax.ppermute(array, 'zl', [(0, 1), (1, 0)])  11.1 us
    all_to_all x1, blocking collectives, reduced(): lax.all_to_all(tiles, axis, 0, 0, tiled=True).astype(F32)  10.4 us
    ppermute x4, waiting for transfers between devices, swapped(): return lax.ppermute(array, 'zl', [(0, 1), (1, 0)])  9.43 us
    all_to_all x1, waiting for transfers between devices, reduced(): lax.all_to_all(tiles, axis, 0, 0, tiled=True).astype(F32)  8.85 us
  transfers between devices with their start and end apart: 21, of which 14 were waited for; matrix products, arithmetic and copies ran while one was open for 3% of the time, Pallas kernels for 4%

profile of v4, /device:TPU:1, one launch (start us, length us, event | category | flops | bytes accessed | tf_op | source)
XLA Modules:
  0.0 198.4 jit_solution(16791439745092430639)
XLA Ops:
  2.1 13.6 %all-to-all-start = ((bf16[16,8,1024]{2,1,0:T(8,128)(2,1)}), bf16[16,8,1024]{2,1,0:T(8,128)(2,1)S(1)}, u32[]{:S(2)}, u32[]{:S(2)}) async-start(bf16[16,8,1024]{2,1,0:T(8,128)(2,1)} %broadcast_in_dim.17), calls=%async_computation | async-start | bytes 524288 | tf_op jit(solution)/shard_map/all_to_all | solution.py:36
  15.7 10.1 %all-to-all-done = bf16[16,8,1024]{2,1,0:T(8,128)(2,1)S(1)} async-done(((bf16[16,8,1024]{2,1,0:T(8,128)(2,1)}), bf16[16,8,1024]{2,1,0:T(8,128)(2,1)S(1)}, u32[]{:S(2)}, u32[]{:S(2)}) %all-to-all-start) | async-done | bytes 262176 | tf_op jit(solution)/shard_map/all_to_all | solution.py:36
  25.8 7.4 %all_to_all.40 = bf16[2,128,1024]{2,1,0:T(8,128)(2,1)S(1)} all-to-all(bf16[2,128,1024]{2,1,0:T(8,128)(2,1)S(1)} %broadcast_in_dim.18), channel_id=1, replica_groups=mesh['zl'=2,'y'=8,'zh'=4,'x'=4,'core'=2] {'core'}, dimensions={0} | all-to-all | bytes 1048576 | tf_op jit(solution)/shard_map/all_to_all | solution.py:36
  36.6 3.1 %collective-permute-start = (bf16[8,16,2304]{2,1,0:T(8,128)(2,1)}, bf16[8,16,2304]{2,1,0:T(8,128)(2,1)S(1)}, u32[]{:S(2)}, u32[]{:S(2)}) collective-permute-start(bf16[8,16,2304]{2,1,0:T(8,128)(2,1)} %get-tuple-element.39), channel_id=1, source_target_pairs={{0,256},{256,0},{1,257},{257,1},{2,258},{258,2},{3,259},{259,3},{4... | collective-permute-start | bytes 1769480 | tf_op jit(solution)/shard_map/ppermute | solution.py:46
  39.7 6.8 %all-to-all-start.2 = ((bf16[8,32,896]{2,1,0:T(8,128)(2,1)}), bf16[8,32,896]{2,1,0:T(8,128)(2,1)S(1)}, u32[]{:S(2)}, u32[]{:S(2)}) async-start(bf16[8,32,896]{2,1,0:T(8,128)(2,1)} %bitcast.7), calls=%async_computation.2 | async-start | bytes 917504 | tf_op jit(solution)/shard_map/all_to_all | solution.py:42
  46.6 6.7 %collective-permute-done = bf16[8,16,2304]{2,1,0:T(8,128)(2,1)S(1)} collective-permute-done((bf16[8,16,2304]{2,1,0:T(8,128)(2,1)}, bf16[8,16,2304]{2,1,0:T(8,128)(2,1)S(1)}, u32[]{:S(2)}, u32[]{:S(2)}) %collective-permute-start) | collective-permute-done | bytes 589856 | tf_op jit(solution)/shard_map/ppermute | solution.py:46
  54.2 8.8 %all-to-all-done.2 = bf16[8,32,896]{2,1,0:T(8,128)(2,1)S(1)} async-done(((bf16[8,32,896]{2,1,0:T(8,128)(2,1)}), bf16[8,32,896]{2,1,0:T(8,128)(2,1)S(1)}, u32[]{:S(2)}, u32[]{:S(2)}) %all-to-all-start.2) | async-done | bytes 458784 | tf_op jit(solution)/shard_map/all_to_all | solution.py:42
  63.1 3.5 %all-to-all-start.3 = ((bf16[8,16,2304]{2,1,0:T(8,128)(2,1)}), bf16[8,16,2304]{2,1,0:T(8,128)(2,1)S(1)}, u32[]{:S(2)}, u32[]{:S(2)}) async-start(bf16[8,16,2304]{2,1,0:T(8,128)(2,1)} %add_convert_fusion), calls=%async_computation.3 | async-start | bytes 1179648 | tf_op jit(solution)/shard_map/all_to_all | solution.py:492
  69.1 2.8 %collective-permute-done.1 = bf16[1,16,896]{2,1,0:T(8,128)(2,1)S(1)} collective-permute-done((bf16[1,16,896]{2,1,0:T(8,128)(2,1)S(1)}, bf16[1,16,896]{2,1,0:T(8,128)(2,1)S(1)}, u32[]{:S(2)}, u32[]{:S(2)}) %collective-permute-start.1) | collective-permute-done | bytes 28704 | tf_op jit(solution)/shard_map/ppermute | solution.py:46
  71.8 14.1 %all-to-all-done.3.left_parts = bf16[8,16,2304]{2,1,0:T(8,128)(2,1)S(1)} async-done(((bf16[8,16,2304]{2,1,0:T(8,128)(2,1)}), bf16[8,16,2304]{2,1,0:T(8,128)(2,1)S(1)}, u32[]{:S(2)}, u32[]{:S(2)}) %all-to-all-start.3) | async-done | bytes 589856 | tf_op jit(solution)/shard_map/all_to_all | solution.py:492
  87.0 3.5 %all-to-all-start.4 = ((bf16[8,16,2304]{2,1,0:T(8,128)(2,1)}), bf16[8,16,2304]{2,1,0:T(8,128)(2,1)S(1)}, u32[]{:S(2)}, u32[]{:S(2)}) async-start(bf16[8,16,2304]{2,1,0:T(8,128)(2,1)} %get-tuple-element.45), calls=%async_computation.4 | async-start | bytes 1179648 | tf_op jit(solution)/shard_map/all_to_all | solution.py:504
  97.8 3.1 %collective-permute-start.6 = (f32[16,384]{1,0:T(8,128)S(1)}, f32[16,384]{1,0:T(8,128)S(1)}, u32[]{:S(2)}, u32[]{:S(2)}) collective-permute-start(f32[16,384]{1,0:T(8,128)S(1)} %add.48), channel_id=1, source_target_pairs={{0,6},{2,4},{4,2},{6,0},{1,7},{3,5},{5,3},{7,1},{8,14},{10,12},{12... | collective-permute-start | bytes 73736 | tf_op jit(solution)/shard_map/ppermute | solution.py:63
  103.4 3.4 %collective-permute-start.4 = (f32[16,384]{1,0:T(8,128)S(1)}, f32[16,384]{1,0:T(8,128)S(1)}, u32[]{:S(2)}, u32[]{:S(2)}) collective-permute-start(f32[16,384]{1,0:T(8,128)S(1)} %add.48), channel_id=1, source_target_pairs={{0,2},{2,0},{4,6},{6,4},{1,3},{3,1},{5,7},{7,5},{8,10},{10,8},{12,... | collective-permute-start | bytes 73736 | tf_op jit(solution)/shard_map/ppermute | solution.py:63
  108.3 4.0 %collective-permute-start.9 = (f32[16,384]{1,0:T(8,128)S(1)}, f32[16,384]{1,0:T(8,128)S(1)}, u32[]{:S(2)}, u32[]{:S(2)}) collective-permute-start(f32[16,384]{1,0:T(8,128)S(1)} %add_add_fusion), channel_id=1, source_target_pairs={{0,24},{8,16},{16,8},{24,0},{1,25},{9,17},{17,9},{25,1},{2,26},{10... | collective-permute-start | bytes 73736 | tf_op jit(solution)/shard_map/ppermute | solution.py:63
  112.3 3.6 %collective-permute-start.8 = (f32[16,384]{1,0:T(8,128)S(1)}, f32[16,384]{1,0:T(8,128)S(1)}, u32[]{:S(2)}, u32[]{:S(2)}) collective-permute-start(f32[16,384]{1,0:T(8,128)S(1)} %add_add_fusion), channel_id=1, source_target_pairs={{0,16},{8,24},{16,0},{24,8},{1,17},{9,25},{17,1},{25,9},{2,18},{10... | collective-permute-start | bytes 73736 | tf_op jit(solution)/shard_map/ppermute | solution.py:63
  115.9 3.8 %collective-permute-start.7 = (f32[16,384]{1,0:T(8,128)S(1)}, f32[16,384]{1,0:T(8,128)S(1)}, u32[]{:S(2)}, u32[]{:S(2)}) collective-permute-start(f32[16,384]{1,0:T(8,128)S(1)} %add_add_fusion), channel_id=1, source_target_pairs={{0,8},{8,0},{16,24},{24,16},{1,9},{9,1},{17,25},{25,17},{2,10},{10... | collective-permute-start | bytes 73736 | tf_op jit(solution)/shard_map/ppermute | solution.py:63
  121.6 3.6 %collective-permute-start.10 = (bf16[8,16,2304]{2,1,0:T(8,128)(2,1)S(1)}, bf16[8,16,2304]{2,1,0:T(8,128)(2,1)}, u32[]{:S(2)}, u32[]{:S(2)}) collective-permute-start(bf16[8,16,2304]{2,1,0:T(8,128)(2,1)S(1)} %all-to-all-done.4), channel_id=1, source_target_pairs={{0,256},{256,0},{1,257},{257,1},{2,258},{258,2},{3,259},{259,3},{4... | collective-permute-start | bytes 1769480 | tf_op jit(solution)/shard_map/ppermute | solution.py:46
  127.9 6.4 %all-to-all-start.5 = ((bf16[8,32,896]{2,1,0:T(8,128)(2,1)}), bf16[8,32,896]{2,1,0:T(8,128)(2,1)S(1)}, u32[]{:S(2)}, u32[]{:S(2)}) async-start(bf16[8,32,896]{2,1,0:T(8,128)(2,1)} %broadcast_in_dim.20), calls=%async_computation.5 | async-start | bytes 917504 | tf_op jit(solution)/shard_map/all_to_all | solution.py:36
  137.2 8.4 %all-to-all-done.5 = bf16[8,32,896]{2,1,0:T(8,128)(2,1)S(1)} async-done(((bf16[8,32,896]{2,1,0:T(8,128)(2,1)}), bf16[8,32,896]{2,1,0:T(8,128)(2,1)S(1)}, u32[]{:S(2)}, u32[]{:S(2)}) %all-to-all-start.5) | async-done | bytes 458784 | tf_op jit(solution)/shard_map/all_to_all | solution.py:36
  156.3 6.5 %shard_map.236 = (bf16[256,1024]{1,0:T(8,128)(2,1)S(1)}, f32[64,896]{1,0:T(8,128)}, f32[64,896]{1,0:T(8,128)}, f32[64,896]{1,0:T(8,128)}) custom-call(bf16[256,2304]{1,0:T(8,128)(2,1)S(1)} %bitcast.44, bf16[256,896]{1,0:T(8,128)(2,1)S(1)} %bitcast.47, bf16[512,896]{1,0:T(8,128)(2,1)S(1)} %copy-done.3, bf16[512,896]{1,0:T(8,128)(2,1)S(1)} %copy-done, ...), custom_call_target="tpu_custom_call" | custom-call | flops 1379926016 | bytes 3670016 | tf_op jit(solution)/shard_map/pallas_call | solution.py:262
  164.8 10.4 %all_to_all.41 = bf16[2,128,1024]{2,1,0:T(8,128)(2,1)S(1)} all-to-all(bf16[2,128,1024]{2,1,0:T(8,128)(2,1)S(1)} %bitcast.46), channel_id=1, replica_groups=mesh['zl'=2,'y'=8,'zh'=4,'x'=4,'core'=2] {'core'}, dimensions={0} | all-to-all | bytes 1048576 | tf_op jit(solution)/shard_map/all_to_all | solution.py:42
  176.1 4.7 %collective-permute-start.14 = (bf16[128,384]{1,0:T(8,128)(2,1)S(1)}, bf16[128,384]{1,0:T(8,128)(2,1)S(1)}, u32[]{:S(2)}, u32[]{:S(2)}) collective-permute-start(bf16[128,384]{1,0:T(8,128)(2,1)S(1)} %pad_maximum_fusion.2), channel_id=1, source_target_pairs={{0,128},{32,160},{64,192},{96,224},{128,0},{160,32},{192,64},{224,... | collective-permute-start | bytes 294920 | tf_op jit(solution)/shard_map/ppermute | solution.py:63
  180.8 6.6 %all-to-all-start.7 = ((bf16[16,8,1024]{2,1,0:T(8,128)(2,1)}), bf16[16,8,1024]{2,1,0:T(8,128)(2,1)S(1)}, u32[]{:S(2)}, u32[]{:S(2)}) async-start(bf16[16,8,1024]{2,1,0:T(8,128)(2,1)} %bitcast.24), calls=%async_computation.7 | async-start | bytes 524288 | tf_op jit(solution)/shard_map/all_to_all | solution.py:519
  189.8 7.8 %all-to-all-done.7.parts = bf16[16,8,1024]{2,1,0:T(8,128)(2,1)S(1)} async-done(((bf16[16,8,1024]{2,1,0:T(8,128)(2,1)}), bf16[16,8,1024]{2,1,0:T(8,128)(2,1)S(1)}, u32[]{:S(2)}, u32[]{:S(2)}) %all-to-all-start.7) | async-done | bytes 262176 | tf_op jit(solution)/shard_map/all_to_all | solution.py:519
  (113 shorter events, 44.5 us)
Async XLA Ops:
  2.1 31.2 %copy-start.27 = (f32[512]{0:T(512)S(1)}, f32[512]{0:T(512)}, u32[]{:S(2)}) copy-start(f32[512]{0:T(512)} %param.19) | copy-start | bytes 6148
  2.1 23.6 %all-to-all-start = ((bf16[16,8,1024]{2,1,0:T(8,128)(2,1)}), bf16[16,8,1024]{2,1,0:T(8,128)(2,1)S(1)}, u32[]{:S(2)}, u32[]{:S(2)}) async-start(bf16[16,8,1024]{2,1,0:T(8,128)(2,1)} %broadcast_in_dim.17), calls=%async_computation | async-start | bytes 524288 | tf_op jit(solution)/shard_map/all_to_all | solution.py:36
  36.6 16.6 %collective-permute-start = (bf16[8,16,2304]{2,1,0:T(8,128)(2,1)}, bf16[8,16,2304]{2,1,0:T(8,128)(2,1)S(1)}, u32[]{:S(2)}, u32[]{:S(2)}) collective-permute-start(bf16[8,16,2304]{2,1,0:T(8,128)(2,1)} %get-tuple-element.39), channel_id=1, source_target_pairs={{0,256},{256,0},{1,257},{257,1},{2,258},{258,2},{3,259},{259,3},{4... | collective-permute-start | bytes 1769480 | tf_op jit(solution)/shard_map/ppermute | solution.py:46
  39.7 23.3 %all-to-all-start.2 = ((bf16[8,32,896]{2,1,0:T(8,128)(2,1)}), bf16[8,32,896]{2,1,0:T(8,128)(2,1)S(1)}, u32[]{:S(2)}, u32[]{:S(2)}) async-start(bf16[8,32,896]{2,1,0:T(8,128)(2,1)} %bitcast.7), calls=%async_computation.2 | async-start | bytes 917504 | tf_op jit(solution)/shard_map/all_to_all | solution.py:42
  63.1 22.8 %all-to-all-start.3 = ((bf16[8,16,2304]{2,1,0:T(8,128)(2,1)}), bf16[8,16,2304]{2,1,0:T(8,128)(2,1)S(1)}, u32[]{:S(2)}, u32[]{:S(2)}) async-start(bf16[8,16,2304]{2,1,0:T(8,128)(2,1)} %add_convert_fusion), calls=%async_computation.3 | async-start | bytes 1179648 | tf_op jit(solution)/shard_map/all_to_all | solution.py:492
  66.7 26.9 %copy-start.13 = (bf16[64,896]{1,0:T(8,128)(2,1)S(1)}, bf16[64,896]{1,0:T(8,128)(2,1)}, u32[]{:S(2)}) copy-start(bf16[64,896]{1,0:T(8,128)(2,1)} %factors_hbm_0.1) | copy-start | bytes 344068
  66.7 26.9 %copy-start.15 = (bf16[64,896]{1,0:T(8,128)(2,1)S(1)}, bf16[64,896]{1,0:T(8,128)(2,1)}, u32[]{:S(2)}) copy-start(bf16[64,896]{1,0:T(8,128)(2,1)} %factors_hbm_1.1) | copy-start | bytes 344068
  66.8 5.0 %collective-permute-start.1 = (bf16[1,16,896]{2,1,0:T(8,128)(2,1)S(1)}, bf16[1,16,896]{2,1,0:T(8,128)(2,1)S(1)}, u32[]{:S(2)}, u32[]{:S(2)}) collective-permute-start(bf16[1,16,896]{2,1,0:T(8,128)(2,1)S(1)} %dynamic-slice_bitcast_fusion), channel_id=1, source_target_pairs={{0,256},{256,0},{1,257},{257,1},{2,258},{258,2},{3,259},{259,3},{4... | collective-permute-start | bytes 86024 | tf_op jit(solution)/shard_map/ppermute | solution.py:46
  87.0 34.6 %all-to-all-start.4 = ((bf16[8,16,2304]{2,1,0:T(8,128)(2,1)}), bf16[8,16,2304]{2,1,0:T(8,128)(2,1)S(1)}, u32[]{:S(2)}, u32[]{:S(2)}) async-start(bf16[8,16,2304]{2,1,0:T(8,128)(2,1)} %get-tuple-element.45), calls=%async_computation.4 | async-start | bytes 1179648 | tf_op jit(solution)/shard_map/all_to_all | solution.py:504
  91.4 15.4 %collective-permute-start.2 = (bf16[1,16,896]{2,1,0:T(8,128)(2,1)S(1)}, bf16[1,16,896]{2,1,0:T(8,128)(2,1)S(1)}, u32[]{:S(2)}, u32[]{:S(2)}) collective-permute-start(bf16[1,16,896]{2,1,0:T(8,128)(2,1)S(1)} %bitcast.60), channel_id=1, source_target_pairs={{0,256},{256,0},{1,257},{257,1},{2,258},{258,2},{3,259},{259,3},{4... | collective-permute-start | bytes 86024 | tf_op jit(solution)/shard_map/ppermute | solution.py:46
  94.3 3.5 %collective-permute-start.3 = (f32[16,384]{1,0:T(8,128)S(1)}, f32[16,384]{1,0:T(8,128)S(1)}, u32[]{:S(2)}, u32[]{:S(2)}) collective-permute-start(f32[16,384]{1,0:T(8,128)S(1)} %shard_map.235), channel_id=1, source_target_pairs={{0,1},{1,0},{2,3},{3,2},{4,5},{5,4},{6,7},{7,6},{8,9},{9,8},{10,11... | collective-permute-start | bytes 73736 | tf_op jit(solution)/shard_map/ppermute | solution.py:63
  97.8 9.0 %collective-permute-start.6 = (f32[16,384]{1,0:T(8,128)S(1)}, f32[16,384]{1,0:T(8,128)S(1)}, u32[]{:S(2)}, u32[]{:S(2)}) collective-permute-start(f32[16,384]{1,0:T(8,128)S(1)} %add.48), channel_id=1, source_target_pairs={{0,6},{2,4},{4,2},{6,0},{1,7},{3,5},{5,3},{7,1},{8,14},{10,12},{12... | collective-permute-start | bytes 73736 | tf_op jit(solution)/shard_map/ppermute | solution.py:63
  100.9 6.4 %collective-permute-start.5 = (f32[16,384]{1,0:T(8,128)S(1)}, f32[16,384]{1,0:T(8,128)S(1)}, u32[]{:S(2)}, u32[]{:S(2)}) collective-permute-start(f32[16,384]{1,0:T(8,128)S(1)} %add.48), channel_id=1, source_target_pairs={{0,4},{2,6},{4,0},{6,2},{1,5},{3,7},{5,1},{7,3},{8,12},{10,14},{12... | collective-permute-start | bytes 73736 | tf_op jit(solution)/shard_map/ppermute | solution.py:63
  103.4 4.9 %collective-permute-start.4 = (f32[16,384]{1,0:T(8,128)S(1)}, f32[16,384]{1,0:T(8,128)S(1)}, u32[]{:S(2)}, u32[]{:S(2)}) collective-permute-start(f32[16,384]{1,0:T(8,128)S(1)} %add.48), channel_id=1, source_target_pairs={{0,2},{2,0},{4,6},{6,4},{1,3},{3,1},{5,7},{7,5},{8,10},{10,8},{12,... | collective-permute-start | bytes 73736 | tf_op jit(solution)/shard_map/ppermute | solution.py:63
  108.3 11.4 %collective-permute-start.9 = (f32[16,384]{1,0:T(8,128)S(1)}, f32[16,384]{1,0:T(8,128)S(1)}, u32[]{:S(2)}, u32[]{:S(2)}) collective-permute-start(f32[16,384]{1,0:T(8,128)S(1)} %add_add_fusion), channel_id=1, source_target_pairs={{0,24},{8,16},{16,8},{24,0},{1,25},{9,17},{17,9},{25,1},{2,26},{10... | collective-permute-start | bytes 73736 | tf_op jit(solution)/shard_map/ppermute | solution.py:63
  112.3 8.5 %collective-permute-start.8 = (f32[16,384]{1,0:T(8,128)S(1)}, f32[16,384]{1,0:T(8,128)S(1)}, u32[]{:S(2)}, u32[]{:S(2)}) collective-permute-start(f32[16,384]{1,0:T(8,128)S(1)} %add_add_fusion), channel_id=1, source_target_pairs={{0,16},{8,24},{16,0},{24,8},{1,17},{9,25},{17,1},{25,9},{2,18},{10... | collective-permute-start | bytes 73736 | tf_op jit(solution)/shard_map/ppermute | solution.py:63
  115.9 5.6 %collective-permute-start.7 = (f32[16,384]{1,0:T(8,128)S(1)}, f32[16,384]{1,0:T(8,128)S(1)}, u32[]{:S(2)}, u32[]{:S(2)}) collective-permute-start(f32[16,384]{1,0:T(8,128)S(1)} %add_add_fusion), channel_id=1, source_target_pairs={{0,8},{8,0},{16,24},{24,16},{1,9},{9,1},{17,25},{25,17},{2,10},{10... | collective-permute-start | bytes 73736 | tf_op jit(solution)/shard_map/ppermute | solution.py:63
  121.6 14.3 %collective-permute-start.10 = (bf16[8,16,2304]{2,1,0:T(8,128)(2,1)S(1)}, bf16[8,16,2304]{2,1,0:T(8,128)(2,1)}, u32[]{:S(2)}, u32[]{:S(2)}) collective-permute-start(bf16[8,16,2304]{2,1,0:T(8,128)(2,1)S(1)} %all-to-all-done.4), channel_id=1, source_target_pairs={{0,256},{256,0},{1,257},{257,1},{2,258},{258,2},{3,259},{259,3},{4... | collective-permute-start | bytes 1769480 | tf_op jit(solution)/shard_map/ppermute | solution.py:46
  125.2 10.6 %collective-permute-start.11 = (bf16[16,384]{1,0:T(8,128)(2,1)S(1)}, bf16[16,384]{1,0:T(8,128)(2,1)S(1)}, u32[]{:S(2)}, u32[]{:S(2)}) collective-permute-start(bf16[16,384]{1,0:T(8,128)(2,1)S(1)} %multiply_convert_fusion.1), channel_id=1, source_target_pairs={{0,256},{256,0},{1,257},{257,1},{2,258},{258,2},{3,259},{259,3},{4... | collective-permute-start | bytes 36872 | tf_op jit(solution)/shard_map/ppermute | solution.py:63
  127.9 17.7 %all-to-all-start.5 = ((bf16[8,32,896]{2,1,0:T(8,128)(2,1)}), bf16[8,32,896]{2,1,0:T(8,128)(2,1)S(1)}, u32[]{:S(2)}, u32[]{:S(2)}) async-start(bf16[8,32,896]{2,1,0:T(8,128)(2,1)} %broadcast_in_dim.20), calls=%async_computation.5 | async-start | bytes 917504 | tf_op jit(solution)/shard_map/all_to_all | solution.py:36
  146.4 16.4 %collective-permute-start.12 = (bf16[32,384]{1,0:T(8,128)(2,1)S(1)}, bf16[32,384]{1,0:T(8,128)(2,1)S(1)}, u32[]{:S(2)}, u32[]{:S(2)}) collective-permute-start(bf16[32,384]{1,0:T(8,128)(2,1)S(1)} %pad_maximum_fusion.5), channel_id=1, source_target_pairs={{0,32},{32,0},{64,96},{96,64},{128,160},{160,128},{192,224},{224,1... | collective-permute-start | bytes 73736 | tf_op jit(solution)/shard_map/ppermute | solution.py:63
  162.9 13.2 %collective-permute-start.13 = (bf16[64,384]{1,0:T(8,128)(2,1)S(1)}, bf16[64,384]{1,0:T(8,128)(2,1)S(1)}, u32[]{:S(2)}, u32[]{:S(2)}) collective-permute-start(bf16[64,384]{1,0:T(8,128)(2,1)S(1)} %pad_maximum_fusion.4), channel_id=1, source_target_pairs={{0,64},{32,96},{64,0},{96,32},{128,192},{160,224},{192,128},{224,1... | collective-permute-start | bytes 147464 | tf_op jit(solution)/shard_map/ppermute | solution.py:63
  176.1 12.5 %collective-permute-start.14 = (bf16[128,384]{1,0:T(8,128)(2,1)S(1)}, bf16[128,384]{1,0:T(8,128)(2,1)S(1)}, u32[]{:S(2)}, u32[]{:S(2)}) collective-permute-start(bf16[128,384]{1,0:T(8,128)(2,1)S(1)} %pad_maximum_fusion.2), channel_id=1, source_target_pairs={{0,128},{32,160},{64,192},{96,224},{128,0},{160,32},{192,64},{224,... | collective-permute-start | bytes 294920 | tf_op jit(solution)/shard_map/ppermute | solution.py:63
  180.8 16.8 %all-to-all-start.7 = ((bf16[16,8,1024]{2,1,0:T(8,128)(2,1)}), bf16[16,8,1024]{2,1,0:T(8,128)(2,1)S(1)}, u32[]{:S(2)}, u32[]{:S(2)}) async-start(bf16[16,8,1024]{2,1,0:T(8,128)(2,1)} %bitcast.24), calls=%async_computation.7 | async-start | bytes 524288 | tf_op jit(solution)/shard_map/all_to_all | solution.py:519
  (25 other events, 172.9 us)

commit v5 on v4

v5 whole, which is shorter than its diff:
```python
import functools

import jax
import jax.numpy as jnp
from jax import lax
from jax.experimental import pallas as pl
from jax.experimental.pallas import tpu as pltpu
from jax.sharding import Mesh
from jax.sharding import PartitionSpec as P

D = 8192
ROW = ("zl", "y")
CHIPS = ("zh", "x")
COL = ("zh", "x", "core")
SCALE = 0.5
EPSILON = 1e-05
BF = jnp.bfloat16
F32 = jnp.float32


def nn(left, right):
    return lax.dot_general(left, right, (((1,), (0,)), ((), ())), preferred_element_type=F32)


def nt(left, right):
    return lax.dot_general(left, right, (((1,), (1,)), ((), ())), preferred_element_type=F32)


def tn(left, right):
    return lax.dot_general(left, right, (((0,), (0,)), ((), ())), preferred_element_type=F32)


def spread(array, axis):
    peers = lax.axis_size(axis)
    copies = jnp.broadcast_to(array, (peers, *array.shape))
    return lax.all_to_all(copies, axis, 0, 0, tiled=True).reshape(-1, *array.shape[1:])


def reduced(array, axis):
    peers = lax.axis_size(axis)
    tiles = array.reshape(peers, array.shape[0] // peers, *array.shape[1:])
    return jnp.sum(lax.all_to_all(tiles, axis, 0, 0, tiled=True).astype(F32), axis=0)


def swapped(array):
    return lax.ppermute(array, "zl", [(0, 1), (1, 0)])


def pair_sum(array):
    index = lax.axis_index("zl")
    kept = lax.dynamic_index_in_dim(array, index, 1, keepdims=False)
    sent = lax.dynamic_index_in_dim(array, 1 - index, 1, keepdims=False)
    return kept.astype(F32) + swapped(sent).astype(F32)


def pair_join(array):
    other = swapped(array)
    first = lax.axis_index("zl") == 0
    return jnp.stack([jnp.where(first, array, other), jnp.where(first, other, array)], axis=1)


LANES = 128
CHUNK = 32


def second_order(gate_pre, up_pre, adj, gate_tan, up_tan, adj_tan):
    sig = 1.0 / (1.0 + jnp.exp(-gate_pre))
    rest = 1.0 - sig
    act = gate_pre * sig
    slope = sig * (1.0 + gate_pre * rest)
    bend = sig * rest * (2.0 + gate_pre * (1.0 - 2.0 * sig))
    slope_tan = slope * gate_tan
    up_slope = up_pre * slope
    return (
        (act * up_pre).astype(BF),
        (slope_tan * up_pre + act * up_tan).astype(BF),
        (adj * up_slope).astype(BF),
        (adj * act).astype(BF),
        (adj_tan * up_slope + adj * (up_tan * slope + up_pre * bend * gate_tan)).astype(BF),
        (adj_tan * act + adj * slope_tan).astype(BF),
    )


def adapter_terms(pair, plain, direction):
    rank = plain.shape[0]
    term = SCALE * nn(pair[:, :rank], plain)
    return term, SCALE * nn(pair, jnp.concatenate([direction, plain], axis=0))


def back_kernel(
    full,
    up_full,
    weights,
    factors,
    in_factors,
    payload,
    curv_gate,
    curv_up,
    curv_down,
    terms,
    d_gate,
    d_up,
    d_gate_dir,
    d_up_dir,
    hidden,
    hidden_dir,
):
    tokens = full.shape[0]
    rows, cols = weights.shape[1:]
    rank = factors.shape[1]
    at = 2 * cols
    pairs = [full[:, at + 2 * k * rank : at + 2 * (k + 1) * rank] for k in range(3)]

    def column_block(block, carry):
        here = pl.ds(pl.multiple_of(block * LANES, LANES), LANES)
        at_adj = pl.ds(pl.multiple_of(cols + block * LANES, LANES), LANES)
        for k in range(3):
            term, tan = adapter_terms(pairs[k], factors[2 * k, :, here], factors[2 * k + 1, :, here])
            terms[2 * k] = term
            terms[2 * k + 1] = tan
        for chunk in range(tokens // CHUNK):
            r = pl.ds(chunk * CHUNK, CHUNK)
            (
                hidden[r, here],
                hidden_dir[r, here],
                d_gate[r, here],
                d_up[r, here],
                d_gate_dir[r, here],
                d_up_dir[r, here],
            ) = second_order(
                full[r, here].astype(F32) + terms[0, r, :],
                up_full[r, here].astype(F32) + terms[2, r, :],
                full[r, at_adj].astype(F32) + terms[4, r, :],
                terms[1, r, :],
                terms[3, r, :],
                terms[5, r, :],
            )
        return carry

    lax.fori_loop(0, cols // LANES, column_block, 0)
    dg, du, dgd, dud = d_gate[...], d_up[...], d_gate_dir[...], d_up_dir[...]
    h, hd = hidden[...], hidden_dir[...]
    gw, uw = weights[0], weights[1]
    go, god, uo, uod, di, did = [factors[k] for k in range(6)]
    q_gate, q_up = nt(dg, go), nt(du, uo)
    q_gate_dir = nt(dgd, go) + nt(dg, god)
    q_up_dir = nt(dud, uo) + nt(du, uod)
    q_all = jnp.concatenate([q_gate_dir, q_up_dir, nt(hd, di) + nt(h, did)], axis=1) * SCALE
    gi, ui, gid, uid = [in_factors[k] for k in range(4)]
    qg, qu = (SCALE * q_gate).astype(BF), (SCALE * q_up).astype(BF)
    qgd, qud = (SCALE * q_gate_dir).astype(BF), (SCALE * q_up_dir).astype(BF)
    first = nt(dg, gw) + nt(du, uw) + nn(qg, gi) + nn(qu, ui)
    second = nt(dgd, gw) + nt(dud, uw) + nn(qgd, gi) + nn(qg, gid) + nn(qud, ui) + nn(qu, uid)
    half = tokens // 2
    for k in range(2):
        payload[k, :, :rows] = first[k * half : (k + 1) * half].astype(BF)
        payload[k, :, rows : 2 * rows] = second[k * half : (k + 1) * half].astype(BF)
    groups = q_all.reshape(tokens // 32, 4, 8, q_all.shape[1])
    groups = [groups[:, g].reshape(tokens // 4, q_all.shape[1]) for g in range(4)]
    for g in range(2):
        block = jnp.concatenate(groups[2 * g : 2 * g + 2], axis=1).astype(BF)
        for k in range(2):
            payload[k, g * tokens // 4 : (g + 1) * tokens // 4, 2 * rows :] = block
    low, low_dir = pairs[0][:, :rank], pairs[0][:, rank:]
    curv_gate[...] = SCALE * (tn(low_dir, dg) + tn(low, dgd))
    low, low_dir = pairs[1][:, :rank], pairs[1][:, rank:]
    curv_up[...] = SCALE * (tn(low_dir, du) + tn(low, dud))
    low, low_dir = pairs[2][:, :rank], pairs[2][:, rank:]
    curv_down[...] = SCALE * (tn(low, hd) + tn(low_dir, h))


def backward(full, up_full, weights, factors, in_factors):
    tokens = full.shape[0]
    rows, cols = weights.shape[1:]
    rank = factors.shape[1]
    whole = pl.BlockSpec(memory_space=pltpu.VMEM)
    curvature = jax.ShapeDtypeStruct((rank, cols), F32)
    panel = pltpu.VMEM((tokens, cols), BF)
    return pl.pallas_call(
        back_kernel,
        out_shape=(
            jax.ShapeDtypeStruct((2, tokens // 2, 2 * rows + 6 * rank), BF),
            curvature,
            curvature,
            curvature,
        ),
        in_specs=[whole] * 5,
        out_specs=[whole] * 4,
        scratch_shapes=[pltpu.VMEM((6, tokens, LANES), F32)] + [panel] * 6,
        compiler_params=pltpu.CompilerParams(vmem_limit_bytes=16 * 1024 * 1024),
        cost_estimate=pl.CostEstimate(
            flops=2 * tokens * cols * (4 * rows + 15 * rank),
            bytes_accessed=2 * cols * (2 * rows + 4 * tokens),
            transcendentals=tokens * cols,
        ),
    )(full, up_full, weights, factors, in_factors)


def spread_kernel(flag, scaled, panel, gate_w, down_w, gi, gid, ui, uid, db, dbd, kept, sent):
    rows, cols = gate_w.shape
    peers, own_rows = kept.shape[:2]
    tokens_f = panel[:, :rows].astype(F32)
    squares = jnp.sum(tokens_f * tokens_f, axis=1, keepdims=True)
    high = squares.astype(BF).astype(F32)
    lane = lax.broadcasted_iota(jnp.int32, (tokens_f.shape[0], LANES), 1)
    first = flag[0] == 0

    def put(value, at):
        value = value.astype(F32).reshape(peers, 2, own_rows, value.shape[1])
        here = slice(at, at + value.shape[3])
        zero, one = value[:, 0], value[:, 1]
        kept[:, :, here] = jnp.where(first, zero, one).astype(BF)
        sent[:, :, here] = jnp.where(first, one, zero).astype(BF)

    x, cot = scaled[...], panel[:, rows:]
    put(nn(x, gate_w[...]), 0)
    put(nt(cot, down_w[...]), cols)
    at = 2 * cols
    for left, factors in ((x, (gi, gid)), (x, (ui, uid)), (cot, (db, dbd))):
        both = jnp.concatenate([factors[0][...], factors[1][...]], axis=0)
        put(nt(left, both), at)
        at += both.shape[0]
    put(jnp.where(lane == 0, high, jnp.where(lane == 1, squares - high, 0.0)), at)


def forward(flag, scaled, panel, gate_w, down_w, peers, *factors):
    tokens = scaled.shape[0]
    rows, cols = gate_w.shape
    rank = factors[0].shape[0]
    whole = pl.BlockSpec(memory_space=pltpu.VMEM)
    half = jax.ShapeDtypeStruct(
        (peers, tokens // (2 * peers), 2 * cols + 6 * rank + LANES), BF
    )
    return pl.pallas_call(
        spread_kernel,
        out_shape=(half, half),
        in_specs=[pl.BlockSpec(memory_space=pltpu.SMEM)] + [whole] * (4 + len(factors)),
        out_specs=[whole] * 2,
        compiler_params=pltpu.CompilerParams(vmem_limit_bytes=20 * 1024 * 1024),
        cost_estimate=pl.CostEstimate(
            flops=4 * tokens * rows * (cols + 3 * rank),
            bytes_accessed=4 * rows * cols,
            transcendentals=0,
        ),
    )(flag, scaled, panel, gate_w, down_w, *factors)


def own_kernel(normed_ranks, left_parts, right_sum, copies, right_own):
    cols = right_sum.shape[1]
    total = left_parts[0].astype(F32)
    for k in range(1, left_parts.shape[0]):
        total += left_parts[k].astype(F32)
    at = total.shape[1] - LANES
    squares = total[:, at : at + 1] + total[:, at + 1 : at + 2]
    inv_rms = lax.rsqrt(squares / D + EPSILON)
    high = inv_rms.astype(BF).astype(F32)
    lane = lax.broadcasted_iota(jnp.int32, (total.shape[0], LANES), 1)
    scale = jnp.where(lane == 0, high, jnp.where(lane == 1, inv_rms - high, 0.0))
    low = 2 * cols
    own = jnp.concatenate(
        [
            total[:, :cols] * inv_rms,
            total[:, cols:low],
            total[:, low : low + normed_ranks] * inv_rms,
            total[:, low + normed_ranks : at],
            scale,
        ],
        axis=1,
    ).astype(BF)
    for k in range(copies.shape[0]):
        copies[k] = own
    right_own[...] = (right_sum[...] * inv_rms).astype(BF)


def own_rows_scaled(left_parts, right_sum, normed_ranks):
    whole = pl.BlockSpec(memory_space=pltpu.VMEM)
    return pl.pallas_call(
        functools.partial(own_kernel, normed_ranks),
        out_shape=(
            jax.ShapeDtypeStruct(left_parts.shape, BF),
            jax.ShapeDtypeStruct(right_sum.shape, BF),
        ),
        in_specs=[whole] * 2,
        out_specs=[whole] * 2,
        compiler_params=pltpu.CompilerParams(vmem_limit_bytes=8 * 1024 * 1024),
        cost_estimate=pl.CostEstimate(
            flops=left_parts.size, bytes_accessed=4 * left_parts.size, transcendentals=0
        ),
    )(left_parts, right_sum)


def pack_kernel(place, arrived, out, total):
    width = arrived.shape[2] - 3 * LANES
    total[...] = arrived[0].astype(F32) + arrived[1].astype(F32)
    half = total.shape[0] // 2
    at = pl.multiple_of(place[0] * 8, 8)
    later = pl.multiple_of(place[0] * 8 + half, 8)
    piece = jnp.concatenate(
        [total[pl.ds(at, 8), width:], total[pl.ds(later, 8), width:]], axis=1
    ).astype(BF)
    for k in range(out.shape[0]):
        out[k, :, :width] = total[8 * k : 8 * k + 8, :width].astype(BF)
        out[k, :, width:] = piece


def pack(place, arrived):
    rows, width = arrived.shape[1:]
    return pl.pallas_call(
        pack_kernel,
        out_shape=jax.ShapeDtypeStruct((rows // 8, 8, width + 3 * LANES), BF),
        in_specs=[
            pl.BlockSpec(memory_space=pltpu.SMEM),
            pl.BlockSpec(memory_space=pltpu.VMEM),
        ],
        out_specs=pl.BlockSpec(memory_space=pltpu.VMEM),
        scratch_shapes=[pltpu.VMEM((rows, width), F32)],
        compiler_params=pltpu.CompilerParams(vmem_limit_bytes=8 * 1024 * 1024),
        cost_estimate=pl.CostEstimate(
            flops=rows * width, bytes_accessed=6 * rows * width, transcendentals=0
        ),
    )(place, arrived)


def tail_kernel(parts, adjoint, adjoint_dir, copies):
    rows = adjoint.shape[1]
    total = parts[0].astype(F32)
    for k in range(1, parts.shape[0]):
        total += parts[k].astype(F32)
    adjoint[...] = total[:, :rows]
    adjoint_dir[...] = total[:, rows : 2 * rows]
    q = total[:, 2 * rows :].astype(BF)
    for k in range(copies.shape[0]):
        copies[k] = q


def tail(parts, rows, peers):
    tokens, width = parts.shape[1:]
    whole = pl.BlockSpec(memory_space=pltpu.VMEM)
    out = jax.ShapeDtypeStruct((tokens, rows), F32)
    return pl.pallas_call(
        tail_kernel,
        out_shape=(out, out, jax.ShapeDtypeStruct((peers, tokens, width - 2 * rows), BF)),
        in_specs=[whole],
        out_specs=[whole] * 3,
        compiler_params=pltpu.CompilerParams(vmem_limit_bytes=8 * 1024 * 1024),
        cost_estimate=pl.CostEstimate(
            flops=parts.size, bytes_accessed=2 * parts.size, transcendentals=0
        ),
    )(parts)


def curvature_kernel(q_parts, scaled, panel, block, gate, up, down):
    rank, rows = gate.shape
    q = q_parts[...].astype(F32)
    groups = [q[:, :, g * 3 * rank : (g + 1) * 3 * rank] for g in range(4)]
    q = jnp.stack(groups, axis=1).reshape(scaled.shape[0], 3 * rank)
    last = block[:, block.shape[1] - LANES :].astype(F32)
    inv_rms = last[:, :1] + last[:, 1:2]
    x, cot = scaled[...], panel[:, rows:]
    gate[...] = tn((q[:, :rank] * inv_rms).astype(BF), x)
    up[...] = tn((q[:, rank : 2 * rank] * inv_rms).astype(BF), x)
    down[...] = tn(q[:, 2 * rank :].astype(BF), cot)


def curvatures(q_parts, scaled, panel, block, rank):
    tokens, rows = scaled.shape
    whole = pl.BlockSpec(memory_space=pltpu.VMEM)
    out = jax.ShapeDtypeStruct((rank, rows), F32)
    return pl.pallas_call(
        curvature_kernel,
        out_shape=(out, out, out),
        in_specs=[whole] * 4,
        out_specs=[whole] * 3,
        compiler_params=pltpu.CompilerParams(vmem_limit_bytes=8 * 1024 * 1024),
        cost_estimate=pl.CostEstimate(
            flops=6 * tokens * rank * rows,
            bytes_accessed=4 * tokens * rows,
            transcendentals=0,
        ),
    )(q_parts, scaled, panel, block)


def on_device(
    tokens,
    norm_gain,
    cotangent,
    gate_w,
    up_w,
    down_w,
    gate_in,
    gate_out,
    up_in,
    up_out,
    down_in,
    down_b,
    gate_in_dir,
    gate_out_dir,
    up_in_dir,
    up_out_dir,
    down_in_dir,
    down_b_dir,
):
    rank = gate_in.shape[1]
    rows = gate_w.shape[0]
    cols = gate_w.shape[1]
    weights = jnp.stack([gate_w, up_w])
    out_factors = jnp.stack([gate_out, gate_out_dir, up_out, up_out_dir, down_in.T, down_in_dir.T])
    in_factors = jnp.stack([gate_in.T, up_in.T, gate_in_dir.T, up_in_dir.T])
    own = jnp.concatenate([tokens, cotangent], axis=1)
    panel = spread(spread(own, CHIPS), "core")
    scaled = (panel[:, :rows].astype(F32) * norm_gain).astype(BF)
    right = nn(scaled, up_w).astype(BF)
    scaled, right = lax.optimization_barrier((scaled, right))
    peers = lax.axis_size("y")
    own_rows = right.shape[0] // (2 * peers)
    flag = jnp.full((1,), lax.axis_index("zl"), jnp.int32)
    kept, sent = forward(
        flag,
        scaled,
        panel,
        gate_w,
        down_w,
        peers,
        in_factors[0],
        in_factors[2],
        in_factors[1],
        in_factors[3],
        down_b,
        down_b_dir,
    )
    right_half = reduced(right, "y").astype(BF)
    left_half = (kept.astype(F32) + swapped(sent).astype(F32)).astype(BF)
    left_half, right_half = lax.optimization_barrier((left_half, right_half))
    left_parts = lax.all_to_all(left_half, "y", 0, 0, tiled=True)
    right_sum = pair_sum(right_half.reshape(1, 2, own_rows, cols))[0]
    left_parts, right_sum = lax.optimization_barrier((left_parts, right_sum))
    copies, right_own = own_rows_scaled(left_parts, right_sum, 4 * rank)

    right_pair = pair_join(right_own[None]).reshape(2 * own_rows, cols)
    left_line = lax.all_to_all(copies, "y", 0, 0, tiled=True)
    right_pair = jnp.broadcast_to(right_pair, (peers, *right_pair.shape))
    left_line, right_pair, weights, out_factors, in_stack = lax.optimization_barrier(
        (left_line, right_pair, weights, out_factors, in_factors)
    )
    up_full = lax.all_to_all(right_pair, "y", 0, 0, tiled=True).reshape(-1, cols)
    full = pair_join(left_line).reshape(2 * peers * own_rows, -1)
    payload, curv_gate_out, curv_up_out, curv_down_in = backward(
        full, up_full, weights, out_factors, in_stack
    )
    arrived = lax.all_to_all(payload, "core", 0, 0, tiled=True)
    place = jnp.full((1,), lax.axis_index("y"), jnp.int32)
    parts = lax.all_to_all(pack(place, arrived), CHIPS, 0, 0, tiled=True)
    adjoint, adjoint_dir, q_copies = tail(parts, rows, peers)
    q_parts = lax.all_to_all(q_copies, "y", 0, 0, tiled=True)
    curv_gate_in, curv_up_in, curv_down_out = curvatures(q_parts, scaled, panel, full, rank)
    return (
        adjoint,
        adjoint_dir,
        curv_gate_in.T,
        curv_gate_out,
        curv_up_in.T,
        curv_up_out,
        curv_down_in.T,
        curv_down_out,
    )


def solution(mesh):
    split = Mesh(mesh.devices.reshape(2, 8, 4, 4, 2), ("zl", "y", "zh", "x", "core"))
    features = P(ROW, None)
    hidden = P(None, COL)
    return jax.shard_map(
        on_device,
        mesh=split,
        in_specs=(
            P(COL, ROW),
            P(ROW),
            P(COL, ROW),
            P(ROW, COL),
            P(ROW, COL),
            P(COL, ROW),
            features,
            hidden,
            features,
            hidden,
            P(COL, None),
            P(None, ROW),
            features,
            hidden,
            features,
            hidden,
            P(COL, None),
            P(None, ROW),
        ),
        out_specs=(
            P(COL, ROW),
            P(COL, ROW),
            features,
            hidden,
            features,
            hidden,
            P(COL, None),
            P(None, ROW),
        ),
        check_vma=False,
    )
```

time: 201 us -> 179 us (0.89)
  the two profiles are of different devices: /device:TPU:1 before, /device:TPU:4 now
where the time goes in v5:
time: 179 us; the launch traced here: 178 us
  waiting for transfers between devices  67.5 us (38%)
  starting transfers between devices  43.1 us (24%)
  blocking collectives  40.7 us (23%)
  Pallas kernels  10.3 us (6%)
  other arithmetic  8.04 us (4%)
  local copies, waits for them, and re-layouts  6.29 us (4%)
    ppermute x4, waiting for transfers between devices, swapped(): return lax.ppermute(array, 'zl', [(0, 1), (1, 0)])  23.4 us
    all_to_all x1, blocking collectives, on_device(): parts = lax.all_to_all(pack(place, arrived), CHIPS, 0, 0, tiled=True)  21 us
    all_to_all x1, starting transfers between devices, spread(): lax.all_to_all(copies, axis, 0, 0, tiled=True).reshape(-1, *array.shape[1:])  13.4 us
    all_to_all x1, waiting for transfers between devices, on_device(): left_parts = lax.all_to_all(left_half, 'y', 0, 0, tiled=True)  11.6 us
    ppermute x4, starting transfers between devices, swapped(): return lax.ppermute(array, 'zl', [(0, 1), (1, 0)])  11.4 us
    all_to_all x1, waiting for transfers between devices, spread(): lax.all_to_all(copies, axis, 0, 0, tiled=True).reshape(-1, *array.shape[1:])  11.2 us
    all_to_all x1, blocking collectives, on_device(): q_parts = lax.all_to_all(q_copies, 'y', 0, 0, tiled=True)  11.1 us
    all_to_all x1, waiting for transfers between devices, on_device(): left_line = lax.all_to_all(copies, 'y', 0, 0, tiled=True)  10.8 us
  transfers between devices with their start and end apart: 9, of which 9 were waited for; matrix products, arithmetic and copies ran while one was open for 5% of the time, Pallas kernels for 0%

profile of v5, /device:TPU:4, one launch (start us, length us, event | category | flops | bytes accessed | tf_op | source)
XLA Modules:
  0.0 178.0 jit_solution(18029924816868714141)
XLA Ops:
  2.1 13.4 %all-to-all-start = ((bf16[16,8,1024]{2,1,0:T(8,128)(2,1)}), bf16[16,8,1024]{2,1,0:T(8,128)(2,1)S(1)}, u32[]{:S(2)}, u32[]{:S(2)}) async-start(bf16[16,8,1024]{2,1,0:T(8,128)(2,1)} %broadcast_in_dim.21), calls=%async_computation | async-start | bytes 524288 | tf_op jit(solution)/shard_map/all_to_all | solution.py:36
  15.5 11.2 %all-to-all-done = bf16[16,8,1024]{2,1,0:T(8,128)(2,1)S(1)} async-done(((bf16[16,8,1024]{2,1,0:T(8,128)(2,1)}), bf16[16,8,1024]{2,1,0:T(8,128)(2,1)S(1)}, u32[]{:S(2)}, u32[]{:S(2)}) %all-to-all-start) | async-done | bytes 262176 | tf_op jit(solution)/shard_map/all_to_all | solution.py:36
  26.7 4.3 %all_to_all.45 = bf16[2,128,1024]{2,1,0:T(8,128)(2,1)S(1)} all-to-all(bf16[2,128,1024]{2,1,0:T(8,128)(2,1)S(1)} %broadcast_in_dim.22), channel_id=1, replica_groups=mesh['zl'=2,'y'=8,'zh'=4,'x'=4,'core'=2] {'core'}, dimensions={0} | all-to-all | bytes 1048576 | tf_op jit(solution)/shard_map/all_to_all | solution.py:36
  33.6 3.1 %collective-permute-start = (bf16[8,16,2304]{2,1,0:T(8,128)(2,1)S(1)}, bf16[8,16,2304]{2,1,0:T(8,128)(2,1)}, u32[]{:S(2)}, u32[]{:S(2)}) collective-permute-start(bf16[8,16,2304]{2,1,0:T(8,128)(2,1)S(1)} %get-tuple-element.35), channel_id=1, source_target_pairs={{0,256},{256,0},{1,257},{257,1},{2,258},{258,2},{3,259},{259,3},{4... | collective-permute-start | bytes 1769480 | tf_op jit(solution)/shard_map/ppermute | solution.py:46
  36.7 7.1 %all-to-all-start.2 = ((bf16[8,32,896]{2,1,0:T(8,128)(2,1)}), bf16[8,32,896]{2,1,0:T(8,128)(2,1)}, u32[]{:S(2)}, u32[]{:S(2)}) async-start(bf16[8,32,896]{2,1,0:T(8,128)(2,1)} %bitcast.79), calls=%async_computation.2 | async-start | bytes 917504 | tf_op jit(solution)/shard_map/all_to_all | solution.py:42
  43.8 7.2 %collective-permute-done = bf16[8,16,2304]{2,1,0:T(8,128)(2,1)} collective-permute-done((bf16[8,16,2304]{2,1,0:T(8,128)(2,1)S(1)}, bf16[8,16,2304]{2,1,0:T(8,128)(2,1)}, u32[]{:S(2)}, u32[]{:S(2)}) %collective-permute-start) | collective-permute-done | bytes 589856 | tf_op jit(solution)/shard_map/ppermute | solution.py:46
  53.0 7.0 %all-to-all-done.2 = bf16[8,32,896]{2,1,0:T(8,128)(2,1)} async-done(((bf16[8,32,896]{2,1,0:T(8,128)(2,1)}), bf16[8,32,896]{2,1,0:T(8,128)(2,1)}, u32[]{:S(2)}, u32[]{:S(2)}) %all-to-all-start.2) | async-done | bytes 458784 | tf_op jit(solution)/shard_map/all_to_all | solution.py:42
  61.1 3.5 %all-to-all-start.3 = ((bf16[8,16,2304]{2,1,0:T(8,128)(2,1)}), bf16[8,16,2304]{2,1,0:T(8,128)(2,1)S(1)}, u32[]{:S(2)}, u32[]{:S(2)}) async-start(bf16[8,16,2304]{2,1,0:T(8,128)(2,1)} %add_convert_fusion), calls=%async_computation.3 | async-start | bytes 1179648 | tf_op jit(solution)/shard_map/all_to_all | solution.py:434
  66.6 2.8 %collective-permute-start.1 = (bf16[1,16,896]{2,1,0:T(8,128)(2,1)S(1)}, bf16[1,16,896]{2,1,0:T(8,128)(2,1)S(1)}, u32[]{:S(2)}, u32[]{:S(2)}) collective-permute-start(bf16[1,16,896]{2,1,0:T(8,128)(2,1)S(1)} %dynamic-slice_bitcast_fusion), channel_id=1, source_target_pairs={{0,256},{256,0},{1,257},{257,1},{2,258},{258,2},{3,259},{259,3},{4... | collective-permute-start | bytes 86024 | tf_op jit(solution)/shard_map/ppermute | solution.py:46
  70.3 2.1 %collective-permute-done.1 = bf16[1,16,896]{2,1,0:T(8,128)(2,1)S(1)} collective-permute-done((bf16[1,16,896]{2,1,0:T(8,128)(2,1)S(1)}, bf16[1,16,896]{2,1,0:T(8,128)(2,1)S(1)}, u32[]{:S(2)}, u32[]{:S(2)}) %collective-permute-start.1) | collective-permute-done | bytes 28704 | tf_op jit(solution)/shard_map/ppermute | solution.py:46
  72.3 11.6 %all-to-all-done.3.left_parts = bf16[8,16,2304]{2,1,0:T(8,128)(2,1)S(1)} async-done(((bf16[8,16,2304]{2,1,0:T(8,128)(2,1)}), bf16[8,16,2304]{2,1,0:T(8,128)(2,1)S(1)}, u32[]{:S(2)}, u32[]{:S(2)}) %all-to-all-start.3) | async-done | bytes 589856 | tf_op jit(solution)/shard_map/all_to_all | solution.py:434
  84.9 4.2 %all-to-all-start.4 = ((bf16[8,16,2304]{2,1,0:T(8,128)(2,1)}), bf16[8,16,2304]{2,1,0:T(8,128)(2,1)}, u32[]{:S(2)}, u32[]{:S(2)}) async-start(bf16[8,16,2304]{2,1,0:T(8,128)(2,1)} %get-tuple-element.41), calls=%async_computation.4 | async-start | bytes 1179648 | tf_op jit(solution)/shard_map/all_to_all | solution.py:440
  89.2 2.7 %pad_maximum_fusion.weights = bf16[2,512,896]{2,1,0:T(8,128)(2,1)} fusion(bf16[1,512,896]{2,1,0:T(8,128)(2,1)} %bitcast.78, bf16[1,512,896]{2,1,0:T(8,128)(2,1)S(1)} %bitcast.67), kind=kLoop, calls=%fused_computation | loop fusion | flops 917504 | bytes 3670016 | tf_op jit(solution)/shard_map/stack | solution.py:406
  91.9 2.8 %collective-permute-start.2 = (bf16[1,16,896]{2,1,0:T(8,128)(2,1)S(1)}, bf16[1,16,896]{2,1,0:T(8,128)(2,1)S(1)}, u32[]{:S(2)}, u32[]{:S(2)}) collective-permute-start(bf16[1,16,896]{2,1,0:T(8,128)(2,1)S(1)} %bitcast.77), channel_id=1, source_target_pairs={{0,256},{256,0},{1,257},{257,1},{2,258},{258,2},{3,259},{259,3},{4... | collective-permute-start | bytes 86024 | tf_op jit(solution)/shard_map/ppermute | solution.py:46
  94.7 2.9 %collective-permute-done.2 = bf16[1,16,896]{2,1,0:T(8,128)(2,1)S(1)} collective-permute-done((bf16[1,16,896]{2,1,0:T(8,128)(2,1)S(1)}, bf16[1,16,896]{2,1,0:T(8,128)(2,1)S(1)}, u32[]{:S(2)}, u32[]{:S(2)}) %collective-permute-start.2) | collective-permute-done | bytes 28704 | tf_op jit(solution)/shard_map/ppermute | solution.py:46
  97.7 10.8 %all-to-all-done.4 = bf16[8,16,2304]{2,1,0:T(8,128)(2,1)} async-done(((bf16[8,16,2304]{2,1,0:T(8,128)(2,1)}), bf16[8,16,2304]{2,1,0:T(8,128)(2,1)}, u32[]{:S(2)}, u32[]{:S(2)}) %all-to-all-start.4) | async-done | bytes 589856 | tf_op jit(solution)/shard_map/all_to_all | solution.py:440
  109.3 2.8 %collective-permute-start.3 = (bf16[8,16,2304]{2,1,0:T(8,128)(2,1)}, bf16[8,16,2304]{2,1,0:T(8,128)(2,1)}, u32[]{:S(2)}, u32[]{:S(2)}) collective-permute-start(bf16[8,16,2304]{2,1,0:T(8,128)(2,1)} %all-to-all-done.4), channel_id=1, source_target_pairs={{0,256},{256,0},{1,257},{257,1},{2,258},{258,2},{3,259},{259,3},{4... | collective-permute-start | bytes 1769480 | tf_op jit(solution)/shard_map/ppermute | solution.py:46
  112.1 3.5 %all-to-all-start.5 = ((bf16[8,32,896]{2,1,0:T(8,128)(2,1)}), bf16[8,32,896]{2,1,0:T(8,128)(2,1)S(1)}, u32[]{:S(2)}, u32[]{:S(2)}) async-start(bf16[8,32,896]{2,1,0:T(8,128)(2,1)} %broadcast_in_dim.24), calls=%async_computation.5 | async-start | bytes 917504 | tf_op jit(solution)/shard_map/all_to_all | solution.py:445
  115.6 11.2 %collective-permute-done.3 = bf16[8,16,2304]{2,1,0:T(8,128)(2,1)} collective-permute-done((bf16[8,16,2304]{2,1,0:T(8,128)(2,1)}, bf16[8,16,2304]{2,1,0:T(8,128)(2,1)}, u32[]{:S(2)}, u32[]{:S(2)}) %collective-permute-start.3) | collective-permute-done | bytes 589856 | tf_op jit(solution)/shard_map/ppermute | solution.py:46
  128.3 3.5 %all-to-all-done.5 = bf16[8,32,896]{2,1,0:T(8,128)(2,1)S(1)} async-done(((bf16[8,32,896]{2,1,0:T(8,128)(2,1)}), bf16[8,32,896]{2,1,0:T(8,128)(2,1)S(1)}, u32[]{:S(2)}, u32[]{:S(2)}) %all-to-all-start.5) | async-done | bytes 458784 | tf_op jit(solution)/shard_map/all_to_all | solution.py:445
  133.3 6.4 %shard_map.235 = (bf16[2,128,1408]{2,1,0:T(8,128)(2,1)S(1)}, f32[64,896]{1,0:T(8,128)}, f32[64,896]{1,0:T(8,128)}, f32[64,896]{1,0:T(8,128)}) custom-call(bf16[256,2304]{1,0:T(8,128)(2,1)S(1)} %bitcast.65, bf16[256,896]{1,0:T(8,128)(2,1)S(1)} %bitcast.68, bf16[2,512,896]{2,1,0:T(8,128)(2,1)S(1)} %copy-done.1, ...), custom_call_target="tpu_custom_call" | custom-call | flops 1379926016 | bytes 3670016 | tf_op jit(solution)/shard_map/pallas_call | solution.py:179
  139.7 4.3 %all_to_all.46.arrived = bf16[2,128,1408]{2,1,0:T(8,128)(2,1)S(1)} all-to-all(bf16[2,128,1408]{2,1,0:T(8,128)(2,1)S(1)} %get-tuple-element.48), channel_id=1, replica_groups=mesh['zl'=2,'y'=8,'zh'=4,'x'=4,'core'=2] {'core'}, dimensions={0} | all-to-all | bytes 1441792 | tf_op jit(solution)/shard_map/all_to_all | solution.py:450
  144.2 21.0 %all_to_all.47.parts = bf16[16,8,1792]{2,1,0:T(8,128)(2,1)S(1)} all-to-all(bf16[16,8,1792]{2,1,0:T(8,128)(2,1)S(1)} %shard_map.236), channel_id=1, replica_groups=mesh['zl'=2,'y'=8,'zh'=4,'x'=4,'core'=2] {'zh','x'}, dimensions={0} | all-to-all | bytes 917504 | tf_op jit(solution)/shard_map/all_to_all | solution.py:452
  165.8 11.1 %all_to_all.48.q_parts = bf16[8,8,768]{2,1,0:T(8,128)(2,1)S(1)} all-to-all(bf16[8,8,768]{2,1,0:T(8,128)(2,1)S(1)} %get-tuple-element.51), channel_id=1, replica_groups=mesh['zl'=2,'y'=8,'zh'=4,'x'=4,'core'=2] {'y'}, dimensions={0} | all-to-all | bytes 196608 | tf_op jit(solution)/shard_map/all_to_all | solution.py:454
  (55 shorter events, 16.7 us)
Async XLA Ops:
  2.1 29.0 %copy-start.13 = (f32[512]{0:T(512)S(1)}, f32[512]{0:T(512)}, u32[]{:S(2)}) copy-start(f32[512]{0:T(512)} %param.19) | copy-start | bytes 6148
  2.1 24.6 %all-to-all-start = ((bf16[16,8,1024]{2,1,0:T(8,128)(2,1)}), bf16[16,8,1024]{2,1,0:T(8,128)(2,1)S(1)}, u32[]{:S(2)}, u32[]{:S(2)}) async-start(bf16[16,8,1024]{2,1,0:T(8,128)(2,1)} %broadcast_in_dim.21), calls=%async_computation | async-start | bytes 524288 | tf_op jit(solution)/shard_map/all_to_all | solution.py:36
  26.7 4.5 %copy-start.9 = (bf16[512,896]{1,0:T(8,128)(2,1)S(1)}, bf16[512,896]{1,0:T(8,128)(2,1)}, u32[]{:S(2)}) copy-start(bf16[512,896]{1,0:T(8,128)(2,1)} %param.22) | copy-start | bytes 2752516
  26.7 5.6 %copy-start.8 = (bf16[64,512]{1,0:T(8,128)(2,1)S(1)}, bf16[64,512]{1,0:T(8,128)(2,1)}, u32[]{:S(2)}) copy-start(bf16[64,512]{1,0:T(8,128)(2,1)} %dbd.1) | copy-start | bytes 196612
  31.0 1.3 copy-start
  31.0 1.5 copy-start.2
  31.0 1.5 copy-start.3
  31.0 1.5 copy-start.4
  31.0 1.5 copy-start.5
  31.1 1.5 copy-start.6
  31.1 1.6 copy-start.7
  33.6 17.4 %collective-permute-start = (bf16[8,16,2304]{2,1,0:T(8,128)(2,1)S(1)}, bf16[8,16,2304]{2,1,0:T(8,128)(2,1)}, u32[]{:S(2)}, u32[]{:S(2)}) collective-permute-start(bf16[8,16,2304]{2,1,0:T(8,128)(2,1)S(1)} %get-tuple-element.35), channel_id=1, source_target_pairs={{0,256},{256,0},{1,257},{257,1},{2,258},{258,2},{3,259},{259,3},{4... | collective-permute-start | bytes 1769480 | tf_op jit(solution)/shard_map/ppermute | solution.py:46
  36.7 23.4 %all-to-all-start.2 = ((bf16[8,32,896]{2,1,0:T(8,128)(2,1)}), bf16[8,32,896]{2,1,0:T(8,128)(2,1)}, u32[]{:S(2)}, u32[]{:S(2)}) async-start(bf16[8,32,896]{2,1,0:T(8,128)(2,1)} %bitcast.79), calls=%async_computation.2 | async-start | bytes 917504 | tf_op jit(solution)/shard_map/all_to_all | solution.py:42
  53.0 11.7 %copy-start.10 = (bf16[64,896]{1,0:T(8,128)(2,1)S(1)}, bf16[64,896]{1,0:T(8,128)(2,1)}, u32[]{:S(2)}) copy-start(bf16[64,896]{1,0:T(8,128)(2,1)} %param.25) | copy-start | bytes 344068
  61.1 22.8 %all-to-all-start.3 = ((bf16[8,16,2304]{2,1,0:T(8,128)(2,1)}), bf16[8,16,2304]{2,1,0:T(8,128)(2,1)S(1)}, u32[]{:S(2)}, u32[]{:S(2)}) async-start(bf16[8,16,2304]{2,1,0:T(8,128)(2,1)} %add_convert_fusion), calls=%async_computation.3 | async-start | bytes 1179648 | tf_op jit(solution)/shard_map/all_to_all | solution.py:434
  66.6 5.8 %collective-permute-start.1 = (bf16[1,16,896]{2,1,0:T(8,128)(2,1)S(1)}, bf16[1,16,896]{2,1,0:T(8,128)(2,1)S(1)}, u32[]{:S(2)}, u32[]{:S(2)}) collective-permute-start(bf16[1,16,896]{2,1,0:T(8,128)(2,1)S(1)} %dynamic-slice_bitcast_fusion), channel_id=1, source_target_pairs={{0,256},{256,0},{1,257},{257,1},{2,258},{258,2},{3,259},{259,3},{4... | collective-permute-start | bytes 86024 | tf_op jit(solution)/shard_map/ppermute | solution.py:46
  84.9 23.6 %all-to-all-start.4 = ((bf16[8,16,2304]{2,1,0:T(8,128)(2,1)}), bf16[8,16,2304]{2,1,0:T(8,128)(2,1)}, u32[]{:S(2)}, u32[]{:S(2)}) async-start(bf16[8,16,2304]{2,1,0:T(8,128)(2,1)} %get-tuple-element.41), calls=%async_computation.4 | async-start | bytes 1179648 | tf_op jit(solution)/shard_map/all_to_all | solution.py:440
  89.1 2.7 %copy-start.11 = (bf16[896,64]{0,1:T(8,128)(2,1)S(1)}, bf16[896,64]{0,1:T(8,128)(2,1)}, u32[]{:S(2)}) copy-start(bf16[896,64]{0,1:T(8,128)(2,1)} %param.28) | copy-start | bytes 344068
  89.2 2.7 %copy-start.12 = (bf16[896,64]{0,1:T(8,128)(2,1)S(1)}, bf16[896,64]{0,1:T(8,128)(2,1)}, u32[]{:S(2)}) copy-start(bf16[896,64]{0,1:T(8,128)(2,1)} %param.34) | copy-start | bytes 344068
  91.9 5.8 %collective-permute-start.2 = (bf16[1,16,896]{2,1,0:T(8,128)(2,1)S(1)}, bf16[1,16,896]{2,1,0:T(8,128)(2,1)S(1)}, u32[]{:S(2)}, u32[]{:S(2)}) collective-permute-start(bf16[1,16,896]{2,1,0:T(8,128)(2,1)S(1)} %bitcast.77), channel_id=1, source_target_pairs={{0,256},{256,0},{1,257},{257,1},{2,258},{258,2},{3,259},{259,3},{4... | collective-permute-start | bytes 86024 | tf_op jit(solution)/shard_map/ppermute | solution.py:46
  109.3 17.5 %collective-permute-start.3 = (bf16[8,16,2304]{2,1,0:T(8,128)(2,1)}, bf16[8,16,2304]{2,1,0:T(8,128)(2,1)}, u32[]{:S(2)}, u32[]{:S(2)}) collective-permute-start(bf16[8,16,2304]{2,1,0:T(8,128)(2,1)} %all-to-all-done.4), channel_id=1, source_target_pairs={{0,256},{256,0},{1,257},{257,1},{2,258},{258,2},{3,259},{259,3},{4... | collective-permute-start | bytes 1769480 | tf_op jit(solution)/shard_map/ppermute | solution.py:46
  112.1 19.7 %all-to-all-start.5 = ((bf16[8,32,896]{2,1,0:T(8,128)(2,1)}), bf16[8,32,896]{2,1,0:T(8,128)(2,1)S(1)}, u32[]{:S(2)}, u32[]{:S(2)}) async-start(bf16[8,32,896]{2,1,0:T(8,128)(2,1)} %broadcast_in_dim.24), calls=%async_computation.5 | async-start | bytes 917504 | tf_op jit(solution)/shard_map/all_to_all | solution.py:445
  131.8 1.5 copy-start.1

commit v6 on v5

--- a/solution.py
+++ b/solution.py
@@ -287,6 +287,31 @@
             flops=left_parts.size, bytes_accessed=4 * left_parts.size, transcendentals=0
         ),
     )(left_parts, right_sum)
+
+
+def pair_copies_kernel(flag, own, other, copies):
+    first = flag[0] == 0
+    mine, theirs = own[...].astype(F32), other[...].astype(F32)
+    pair = jnp.concatenate(
+        [jnp.where(first, mine, theirs), jnp.where(first, theirs, mine)], axis=0
+    ).astype(BF)
+    for k in range(copies.shape[0]):
+        copies[k] = pair
+
+
+def pair_copies(flag, own, other, peers):
+    rows, cols = own.shape
+    whole = pl.BlockSpec(memory_space=pltpu.VMEM)
+    return pl.pallas_call(
+        pair_copies_kernel,
+        out_shape=jax.ShapeDtypeStruct((peers, 2 * rows, cols), BF),
+        in_specs=[pl.BlockSpec(memory_space=pltpu.SMEM), whole, whole],
+        out_specs=whole,
+        compiler_params=pltpu.CompilerParams(vmem_limit_bytes=8 * 1024 * 1024),
+        cost_estimate=pl.CostEstimate(
+            flops=rows * cols, bytes_accessed=4 * peers * rows * cols, transcendentals=0
+        ),
+    )(flag, own, other)
 
 
 def pack_kernel(place, arrived, out, total):
@@ -428,17 +453,17 @@
         down_b,
         down_b_dir,
     )
-    right_half = reduced(right, "y").astype(BF)
+    right_parts = lax.all_to_all(right.reshape(peers, 2 * own_rows, cols), "y", 0, 0, tiled=True)
     left_half = (kept.astype(F32) + swapped(sent).astype(F32)).astype(BF)
-    left_half, right_half = lax.optimization_barrier((left_half, right_half))
+    left_half, right_parts = lax.optimization_barrier((left_half, right_parts))
     left_parts = lax.all_to_all(left_half, "y", 0, 0, tiled=True)
+    right_half = jnp.sum(right_parts.astype(F32), axis=0).astype(BF)
     right_sum = pair_sum(right_half.reshape(1, 2, own_rows, cols))[0]
     left_parts, right_sum = lax.optimization_barrier((left_parts, right_sum))
     copies, right_own = own_rows_scaled(left_parts, right_sum, 4 * rank)
 
-    right_pair = pair_join(right_own[None]).reshape(2 * own_rows, cols)
+    right_pair = pair_copies(flag, right_own, swapped(right_own), peers)
     left_line = lax.all_to_all(copies, "y", 0, 0, tiled=True)
-    right_pair = jnp.broadcast_to(right_pair, (peers, *right_pair.shape))
     left_line, right_pair, weights, out_factors, in_stack = lax.optimization_barrier(
         (left_line, right_pair, weights, out_factors, in_factors)
     )

time: 179 us -> 176 us (0.983)
  local copies, waits for them, and re-layouts: 6.29 us -> 2.78 us
    unnamed x33 -> x39, local copies, waits for them, and re-layouts: 4.6 us -> 1.89 us
    ppermute x4, waiting for transfers between devices: 23.4 us -> 21.5 us  [swapped(): return lax.ppermute(array, 'zl', [(0, 1), (1, 0)])]
  transfers between devices with their start and end apart: 9 -> 9, of which waited for: 9 -> 9; matrix products, arithmetic and copies ran while one was open for 5% -> 4% of each run, Pallas kernels for 0% -> 0%
where the time goes in v6:
time: 176 us; the launch traced here: 175 us
  waiting for transfers between devices  68.4 us (39%)
  starting transfers between devices  42.5 us (24%)
  blocking collectives  40.7 us (23%)
  Pallas kernels  11.1 us (6%)
  other arithmetic  7.83 us (4%)
  local copies, waits for them, and re-layouts  2.78 us (2%)
    ppermute x4, waiting for transfers between devices, swapped(): return lax.ppermute(array, 'zl', [(0, 1), (1, 0)])  21.5 us
    all_to_all x1, blocking collectives, on_device(): parts = lax.all_to_all(pack(place, arrived), CHIPS, 0, 0, tiled=True)  21 us
    all_to_all x1, starting transfers between devices, spread(): lax.all_to_all(copies, axis, 0, 0, tiled=True).reshape(-1, *array.shape[1:])  13.4 us
    all_to_all x1, waiting for transfers between devices, on_device(): left_line = lax.all_to_all(copies, 'y', 0, 0, tiled=True)  12.6 us
    all_to_all x1, waiting for transfers between devices, on_device(): left_parts = lax.all_to_all(left_half, 'y', 0, 0, tiled=True)  12.3 us
    ppermute x4, starting transfers between devices, swapped(): return lax.ppermute(array, 'zl', [(0, 1), (1, 0)])  11.4 us
    all_to_all x1, waiting for transfers between devices, spread(): lax.all_to_all(copies, axis, 0, 0, tiled=True).reshape(-1, *array.shape[1:])  11.2 us
    all_to_all x1, blocking collectives, on_device(): q_parts = lax.all_to_all(q_copies, 'y', 0, 0, tiled=True)  11.1 us
  transfers between devices with their start and end apart: 9, of which 9 were waited for; matrix products, arithmetic and copies ran while one was open for 4% of the time, Pallas kernels for 0%

profile of v6, /device:TPU:4, one launch (start us, length us, event | category | flops | bytes accessed | tf_op | source)
XLA Modules:
  0.0 175.4 jit_solution(6963133791051564366)
XLA Ops:
  2.1 13.4 %all-to-all-start = ((bf16[16,8,1024]{2,1,0:T(8,128)(2,1)}), bf16[16,8,1024]{2,1,0:T(8,128)(2,1)S(1)}, u32[]{:S(2)}, u32[]{:S(2)}) async-start(bf16[16,8,1024]{2,1,0:T(8,128)(2,1)} %broadcast_in_dim.15), calls=%async_computation | async-start | bytes 524288 | tf_op jit(solution)/shard_map/all_to_all | solution.py:36
  15.5 11.2 %all-to-all-done = bf16[16,8,1024]{2,1,0:T(8,128)(2,1)S(1)} async-done(((bf16[16,8,1024]{2,1,0:T(8,128)(2,1)}), bf16[16,8,1024]{2,1,0:T(8,128)(2,1)S(1)}, u32[]{:S(2)}, u32[]{:S(2)}) %all-to-all-start) | async-done | bytes 262176 | tf_op jit(solution)/shard_map/all_to_all | solution.py:36
  26.7 4.3 %all_to_all.45 = bf16[2,128,1024]{2,1,0:T(8,128)(2,1)S(1)} all-to-all(bf16[2,128,1024]{2,1,0:T(8,128)(2,1)S(1)} %broadcast_in_dim.16), channel_id=1, replica_groups=mesh['zl'=2,'y'=8,'zh'=4,'x'=4,'core'=2] {'core'}, dimensions={0} | all-to-all | bytes 1048576 | tf_op jit(solution)/shard_map/all_to_all | solution.py:36
  33.6 3.1 %collective-permute-start = (bf16[8,16,2304]{2,1,0:T(8,128)(2,1)S(1)}, bf16[8,16,2304]{2,1,0:T(8,128)(2,1)}, u32[]{:S(2)}, u32[]{:S(2)}) collective-permute-start(bf16[8,16,2304]{2,1,0:T(8,128)(2,1)S(1)} %get-tuple-element.35), channel_id=1, source_target_pairs={{0,256},{256,0},{1,257},{257,1},{2,258},{258,2},{3,259},{259,3},{4... | collective-permute-start | bytes 1769480 | tf_op jit(solution)/shard_map/ppermute | solution.py:46
  36.7 7.1 %all-to-all-start.2 = ((bf16[8,32,896]{2,1,0:T(8,128)(2,1)}), bf16[8,32,896]{2,1,0:T(8,128)(2,1)}, u32[]{:S(2)}, u32[]{:S(2)}) async-start(bf16[8,32,896]{2,1,0:T(8,128)(2,1)} %bitcast.70), calls=%async_computation.2 | async-start | bytes 917504 | tf_op jit(solution)/shard_map/all_to_all | solution.py:456
  43.8 7.2 %collective-permute-done = bf16[8,16,2304]{2,1,0:T(8,128)(2,1)} collective-permute-done((bf16[8,16,2304]{2,1,0:T(8,128)(2,1)S(1)}, bf16[8,16,2304]{2,1,0:T(8,128)(2,1)}, u32[]{:S(2)}, u32[]{:S(2)}) %collective-permute-start) | collective-permute-done | bytes 589856 | tf_op jit(solution)/shard_map/ppermute | solution.py:46
  51.0 2.0 %add_convert_fusion = bf16[8,16,2304]{2,1,0:T(8,128)(2,1)} fusion(bf16[8,16,2304]{2,1,0:T(8,128)(2,1)} %collective-permute-done, bf16[8,16,2304]{2,1,0:T(8,128)(2,1)S(1)} %get-tuple-element.34), kind=kLoop, calls=%fused_computation.3 | loop fusion | flops 1179648 | bytes 1769472 | tf_op jit(solution)/shard_map/convert_element_type | solution.py:457
  53.0 7.0 %all-to-all-done.2 = bf16[8,32,896]{2,1,0:T(8,128)(2,1)} async-done(((bf16[8,32,896]{2,1,0:T(8,128)(2,1)}), bf16[8,32,896]{2,1,0:T(8,128)(2,1)}, u32[]{:S(2)}, u32[]{:S(2)}) %all-to-all-start.2) | async-done | bytes 458784 | tf_op jit(solution)/shard_map/all_to_all | solution.py:456
  60.0 3.5 %all-to-all-start.3 = ((bf16[8,16,2304]{2,1,0:T(8,128)(2,1)}), bf16[8,16,2304]{2,1,0:T(8,128)(2,1)S(1)}, u32[]{:S(2)}, u32[]{:S(2)}) async-start(bf16[8,16,2304]{2,1,0:T(8,128)(2,1)} %add_convert_fusion), calls=%async_computation.3 | async-start | bytes 1179648 | tf_op jit(solution)/shard_map/all_to_all | solution.py:459
  64.8 2.8 %collective-permute-start.1 = (bf16[1,16,896]{2,1,0:T(8,128)(2,1)S(1)}, bf16[1,16,896]{2,1,0:T(8,128)(2,1)S(1)}, u32[]{:S(2)}, u32[]{:S(2)}) collective-permute-start(bf16[1,16,896]{2,1,0:T(8,128)(2,1)S(1)} %dynamic-slice_bitcast_fusion), channel_id=1, source_target_pairs={{0,256},{256,0},{1,257},{257,1},{2,258},{258,2},{3,259},{259,3},{4... | collective-permute-start | bytes 86024 | tf_op jit(solution)/shard_map/ppermute | solution.py:46
  67.5 2.6 %pad_maximum_fusion.weights = bf16[2,512,896]{2,1,0:T(8,128)(2,1)} fusion(bf16[1,512,896]{2,1,0:T(8,128)(2,1)} %bitcast.69, bf16[1,512,896]{2,1,0:T(8,128)(2,1)S(1)} %bitcast.59), kind=kLoop, calls=%fused_computation | loop fusion | flops 917504 | bytes 3670016 | tf_op jit(solution)/shard_map/stack | solution.py:431
  70.5 12.3 %all-to-all-done.3.left_parts = bf16[8,16,2304]{2,1,0:T(8,128)(2,1)S(1)} async-done(((bf16[8,16,2304]{2,1,0:T(8,128)(2,1)}), bf16[8,16,2304]{2,1,0:T(8,128)(2,1)S(1)}, u32[]{:S(2)}, u32[]{:S(2)}) %all-to-all-start.3) | async-done | bytes 589856 | tf_op jit(solution)/shard_map/all_to_all | solution.py:459
  83.8 3.5 %all-to-all-start.4 = ((bf16[8,16,2304]{2,1,0:T(8,128)(2,1)}), bf16[8,16,2304]{2,1,0:T(8,128)(2,1)S(1)}, u32[]{:S(2)}, u32[]{:S(2)}) async-start(bf16[8,16,2304]{2,1,0:T(8,128)(2,1)} %get-tuple-element.41), calls=%async_computation.4 | async-start | bytes 1179648 | tf_op jit(solution)/shard_map/all_to_all | solution.py:466
  87.5 2.8 %collective-permute-start.2 = (bf16[16,896]{1,0:T(8,128)(2,1)S(1)}, bf16[16,896]{1,0:T(8,128)(2,1)S(1)}, u32[]{:S(2)}, u32[]{:S(2)}) collective-permute-start(bf16[16,896]{1,0:T(8,128)(2,1)S(1)} %get-tuple-element.42.own), channel_id=1, source_target_pairs={{0,256},{256,0},{1,257},{257,1},{2,258},{258,2},{3,259},{259,3},{4... | collective-permute-start | bytes 86024 | tf_op jit(solution)/shard_map/ppermute | solution.py:46
  90.3 2.9 %collective-permute-done.2.other = bf16[16,896]{1,0:T(8,128)(2,1)S(1)} collective-permute-done((bf16[16,896]{1,0:T(8,128)(2,1)S(1)}, bf16[16,896]{1,0:T(8,128)(2,1)S(1)}, u32[]{:S(2)}, u32[]{:S(2)}) %collective-permute-start.2) | collective-permute-done | bytes 28704 | tf_op jit(solution)/shard_map/ppermute | solution.py:46
  94.1 12.6 %all-to-all-done.4 = bf16[8,16,2304]{2,1,0:T(8,128)(2,1)S(1)} async-done(((bf16[8,16,2304]{2,1,0:T(8,128)(2,1)}), bf16[8,16,2304]{2,1,0:T(8,128)(2,1)S(1)}, u32[]{:S(2)}, u32[]{:S(2)}) %all-to-all-start.4) | async-done | bytes 589856 | tf_op jit(solution)/shard_map/all_to_all | solution.py:466
  106.7 2.8 %collective-permute-start.3 = (bf16[8,16,2304]{2,1,0:T(8,128)(2,1)S(1)}, bf16[8,16,2304]{2,1,0:T(8,128)(2,1)}, u32[]{:S(2)}, u32[]{:S(2)}) collective-permute-start(bf16[8,16,2304]{2,1,0:T(8,128)(2,1)S(1)} %all-to-all-done.4), channel_id=1, source_target_pairs={{0,256},{256,0},{1,257},{257,1},{2,258},{258,2},{3,259},{259,3},{4... | collective-permute-start | bytes 1769480 | tf_op jit(solution)/shard_map/ppermute | solution.py:46
  109.4 3.5 %all-to-all-start.5 = ((bf16[8,32,896]{2,1,0:T(8,128)(2,1)}), bf16[8,32,896]{2,1,0:T(8,128)(2,1)S(1)}, u32[]{:S(2)}, u32[]{:S(2)}) async-start(bf16[8,32,896]{2,1,0:T(8,128)(2,1)} %shard_map.235), calls=%async_computation.5 | async-start | bytes 917504 | tf_op jit(solution)/shard_map/all_to_all | solution.py:470
  112.9 11.0 %collective-permute-done.3 = bf16[8,16,2304]{2,1,0:T(8,128)(2,1)} collective-permute-done((bf16[8,16,2304]{2,1,0:T(8,128)(2,1)S(1)}, bf16[8,16,2304]{2,1,0:T(8,128)(2,1)}, u32[]{:S(2)}, u32[]{:S(2)}) %collective-permute-start.3) | collective-permute-done | bytes 589856 | tf_op jit(solution)/shard_map/ppermute | solution.py:46
  125.3 3.8 %all-to-all-done.5 = bf16[8,32,896]{2,1,0:T(8,128)(2,1)S(1)} async-done(((bf16[8,32,896]{2,1,0:T(8,128)(2,1)}), bf16[8,32,896]{2,1,0:T(8,128)(2,1)S(1)}, u32[]{:S(2)}, u32[]{:S(2)}) %all-to-all-start.5) | async-done | bytes 458784 | tf_op jit(solution)/shard_map/all_to_all | solution.py:470
  130.6 6.4 %shard_map.236 = (bf16[2,128,1408]{2,1,0:T(8,128)(2,1)S(1)}, f32[64,896]{1,0:T(8,128)}, f32[64,896]{1,0:T(8,128)}, f32[64,896]{1,0:T(8,128)}) custom-call(bf16[256,2304]{1,0:T(8,128)(2,1)S(1)} %bitcast.57, bf16[256,896]{1,0:T(8,128)(2,1)S(1)} %bitcast.60, bf16[2,512,896]{2,1,0:T(8,128)(2,1)S(1)} %copy-done.1, ...), custom_call_target="tpu_custom_call" | custom-call | flops 1379926016 | bytes 3670016 | tf_op jit(solution)/shard_map/pallas_call | solution.py:179
  137.0 4.3 %all_to_all.46.arrived = bf16[2,128,1408]{2,1,0:T(8,128)(2,1)S(1)} all-to-all(bf16[2,128,1408]{2,1,0:T(8,128)(2,1)S(1)} %get-tuple-element.48), channel_id=1, replica_groups=mesh['zl'=2,'y'=8,'zh'=4,'x'=4,'core'=2] {'core'}, dimensions={0} | all-to-all | bytes 1441792 | tf_op jit(solution)/shard_map/all_to_all | solution.py:475
  141.5 21.0 %all_to_all.47.parts = bf16[16,8,1792]{2,1,0:T(8,128)(2,1)S(1)} all-to-all(bf16[16,8,1792]{2,1,0:T(8,128)(2,1)S(1)} %shard_map.237), channel_id=1, replica_groups=mesh['zl'=2,'y'=8,'zh'=4,'x'=4,'core'=2] {'zh','x'}, dimensions={0} | all-to-all | bytes 917504 | tf_op jit(solution)/shard_map/all_to_all | solution.py:477
  163.1 11.1 %all_to_all.48.q_parts = bf16[8,8,768]{2,1,0:T(8,128)(2,1)S(1)} all-to-all(bf16[8,8,768]{2,1,0:T(8,128)(2,1)S(1)} %get-tuple-element.51), channel_id=1, replica_groups=mesh['zl'=2,'y'=8,'zh'=4,'x'=4,'core'=2] {'y'}, dimensions={0} | all-to-all | bytes 196608 | tf_op jit(solution)/shard_map/all_to_all | solution.py:479
  (59 shorter events, 12.2 us)
Async XLA Ops:
  2.1 29.0 %copy-start.16 = (f32[512]{0:T(512)S(1)}, f32[512]{0:T(512)}, u32[]{:S(2)}) copy-start(f32[512]{0:T(512)} %param.19) | copy-start | bytes 6148
  2.1 24.6 %all-to-all-start = ((bf16[16,8,1024]{2,1,0:T(8,128)(2,1)}), bf16[16,8,1024]{2,1,0:T(8,128)(2,1)S(1)}, u32[]{:S(2)}, u32[]{:S(2)}) async-start(bf16[16,8,1024]{2,1,0:T(8,128)(2,1)} %broadcast_in_dim.15), calls=%async_computation | async-start | bytes 524288 | tf_op jit(solution)/shard_map/all_to_all | solution.py:36
  26.7 4.5 %copy-start.9 = (bf16[512,896]{1,0:T(8,128)(2,1)S(1)}, bf16[512,896]{1,0:T(8,128)(2,1)}, u32[]{:S(2)}) copy-start(bf16[512,896]{1,0:T(8,128)(2,1)} %param.22) | copy-start | bytes 2752516
  26.7 5.7 %copy-start.8 = (bf16[64,512]{1,0:T(8,128)(2,1)S(1)}, bf16[64,512]{1,0:T(8,128)(2,1)}, u32[]{:S(2)}) copy-start(bf16[64,512]{1,0:T(8,128)(2,1)} %dbd.1) | copy-start | bytes 196612
  31.0 1.5 copy-start.3
  31.0 1.5 copy-start.4
  31.0 1.5 copy-start.5
  31.1 1.5 copy-start.6
  31.1 1.6 copy-start.7
  33.6 17.4 %collective-permute-start = (bf16[8,16,2304]{2,1,0:T(8,128)(2,1)S(1)}, bf16[8,16,2304]{2,1,0:T(8,128)(2,1)}, u32[]{:S(2)}, u32[]{:S(2)}) collective-permute-start(bf16[8,16,2304]{2,1,0:T(8,128)(2,1)S(1)} %get-tuple-element.35), channel_id=1, source_target_pairs={{0,256},{256,0},{1,257},{257,1},{2,258},{258,2},{3,259},{259,3},{4... | collective-permute-start | bytes 1769480 | tf_op jit(solution)/shard_map/ppermute | solution.py:46
  36.7 23.4 %all-to-all-start.2 = ((bf16[8,32,896]{2,1,0:T(8,128)(2,1)}), bf16[8,32,896]{2,1,0:T(8,128)(2,1)}, u32[]{:S(2)}, u32[]{:S(2)}) async-start(bf16[8,32,896]{2,1,0:T(8,128)(2,1)} %bitcast.70), calls=%async_computation.2 | async-start | bytes 917504 | tf_op jit(solution)/shard_map/all_to_all | solution.py:456
  51.0 12.6 %copy-start.10 = (bf16[64,896]{1,0:T(8,128)(2,1)S(1)}, bf16[64,896]{1,0:T(8,128)(2,1)}, u32[]{:S(2)}) copy-start(bf16[64,896]{1,0:T(8,128)(2,1)} %param.25) | copy-start | bytes 344068
  51.0 12.6 %copy-start.11 = (bf16[64,896]{1,0:T(8,128)(2,1)S(1)}, bf16[64,896]{1,0:T(8,128)(2,1)}, u32[]{:S(2)}) copy-start(bf16[64,896]{1,0:T(8,128)(2,1)} %param.31) | copy-start | bytes 344068
  60.0 22.8 %all-to-all-start.3 = ((bf16[8,16,2304]{2,1,0:T(8,128)(2,1)}), bf16[8,16,2304]{2,1,0:T(8,128)(2,1)S(1)}, u32[]{:S(2)}, u32[]{:S(2)}) async-start(bf16[8,16,2304]{2,1,0:T(8,128)(2,1)} %add_convert_fusion), calls=%async_computation.3 | async-start | bytes 1179648 | tf_op jit(solution)/shard_map/all_to_all | solution.py:459
  64.8 5.8 %collective-permute-start.1 = (bf16[1,16,896]{2,1,0:T(8,128)(2,1)S(1)}, bf16[1,16,896]{2,1,0:T(8,128)(2,1)S(1)}, u32[]{:S(2)}, u32[]{:S(2)}) collective-permute-start(bf16[1,16,896]{2,1,0:T(8,128)(2,1)S(1)} %dynamic-slice_bitcast_fusion), channel_id=1, source_target_pairs={{0,256},{256,0},{1,257},{257,1},{2,258},{258,2},{3,259},{259,3},{4... | collective-permute-start | bytes 86024 | tf_op jit(solution)/shard_map/ppermute | solution.py:46
  70.2 17.2 %copy-start.12 = (bf16[64,896]{1,0:T(8,128)(2,1)S(1)}, bf16[64,896]{1,0:T(8,128)(2,1)}, u32[]{:S(2)}) copy-start(bf16[64,896]{1,0:T(8,128)(2,1)} %param.27) | copy-start | bytes 344068
  70.2 17.2 %copy-start.13 = (bf16[64,896]{1,0:T(8,128)(2,1)S(1)}, bf16[64,896]{1,0:T(8,128)(2,1)}, u32[]{:S(2)}) copy-start(bf16[64,896]{1,0:T(8,128)(2,1)} %param.33) | copy-start | bytes 344068
  70.2 17.3 %copy-start.14 = (bf16[896,64]{0,1:T(8,128)(2,1)S(1)}, bf16[896,64]{0,1:T(8,128)(2,1)}, u32[]{:S(2)}) copy-start(bf16[896,64]{0,1:T(8,128)(2,1)} %param.28) | copy-start | bytes 344068
  70.5 16.9 %copy-start.15 = (bf16[896,64]{0,1:T(8,128)(2,1)S(1)}, bf16[896,64]{0,1:T(8,128)(2,1)}, u32[]{:S(2)}) copy-start(bf16[896,64]{0,1:T(8,128)(2,1)} %param.34) | copy-start | bytes 344068
  83.8 22.8 %all-to-all-start.4 = ((bf16[8,16,2304]{2,1,0:T(8,128)(2,1)}), bf16[8,16,2304]{2,1,0:T(8,128)(2,1)S(1)}, u32[]{:S(2)}, u32[]{:S(2)}) async-start(bf16[8,16,2304]{2,1,0:T(8,128)(2,1)} %get-tuple-element.41), calls=%async_computation.4 | async-start | bytes 1179648 | tf_op jit(solution)/shard_map/all_to_all | solution.py:466
  87.5 5.8 %collective-permute-start.2 = (bf16[16,896]{1,0:T(8,128)(2,1)S(1)}, bf16[16,896]{1,0:T(8,128)(2,1)S(1)}, u32[]{:S(2)}, u32[]{:S(2)}) collective-permute-start(bf16[16,896]{1,0:T(8,128)(2,1)S(1)} %get-tuple-element.42.own), channel_id=1, source_target_pairs={{0,256},{256,0},{1,257},{257,1},{2,258},{258,2},{3,259},{259,3},{4... | collective-permute-start | bytes 86024 | tf_op jit(solution)/shard_map/ppermute | solution.py:46
  106.7 17.2 %collective-permute-start.3 = (bf16[8,16,2304]{2,1,0:T(8,128)(2,1)S(1)}, bf16[8,16,2304]{2,1,0:T(8,128)(2,1)}, u32[]{:S(2)}, u32[]{:S(2)}) collective-permute-start(bf16[8,16,2304]{2,1,0:T(8,128)(2,1)S(1)} %all-to-all-done.4), channel_id=1, source_target_pairs={{0,256},{256,0},{1,257},{257,1},{2,258},{258,2},{3,259},{259,3},{4... | collective-permute-start | bytes 1769480 | tf_op jit(solution)/shard_map/ppermute | solution.py:46
  109.4 19.7 %all-to-all-start.5 = ((bf16[8,32,896]{2,1,0:T(8,128)(2,1)}), bf16[8,32,896]{2,1,0:T(8,128)(2,1)S(1)}, u32[]{:S(2)}, u32[]{:S(2)}) async-start(bf16[8,32,896]{2,1,0:T(8,128)(2,1)} %shard_map.235), calls=%async_computation.5 | async-start | bytes 917504 | tf_op jit(solution)/shard_map/all_to_all | solution.py:470
  129.1 1.5 copy-start.1
  (2 other events, 2.8 us)

commit v7 on v6

--- a/solution.py
+++ b/solution.py
@@ -82,9 +82,11 @@
 
 
 def adapter_terms(pair, plain, direction):
-    rank = plain.shape[0]
-    term = SCALE * nn(pair[:, :rank], plain)
-    return term, SCALE * nn(pair, jnp.concatenate([direction, plain], axis=0))
+    both = [
+        jnp.concatenate([plain, jnp.zeros_like(plain)], axis=0),
+        jnp.concatenate([direction, plain], axis=0),
+    ]
+    return SCALE * nn(pair, jnp.concatenate(both, axis=1))
 
 
 def back_kernel(
@@ -115,9 +117,7 @@
         here = pl.ds(pl.multiple_of(block * LANES, LANES), LANES)
         at_adj = pl.ds(pl.multiple_of(cols + block * LANES, LANES), LANES)
         for k in range(3):
-            term, tan = adapter_terms(pairs[k], factors[2 * k, :, here], factors[2 * k + 1, :, here])
-            terms[2 * k] = term
-            terms[2 * k + 1] = tan
+            terms[k] = adapter_terms(pairs[k], factors[2 * k, :, here], factors[2 * k + 1, :, here])
         for chunk in range(tokens // CHUNK):
             r = pl.ds(chunk * CHUNK, CHUNK)
             (
@@ -128,12 +128,12 @@
                 d_gate_dir[r, here],
                 d_up_dir[r, here],
             ) = second_order(
-                full[r, here].astype(F32) + terms[0, r, :],
-                up_full[r, here].astype(F32) + terms[2, r, :],
-                full[r, at_adj].astype(F32) + terms[4, r, :],
-                terms[1, r, :],
-                terms[3, r, :],
-                terms[5, r, :],
+                full[r, here].astype(F32) + terms[0, r, :LANES],
+                up_full[r, here].astype(F32) + terms[1, r, :LANES],
+                full[r, at_adj].astype(F32) + terms[2, r, :LANES],
+                terms[0, r, LANES:],
+                terms[1, r, LANES:],
+                terms[2, r, LANES:],
             )
         return carry
 
@@ -186,7 +186,7 @@
         ),
         in_specs=[whole] * 5,
         out_specs=[whole] * 4,
-        scratch_shapes=[pltpu.VMEM((6, tokens, LANES), F32)] + [panel] * 6,
+        scratch_shapes=[pltpu.VMEM((3, tokens, 2 * LANES), F32)] + [panel] * 6,
         compiler_params=pltpu.CompilerParams(vmem_limit_bytes=16 * 1024 * 1024),
         cost_estimate=pl.CostEstimate(
             flops=2 * tokens * cols * (4 * rows + 15 * rank),
@@ -196,9 +196,12 @@
     )(full, up_full, weights, factors, in_factors)
 
 
-def spread_kernel(flag, scaled, panel, gate_w, down_w, gi, gid, ui, uid, db, dbd, kept, sent):
+def spread_kernel(
+    flag, scaled, panel, gate_w, up_w, down_w, gi, gid, ui, uid, db, dbd, kept, sent
+):
     rows, cols = gate_w.shape
     peers, own_rows = kept.shape[:2]
+    early = 3 * cols + 6 * gi.shape[0] + LANES - kept.shape[2]
     tokens_f = panel[:, :rows].astype(F32)
     squares = jnp.sum(tokens_f * tokens_f, axis=1, keepdims=True)
     high = squares.astype(BF).astype(F32)
@@ -215,7 +218,8 @@
     x, cot = scaled[...], panel[:, rows:]
     put(nn(x, gate_w[...]), 0)
     put(nt(cot, down_w[...]), cols)
-    at = 2 * cols
+    put(nn(x, up_w[:, early:]), 2 * cols)
+    at = 3 * cols - early
     for left, factors in ((x, (gi, gid)), (x, (ui, uid)), (cot, (db, dbd))):
         both = jnp.concatenate([factors[0][...], factors[1][...]], axis=0)
         put(nt(left, both), at)
@@ -223,30 +227,34 @@
     put(jnp.where(lane == 0, high, jnp.where(lane == 1, squares - high, 0.0)), at)
 
 
-def forward(flag, scaled, panel, gate_w, down_w, peers, *factors):
-    tokens = scaled.shape[0]
+def forward(flag, scaled, panel, gate_w, up_w, down_w, peers, early, *factors):
+    tokens = panel.shape[0]
     rows, cols = gate_w.shape
     rank = factors[0].shape[0]
     whole = pl.BlockSpec(memory_space=pltpu.VMEM)
     half = jax.ShapeDtypeStruct(
-        (peers, tokens // (2 * peers), 2 * cols + 6 * rank + LANES), BF
+        (peers, tokens // (2 * peers), 3 * cols - early + 6 * rank + LANES), BF
     )
     return pl.pallas_call(
         spread_kernel,
-        out_shape=(half, half),
-        in_specs=[pl.BlockSpec(memory_space=pltpu.SMEM)] + [whole] * (4 + len(factors)),
+        out_shape=(
+            half,
+            half,
+        ),
+        in_specs=[pl.BlockSpec(memory_space=pltpu.SMEM)] + [whole] * (5 + len(factors)),
         out_specs=[whole] * 2,
         compiler_params=pltpu.CompilerParams(vmem_limit_bytes=20 * 1024 * 1024),
         cost_estimate=pl.CostEstimate(
-            flops=4 * tokens * rows * (cols + 3 * rank),
-            bytes_accessed=4 * rows * cols,
+            flops=6 * tokens * rows * (cols + 2 * rank),
+            bytes_accessed=6 * rows * cols,
             transcendentals=0,
         ),
-    )(flag, scaled, panel, gate_w, down_w, *factors)
+    )(flag, scaled, panel, gate_w, up_w, down_w, *factors)
 
 
 def own_kernel(normed_ranks, left_parts, right_sum, copies, right_own):
-    cols = right_sum.shape[1]
+    cols = right_own.shape[1]
+    early = right_sum.shape[1]
     total = left_parts[0].astype(F32)
     for k in range(1, left_parts.shape[0]):
         total += left_parts[k].astype(F32)
@@ -256,11 +264,11 @@
     high = inv_rms.astype(BF).astype(F32)
     lane = lax.broadcasted_iota(jnp.int32, (total.shape[0], LANES), 1)
     scale = jnp.where(lane == 0, high, jnp.where(lane == 1, inv_rms - high, 0.0))
-    low = 2 * cols
+    low = 3 * cols - early
     own = jnp.concatenate(
         [
             total[:, :cols] * inv_rms,
-            total[:, cols:low],
+            total[:, cols : 2 * cols],
             total[:, low : low + normed_ranks] * inv_rms,
             total[:, low + normed_ranks : at],
             scale,
@@ -269,16 +277,19 @@
     ).astype(BF)
     for k in range(copies.shape[0]):
         copies[k] = own
-    right_own[...] = (right_sum[...] * inv_rms).astype(BF)
-
-
-def own_rows_scaled(left_parts, right_sum, normed_ranks):
+    up = jnp.concatenate([right_sum[...], total[:, 2 * cols : low]], axis=1)
+    right_own[...] = (up * inv_rms).astype(BF)
+
+
+def own_rows_scaled(left_parts, right_sum, cols, normed_ranks):
+    peers, rows, width = left_parts.shape
+    rest = cols - right_sum.shape[1]
     whole = pl.BlockSpec(memory_space=pltpu.VMEM)
     return pl.pallas_call(
         functools.partial(own_kernel, normed_ranks),
         out_shape=(
-            jax.ShapeDtypeStruct(left_parts.shape, BF),
-            jax.ShapeDtypeStruct(right_sum.shape, BF),
+            jax.ShapeDtypeStruct((peers, rows, width - rest), BF),
+            jax.ShapeDtypeStruct((rows, cols), BF),
         ),
         in_specs=[whole] * 2,
         out_specs=[whole] * 2,
@@ -433,19 +444,22 @@
     in_factors = jnp.stack([gate_in.T, up_in.T, gate_in_dir.T, up_in_dir.T])
     own = jnp.concatenate([tokens, cotangent], axis=1)
     panel = spread(spread(own, CHIPS), "core")
+    peers = lax.axis_size("y")
+    own_rows = panel.shape[0] // (2 * peers)
+    early = cols * 4 // 7
+    flag = jnp.full((1,), lax.axis_index("zl"), jnp.int32)
     scaled = (panel[:, :rows].astype(F32) * norm_gain).astype(BF)
-    right = nn(scaled, up_w).astype(BF)
+    right = nn(scaled, up_w[:, :early]).astype(BF)
     scaled, right = lax.optimization_barrier((scaled, right))
-    peers = lax.axis_size("y")
-    own_rows = right.shape[0] // (2 * peers)
-    flag = jnp.full((1,), lax.axis_index("zl"), jnp.int32)
     kept, sent = forward(
         flag,
         scaled,
         panel,
         gate_w,
+        up_w,
         down_w,
         peers,
+        early,
         in_factors[0],
         in_factors[2],
         in_factors[1],
@@ -453,14 +467,14 @@
         down_b,
         down_b_dir,
     )
-    right_parts = lax.all_to_all(right.reshape(peers, 2 * own_rows, cols), "y", 0, 0, tiled=True)
+    right_parts = lax.all_to_all(right.reshape(peers, 2 * own_rows, early), "y", 0, 0, tiled=True)
     left_half = (kept.astype(F32) + swapped(sent).astype(F32)).astype(BF)
     left_half, right_parts = lax.optimization_barrier((left_half, right_parts))
     left_parts = lax.all_to_all(left_half, "y", 0, 0, tiled=True)
     right_half = jnp.sum(right_parts.astype(F32), axis=0).astype(BF)
-    right_sum = pair_sum(right_half.reshape(1, 2, own_rows, cols))[0]
+    right_sum = pair_sum(right_half.reshape(1, 2, own_rows, early))[0]
     left_parts, right_sum = lax.optimization_barrier((left_parts, right_sum))
-    copies, right_own = own_rows_scaled(left_parts, right_sum, 4 * rank)
+    copies, right_own = own_rows_scaled(left_parts, right_sum, cols, 4 * rank)
 
     right_pair = pair_copies(flag, right_own, swapped(right_own), peers)
     left_line = lax.all_to_all(copies, "y", 0, 0, tiled=True)

time: 176 us -> 178 us (1.011)
  the two profiles are of different devices: /device:TPU:4 before, /device:TPU:1 now
where the time goes in v7:
time: 178 us; the launch traced here: 177 us
  waiting for transfers between devices  59.6 us (33%)
  starting transfers between devices  46.8 us (26%)
  blocking collectives  40.6 us (23%)
  Pallas kernels  13.2 us (7%)
  local copies, waits for them, and re-layouts  8.18 us (5%)
  other arithmetic  6.32 us (4%)
    ppermute x4, waiting for transfers between devices, swapped(): return lax.ppermute(array, 'zl', [(0, 1), (1, 0)])  20.4 us
    all_to_all x1, blocking collectives, on_device(): parts = lax.all_to_all(pack(place, arrived), CHIPS, 0, 0, tiled=True)  18.7 us
    all_to_all x1, starting transfers between devices, spread(): lax.all_to_all(copies, axis, 0, 0, tiled=True).reshape(-1, *array.shape[1:])  13.6 us
    ppermute x4, starting transfers between devices, swapped(): return lax.ppermute(array, 'zl', [(0, 1), (1, 0)])  12.6 us
    all_to_all x1, waiting for transfers between devices, on_device(): left_parts = lax.all_to_all(left_half, 'y', 0, 0, tiled=True)  11.7 us
    all_to_all x1, waiting for transfers between devices, on_device(): left_line = lax.all_to_all(copies, 'y', 0, 0, tiled=True)  10.9 us
    all_to_all x1, waiting for transfers between devices, spread(): lax.all_to_all(copies, axis, 0, 0, tiled=True).reshape(-1, *array.shape[1:])  10.1 us
    all_to_all x1, blocking collectives, on_device(): q_parts = lax.all_to_all(q_copies, 'y', 0, 0, tiled=True)  10 us
  transfers between devices with their start and end apart: 9, of which 8 were waited for; matrix products, arithmetic and copies ran while one was open for 6% of the time, Pallas kernels for 0%

profile of v7, /device:TPU:1, one launch (start us, length us, event | category | flops | bytes accessed | tf_op | source)
XLA Modules:
  0.0 176.6 jit_solution(4629807298139690781)
XLA Ops:
  2.1 13.6 %all-to-all-start = ((bf16[16,8,1024]{2,1,0:T(8,128)(2,1)}), bf16[16,8,1024]{2,1,0:T(8,128)(2,1)S(1)}, u32[]{:S(2)}, u32[]{:S(2)}) async-start(bf16[16,8,1024]{2,1,0:T(8,128)(2,1)} %broadcast_in_dim.15), calls=%async_computation | async-start | bytes 524288 | tf_op jit(solution)/shard_map/all_to_all | solution.py:36
  15.6 10.1 %all-to-all-done = bf16[16,8,1024]{2,1,0:T(8,128)(2,1)S(1)} async-done(((bf16[16,8,1024]{2,1,0:T(8,128)(2,1)}), bf16[16,8,1024]{2,1,0:T(8,128)(2,1)S(1)}, u32[]{:S(2)}, u32[]{:S(2)}) %all-to-all-start) | async-done | bytes 262176 | tf_op jit(solution)/shard_map/all_to_all | solution.py:36
  25.9 7.4 %all_to_all.45 = bf16[2,128,1024]{2,1,0:T(8,128)(2,1)S(1)} all-to-all(bf16[2,128,1024]{2,1,0:T(8,128)(2,1)S(1)} %broadcast_in_dim.16), channel_id=1, replica_groups=mesh['zl'=2,'y'=8,'zh'=4,'x'=4,'core'=2] {'core'}, dimensions={0} | all-to-all | bytes 1048576 | tf_op jit(solution)/shard_map/all_to_all | solution.py:36
  34.4 1.9 %shard_map.233 = (bf16[8,16,2688]{2,1,0:T(8,128)(2,1)S(1)}, bf16[8,16,2688]{2,1,0:T(8,128)(2,1)}) custom-call(s32[1]{0:T(128)} %bitcast.1.flag, bf16[256,512]{1,0:T(8,128)(2,1)S(1)} %multiply_convert_fusion.scaled, bf16[256,1024]{1,0:T(8,128)(2,1)S(1)} %bitcast.54, bf16[512,896]{1,0:T(8,128)(2,1)S(1)} %copy-done, bf16[512,896]{1,0:T(8,128)(2,1)S(1)} %copy-done.1, ...), custom_call_target="tpu_custom_call" | custom-call | flops 805306368 | bytes 2752512 | tf_op jit(solution)/shard_map/pallas_call | solution.py:238
  36.3 3.1 %collective-permute-start = (bf16[8,16,2688]{2,1,0:T(8,128)(2,1)}, bf16[8,16,2688]{2,1,0:T(8,128)(2,1)}, u32[]{:S(2)}, u32[]{:S(2)}) collective-permute-start(bf16[8,16,2688]{2,1,0:T(8,128)(2,1)} %get-tuple-element.35), channel_id=1, source_target_pairs={{0,256},{256,0},{1,257},{257,1},{2,258},{258,2},{3,259},{259,3},{4... | collective-permute-start | bytes 2064392 | tf_op jit(solution)/shard_map/ppermute | solution.py:46
  39.5 6.8 %all-to-all-start.2 = ((bf16[8,32,512]{2,1,0:T(8,128)(2,1)}), bf16[8,32,512]{2,1,0:T(8,128)(2,1)}, u32[]{:S(2)}, u32[]{:S(2)}) async-start(bf16[8,32,512]{2,1,0:T(8,128)(2,1)} %bitcast.70), calls=%async_computation.2 | async-start | bytes 524288 | tf_op jit(solution)/shard_map/all_to_all | solution.py:470
  46.3 8.9 %collective-permute-done = bf16[8,16,2688]{2,1,0:T(8,128)(2,1)} collective-permute-done((bf16[8,16,2688]{2,1,0:T(8,128)(2,1)}, bf16[8,16,2688]{2,1,0:T(8,128)(2,1)}, u32[]{:S(2)}, u32[]{:S(2)}) %collective-permute-start) | collective-permute-done | bytes 688160 | tf_op jit(solution)/shard_map/ppermute | solution.py:46
  55.2 2.1 %add_convert_fusion = bf16[8,16,2688]{2,1,0:T(8,128)(2,1)} fusion(bf16[8,16,2688]{2,1,0:T(8,128)(2,1)} %collective-permute-done, bf16[8,16,2688]{2,1,0:T(8,128)(2,1)S(1)} %get-tuple-element.34), kind=kLoop, calls=%fused_computation.1 | loop fusion | flops 1376256 | bytes 2064384 | tf_op jit(solution)/shard_map/convert_element_type | solution.py:471
  57.3 6.8 %all-to-all-start.3 = ((bf16[8,16,2688]{2,1,0:T(8,128)(2,1)}), bf16[8,16,2688]{2,1,0:T(8,128)(2,1)S(1)}, u32[]{:S(2)}, u32[]{:S(2)}) async-start(bf16[8,16,2688]{2,1,0:T(8,128)(2,1)} %add_convert_fusion), calls=%async_computation.3 | async-start | bytes 1376256 | tf_op jit(solution)/shard_map/all_to_all | solution.py:473
  64.1 1.6 bitcast_dynamic-update-slice_fusion.5
  68.2 3.2 %collective-permute-start.1 = (bf16[1,16,512]{2,1,0:T(8,128)(2,1)S(1)}, bf16[1,16,512]{2,1,0:T(8,128)(2,1)}, u32[]{:S(2)}, u32[]{:S(2)}) collective-permute-start(bf16[1,16,512]{2,1,0:T(8,128)(2,1)S(1)} %dynamic-slice_bitcast_fusion), channel_id=1, source_target_pairs={{0,256},{256,0},{1,257},{257,1},{2,258},{258,2},{3,259},{259,3},{4... | collective-permute-start | bytes 49160 | tf_op jit(solution)/shard_map/ppermute | solution.py:46
  73.8 11.7 %all-to-all-done.3.left_parts = bf16[8,16,2688]{2,1,0:T(8,128)(2,1)S(1)} async-done(((bf16[8,16,2688]{2,1,0:T(8,128)(2,1)}), bf16[8,16,2688]{2,1,0:T(8,128)(2,1)S(1)}, u32[]{:S(2)}, u32[]{:S(2)}) %all-to-all-start.3) | async-done | bytes 688160 | tf_op jit(solution)/shard_map/all_to_all | solution.py:473
  86.5 3.5 %all-to-all-start.4 = ((bf16[8,16,2304]{2,1,0:T(8,128)(2,1)}), bf16[8,16,2304]{2,1,0:T(8,128)(2,1)S(1)}, u32[]{:S(2)}, u32[]{:S(2)}) async-start(bf16[8,16,2304]{2,1,0:T(8,128)(2,1)} %get-tuple-element.41), calls=%async_computation.4 | async-start | bytes 1179648 | tf_op jit(solution)/shard_map/all_to_all | solution.py:480
  92.7 3.1 %collective-permute-start.2 = (bf16[16,896]{1,0:T(8,128)(2,1)S(1)}, bf16[16,896]{1,0:T(8,128)(2,1)S(1)}, u32[]{:S(2)}, u32[]{:S(2)}) collective-permute-start(bf16[16,896]{1,0:T(8,128)(2,1)S(1)} %get-tuple-element.42.own), channel_id=1, source_target_pairs={{0,256},{256,0},{1,257},{257,1},{2,258},{258,2},{3,259},{259,3},{4... | collective-permute-start | bytes 86024 | tf_op jit(solution)/shard_map/ppermute | solution.py:46
  95.9 1.7 collective-permute-done.2.other
  98.4 10.9 %all-to-all-done.4 = bf16[8,16,2304]{2,1,0:T(8,128)(2,1)S(1)} async-done(((bf16[8,16,2304]{2,1,0:T(8,128)(2,1)}), bf16[8,16,2304]{2,1,0:T(8,128)(2,1)S(1)}, u32[]{:S(2)}, u32[]{:S(2)}) %all-to-all-start.4) | async-done | bytes 589856 | tf_op jit(solution)/shard_map/all_to_all | solution.py:480
  109.3 3.1 %collective-permute-start.3 = (bf16[8,16,2304]{2,1,0:T(8,128)(2,1)S(1)}, bf16[8,16,2304]{2,1,0:T(8,128)(2,1)S(1)}, u32[]{:S(2)}, u32[]{:S(2)}) collective-permute-start(bf16[8,16,2304]{2,1,0:T(8,128)(2,1)S(1)} %all-to-all-done.4), channel_id=1, source_target_pairs={{0,256},{256,0},{1,257},{257,1},{2,258},{258,2},{3,259},{259,3},{4... | collective-permute-start | bytes 1769480 | tf_op jit(solution)/shard_map/ppermute | solution.py:46
  112.5 3.5 %all-to-all-start.5 = ((bf16[8,32,896]{2,1,0:T(8,128)(2,1)}), bf16[8,32,896]{2,1,0:T(8,128)(2,1)S(1)}, u32[]{:S(2)}, u32[]{:S(2)}) async-start(bf16[8,32,896]{2,1,0:T(8,128)(2,1)} %shard_map.235), calls=%async_computation.5 | async-start | bytes 917504 | tf_op jit(solution)/shard_map/all_to_all | solution.py:484
  115.9 9.6 %collective-permute-done.3 = bf16[8,16,2304]{2,1,0:T(8,128)(2,1)S(1)} collective-permute-done((bf16[8,16,2304]{2,1,0:T(8,128)(2,1)S(1)}, bf16[8,16,2304]{2,1,0:T(8,128)(2,1)S(1)}, u32[]{:S(2)}, u32[]{:S(2)}) %collective-permute-start.3) | collective-permute-done | bytes 589856 | tf_op jit(solution)/shard_map/ppermute | solution.py:46
  125.9 6.5 %all-to-all-done.5 = bf16[8,32,896]{2,1,0:T(8,128)(2,1)S(1)} async-done(((bf16[8,32,896]{2,1,0:T(8,128)(2,1)}), bf16[8,32,896]{2,1,0:T(8,128)(2,1)S(1)}, u32[]{:S(2)}, u32[]{:S(2)}) %all-to-all-start.5) | async-done | bytes 458784 | tf_op jit(solution)/shard_map/all_to_all | solution.py:484
  133.9 7.6 %shard_map.236 = (bf16[2,128,1408]{2,1,0:T(8,128)(2,1)S(1)}, f32[64,896]{1,0:T(8,128)}, f32[64,896]{1,0:T(8,128)}, f32[64,896]{1,0:T(8,128)}) custom-call(bf16[256,2304]{1,0:T(8,128)(2,1)S(1)} %bitcast.56, bf16[256,896]{1,0:T(8,128)(2,1)S(1)} %bitcast.60, bf16[2,512,896]{2,1,0:T(8,128)(2,1)S(1)} %copy-done.2, ...), custom_call_target="tpu_custom_call" | custom-call | flops 1379926016 | bytes 3670016 | tf_op jit(solution)/shard_map/pallas_call | solution.py:179
  141.5 4.4 %all_to_all.46.arrived = bf16[2,128,1408]{2,1,0:T(8,128)(2,1)S(1)} all-to-all(bf16[2,128,1408]{2,1,0:T(8,128)(2,1)S(1)} %get-tuple-element.48), channel_id=1, replica_groups=mesh['zl'=2,'y'=8,'zh'=4,'x'=4,'core'=2] {'core'}, dimensions={0} | all-to-all | bytes 1441792 | tf_op jit(solution)/shard_map/all_to_all | solution.py:489
  146.0 18.7 %all_to_all.47.parts = bf16[16,8,1792]{2,1,0:T(8,128)(2,1)S(1)} all-to-all(bf16[16,8,1792]{2,1,0:T(8,128)(2,1)S(1)} %shard_map.237), channel_id=1, replica_groups=mesh['zl'=2,'y'=8,'zh'=4,'x'=4,'core'=2] {'zh','x'}, dimensions={0} | all-to-all | bytes 917504 | tf_op jit(solution)/shard_map/all_to_all | solution.py:491
  165.4 10.0 %all_to_all.48.q_parts = bf16[8,8,768]{2,1,0:T(8,128)(2,1)S(1)} all-to-all(bf16[8,8,768]{2,1,0:T(8,128)(2,1)S(1)} %get-tuple-element.51), channel_id=1, replica_groups=mesh['zl'=2,'y'=8,'zh'=4,'x'=4,'core'=2] {'y'}, dimensions={0} | all-to-all | bytes 196608 | tf_op jit(solution)/shard_map/all_to_all | solution.py:493
  (57 shorter events, 15.7 us)
Async XLA Ops:
  0.6 32.7 %copy-start.15 = (f32[512]{0:T(512)S(1)}, f32[512]{0:T(512)}, u32[]{:S(2)}) copy-start(f32[512]{0:T(512)} %param.19) | copy-start | bytes 6148
  2.1 31.3 %copy-start.1 = (bf16[512,896]{1,0:T(8,128)(2,1)S(1)}, bf16[512,896]{1,0:T(8,128)(2,1)}, u32[]{:S(2)}) copy-start(bf16[512,896]{1,0:T(8,128)(2,1)} %up_w.1) | copy-start | bytes 2752516
  2.1 23.6 %all-to-all-start = ((bf16[16,8,1024]{2,1,0:T(8,128)(2,1)}), bf16[16,8,1024]{2,1,0:T(8,128)(2,1)S(1)}, u32[]{:S(2)}, u32[]{:S(2)}) async-start(bf16[16,8,1024]{2,1,0:T(8,128)(2,1)} %broadcast_in_dim.15), calls=%async_computation | async-start | bytes 524288 | tf_op jit(solution)/shard_map/all_to_all | solution.py:36
  25.8 8.6 %copy-start = (bf16[512,896]{1,0:T(8,128)(2,1)S(1)}, bf16[512,896]{1,0:T(8,128)(2,1)}, u32[]{:S(2)}) copy-start(bf16[512,896]{1,0:T(8,128)(2,1)} %gate_w.1) | copy-start | bytes 2752516
  25.8 8.6 %copy-start.3 = (bf16[896,512]{1,0:T(8,128)(2,1)S(1)}, bf16[896,512]{1,0:T(8,128)(2,1)}, u32[]{:S(2)}) copy-start(bf16[896,512]{1,0:T(8,128)(2,1)} %down_w.1) | copy-start | bytes 2752516
  25.8 8.5 %copy-start.4 = (bf16[512,64]{0,1:T(8,128)(2,1)S(1)}, bf16[512,64]{0,1:T(8,128)(2,1)}, u32[]{:S(2)}) copy-start(bf16[512,64]{0,1:T(8,128)(2,1)} %param.24) | copy-start | bytes 196612
  25.8 8.5 %copy-start.5 = (bf16[512,64]{0,1:T(8,128)(2,1)S(1)}, bf16[512,64]{0,1:T(8,128)(2,1)}, u32[]{:S(2)}) copy-start(bf16[512,64]{0,1:T(8,128)(2,1)} %param.30) | copy-start | bytes 196612
  25.8 8.5 %copy-start.6 = (bf16[512,64]{0,1:T(8,128)(2,1)S(1)}, bf16[512,64]{0,1:T(8,128)(2,1)}, u32[]{:S(2)}) copy-start(bf16[512,64]{0,1:T(8,128)(2,1)} %param.26) | copy-start | bytes 196612
  25.8 8.5 %copy-start.7 = (bf16[512,64]{0,1:T(8,128)(2,1)S(1)}, bf16[512,64]{0,1:T(8,128)(2,1)}, u32[]{:S(2)}) copy-start(bf16[512,64]{0,1:T(8,128)(2,1)} %param.32) | copy-start | bytes 196612
  25.9 8.5 %copy-start.9 = (bf16[64,512]{1,0:T(8,128)(2,1)S(1)}, bf16[64,512]{1,0:T(8,128)(2,1)}, u32[]{:S(2)}) copy-start(bf16[64,512]{1,0:T(8,128)(2,1)} %db.1) | copy-start | bytes 196612
  25.9 8.5 %copy-start.10 = (bf16[64,512]{1,0:T(8,128)(2,1)S(1)}, bf16[64,512]{1,0:T(8,128)(2,1)}, u32[]{:S(2)}) copy-start(bf16[64,512]{1,0:T(8,128)(2,1)} %dbd.1) | copy-start | bytes 196612
  36.3 18.8 %collective-permute-start = (bf16[8,16,2688]{2,1,0:T(8,128)(2,1)}, bf16[8,16,2688]{2,1,0:T(8,128)(2,1)}, u32[]{:S(2)}, u32[]{:S(2)}) collective-permute-start(bf16[8,16,2688]{2,1,0:T(8,128)(2,1)} %get-tuple-element.35), channel_id=1, source_target_pairs={{0,256},{256,0},{1,257},{257,1},{2,258},{258,2},{3,259},{259,3},{4... | collective-permute-start | bytes 2064392 | tf_op jit(solution)/shard_map/ppermute | solution.py:46
  39.5 17.8 %all-to-all-start.2 = ((bf16[8,32,512]{2,1,0:T(8,128)(2,1)}), bf16[8,32,512]{2,1,0:T(8,128)(2,1)}, u32[]{:S(2)}, u32[]{:S(2)}) async-start(bf16[8,32,512]{2,1,0:T(8,128)(2,1)} %bitcast.70), calls=%async_computation.2 | async-start | bytes 524288 | tf_op jit(solution)/shard_map/all_to_all | solution.py:470
  57.3 28.2 %all-to-all-start.3 = ((bf16[8,16,2688]{2,1,0:T(8,128)(2,1)}), bf16[8,16,2688]{2,1,0:T(8,128)(2,1)S(1)}, u32[]{:S(2)}, u32[]{:S(2)}) async-start(bf16[8,16,2688]{2,1,0:T(8,128)(2,1)} %add_convert_fusion), calls=%async_computation.3 | async-start | bytes 1376256 | tf_op jit(solution)/shard_map/all_to_all | solution.py:473
  68.2 4.8 %collective-permute-start.1 = (bf16[1,16,512]{2,1,0:T(8,128)(2,1)S(1)}, bf16[1,16,512]{2,1,0:T(8,128)(2,1)}, u32[]{:S(2)}, u32[]{:S(2)}) collective-permute-start(bf16[1,16,512]{2,1,0:T(8,128)(2,1)S(1)} %dynamic-slice_bitcast_fusion), channel_id=1, source_target_pairs={{0,256},{256,0},{1,257},{257,1},{2,258},{258,2},{3,259},{259,3},{4... | collective-permute-start | bytes 49160 | tf_op jit(solution)/shard_map/ppermute | solution.py:46
  72.8 17.2 %copy-start.11 = (bf16[64,896]{1,0:T(8,128)(2,1)S(1)}, bf16[64,896]{1,0:T(8,128)(2,1)}, u32[]{:S(2)}) copy-start(bf16[64,896]{1,0:T(8,128)(2,1)} %param.27) | copy-start | bytes 344068
  72.8 17.9 %copy-start.12 = (bf16[64,896]{1,0:T(8,128)(2,1)S(1)}, bf16[64,896]{1,0:T(8,128)(2,1)}, u32[]{:S(2)}) copy-start(bf16[64,896]{1,0:T(8,128)(2,1)} %param.33) | copy-start | bytes 344068
  72.8 18.5 %copy-start.13 = (bf16[896,64]{0,1:T(8,128)(2,1)S(1)}, bf16[896,64]{0,1:T(8,128)(2,1)}, u32[]{:S(2)}) copy-start(bf16[896,64]{0,1:T(8,128)(2,1)} %param.28) | copy-start | bytes 344068
  72.8 19.2 %copy-start.14 = (bf16[896,64]{0,1:T(8,128)(2,1)S(1)}, bf16[896,64]{0,1:T(8,128)(2,1)}, u32[]{:S(2)}) copy-start(bf16[896,64]{0,1:T(8,128)(2,1)} %param.34) | copy-start | bytes 344068
  73.8 22.1 %copy-start.8 = (bf16[512,64]{0,1:T(8,128)(2,1)S(1)}, bf16[512,64]{0,1:T(8,128)(2,1)}, u32[]{:S(2)}) copy-start(bf16[512,64]{0,1:T(8,128)(2,1)} %param.32) | copy-start | bytes 196612
  86.5 22.8 %all-to-all-start.4 = ((bf16[8,16,2304]{2,1,0:T(8,128)(2,1)}), bf16[8,16,2304]{2,1,0:T(8,128)(2,1)S(1)}, u32[]{:S(2)}, u32[]{:S(2)}) async-start(bf16[8,16,2304]{2,1,0:T(8,128)(2,1)} %get-tuple-element.41), calls=%async_computation.4 | async-start | bytes 1179648 | tf_op jit(solution)/shard_map/all_to_all | solution.py:480
  92.7 4.9 %collective-permute-start.2 = (bf16[16,896]{1,0:T(8,128)(2,1)S(1)}, bf16[16,896]{1,0:T(8,128)(2,1)S(1)}, u32[]{:S(2)}, u32[]{:S(2)}) collective-permute-start(bf16[16,896]{1,0:T(8,128)(2,1)S(1)} %get-tuple-element.42.own), channel_id=1, source_target_pairs={{0,256},{256,0},{1,257},{257,1},{2,258},{258,2},{3,259},{259,3},{4... | collective-permute-start | bytes 86024 | tf_op jit(solution)/shard_map/ppermute | solution.py:46
  109.3 16.3 %collective-permute-start.3 = (bf16[8,16,2304]{2,1,0:T(8,128)(2,1)S(1)}, bf16[8,16,2304]{2,1,0:T(8,128)(2,1)S(1)}, u32[]{:S(2)}, u32[]{:S(2)}) collective-permute-start(bf16[8,16,2304]{2,1,0:T(8,128)(2,1)S(1)} %all-to-all-done.4), channel_id=1, source_target_pairs={{0,256},{256,0},{1,257},{257,1},{2,258},{258,2},{3,259},{259,3},{4... | collective-permute-start | bytes 1769480 | tf_op jit(solution)/shard_map/ppermute | solution.py:46
  112.5 20.0 %all-to-all-start.5 = ((bf16[8,32,896]{2,1,0:T(8,128)(2,1)}), bf16[8,32,896]{2,1,0:T(8,128)(2,1)S(1)}, u32[]{:S(2)}, u32[]{:S(2)}) async-start(bf16[8,32,896]{2,1,0:T(8,128)(2,1)} %shard_map.235), calls=%async_computation.5 | async-start | bytes 917504 | tf_op jit(solution)/shard_map/all_to_all | solution.py:484
  (1 other events, 1.5 us)

commit v8 on v6

--- a/solution.py
+++ b/solution.py
@@ -142,9 +142,11 @@
     h, hd = hidden[...], hidden_dir[...]
     gw, uw = weights[0], weights[1]
     go, god, uo, uod, di, did = [factors[k] for k in range(6)]
-    q_gate, q_up = nt(dg, go), nt(du, uo)
-    q_gate_dir = nt(dgd, go) + nt(dg, god)
-    q_up_dir = nt(dud, uo) + nt(du, uod)
+    both_gate = nt(dg, jnp.concatenate([go, god], axis=0))
+    both_up = nt(du, jnp.concatenate([uo, uod], axis=0))
+    q_gate, q_up = both_gate[:, :rank], both_up[:, :rank]
+    q_gate_dir = nt(dgd, go) + both_gate[:, rank:]
+    q_up_dir = nt(dud, uo) + both_up[:, rank:]
     q_all = jnp.concatenate([q_gate_dir, q_up_dir, nt(hd, di) + nt(h, did)], axis=1) * SCALE
     gi, ui, gid, uid = [in_factors[k] for k in range(4)]
     qg, qu = (SCALE * q_gate).astype(BF), (SCALE * q_up).astype(BF)

time: 176 us -> 176 us (level)
  no operation moved by 1% of the time
where the time goes in v8:
time: 176 us; the launch traced here: 175 us
  waiting for transfers between devices  68.4 us (39%)
  starting transfers between devices  42.5 us (24%)
  blocking collectives  40.7 us (23%)
  Pallas kernels  10.9 us (6%)
  other arithmetic  7.83 us (4%)
  local copies, waits for them, and re-layouts  2.78 us (2%)
    ppermute x4, waiting for transfers between devices, swapped(): return lax.ppermute(array, 'zl', [(0, 1), (1, 0)])  21.5 us
    all_to_all x1, blocking collectives, on_device(): parts = lax.all_to_all(pack(place, arrived), CHIPS, 0, 0, tiled=True)  21 us
    all_to_all x1, starting transfers between devices, spread(): lax.all_to_all(copies, axis, 0, 0, tiled=True).reshape(-1, *array.shape[1:])  13.4 us
    all_to_all x1, waiting for transfers between devices, on_device(): left_line = lax.all_to_all(copies, 'y', 0, 0, tiled=True)  12.6 us
    all_to_all x1, waiting for transfers between devices, on_device(): left_parts = lax.all_to_all(left_half, 'y', 0, 0, tiled=True)  12.3 us
    ppermute x4, starting transfers between devices, swapped(): return lax.ppermute(array, 'zl', [(0, 1), (1, 0)])  11.4 us
    all_to_all x1, waiting for transfers between devices, spread(): lax.all_to_all(copies, axis, 0, 0, tiled=True).reshape(-1, *array.shape[1:])  11.2 us
    all_to_all x1, blocking collectives, on_device(): q_parts = lax.all_to_all(q_copies, 'y', 0, 0, tiled=True)  11.1 us
  transfers between devices with their start and end apart: 9, of which 9 were waited for; matrix products, arithmetic and copies ran while one was open for 4% of the time, Pallas kernels for 0%

profile of v8, /device:TPU:4, one launch (start us, length us, event | category | flops | bytes accessed | tf_op | source)
XLA Modules:
  0.0 175.1 jit_solution(3709028832302391266)
XLA Ops:
  2.1 13.4 %all-to-all-start = ((bf16[16,8,1024]{2,1,0:T(8,128)(2,1)}), bf16[16,8,1024]{2,1,0:T(8,128)(2,1)S(1)}, u32[]{:S(2)}, u32[]{:S(2)}) async-start(bf16[16,8,1024]{2,1,0:T(8,128)(2,1)} %broadcast_in_dim.15), calls=%async_computation | async-start | bytes 524288 | tf_op jit(solution)/shard_map/all_to_all | solution.py:36
  15.5 11.2 %all-to-all-done = bf16[16,8,1024]{2,1,0:T(8,128)(2,1)S(1)} async-done(((bf16[16,8,1024]{2,1,0:T(8,128)(2,1)}), bf16[16,8,1024]{2,1,0:T(8,128)(2,1)S(1)}, u32[]{:S(2)}, u32[]{:S(2)}) %all-to-all-start) | async-done | bytes 262176 | tf_op jit(solution)/shard_map/all_to_all | solution.py:36
  26.7 4.3 %all_to_all.45 = bf16[2,128,1024]{2,1,0:T(8,128)(2,1)S(1)} all-to-all(bf16[2,128,1024]{2,1,0:T(8,128)(2,1)S(1)} %broadcast_in_dim.16), channel_id=1, replica_groups=mesh['zl'=2,'y'=8,'zh'=4,'x'=4,'core'=2] {'core'}, dimensions={0} | all-to-all | bytes 1048576 | tf_op jit(solution)/shard_map/all_to_all | solution.py:36
  33.6 3.1 %collective-permute-start = (bf16[8,16,2304]{2,1,0:T(8,128)(2,1)S(1)}, bf16[8,16,2304]{2,1,0:T(8,128)(2,1)}, u32[]{:S(2)}, u32[]{:S(2)}) collective-permute-start(bf16[8,16,2304]{2,1,0:T(8,128)(2,1)S(1)} %get-tuple-element.35), channel_id=1, source_target_pairs={{0,256},{256,0},{1,257},{257,1},{2,258},{258,2},{3,259},{259,3},{4... | collective-permute-start | bytes 1769480 | tf_op jit(solution)/shard_map/ppermute | solution.py:46
  36.7 7.1 %all-to-all-start.2 = ((bf16[8,32,896]{2,1,0:T(8,128)(2,1)}), bf16[8,32,896]{2,1,0:T(8,128)(2,1)}, u32[]{:S(2)}, u32[]{:S(2)}) async-start(bf16[8,32,896]{2,1,0:T(8,128)(2,1)} %bitcast.70), calls=%async_computation.2 | async-start | bytes 917504 | tf_op jit(solution)/shard_map/all_to_all | solution.py:458
  43.8 7.2 %collective-permute-done = bf16[8,16,2304]{2,1,0:T(8,128)(2,1)} collective-permute-done((bf16[8,16,2304]{2,1,0:T(8,128)(2,1)S(1)}, bf16[8,16,2304]{2,1,0:T(8,128)(2,1)}, u32[]{:S(2)}, u32[]{:S(2)}) %collective-permute-start) | collective-permute-done | bytes 589856 | tf_op jit(solution)/shard_map/ppermute | solution.py:46
  51.0 2.0 %add_convert_fusion = bf16[8,16,2304]{2,1,0:T(8,128)(2,1)} fusion(bf16[8,16,2304]{2,1,0:T(8,128)(2,1)} %collective-permute-done, bf16[8,16,2304]{2,1,0:T(8,128)(2,1)S(1)} %get-tuple-element.34), kind=kLoop, calls=%fused_computation.3 | loop fusion | flops 1179648 | bytes 1769472 | tf_op jit(solution)/shard_map/convert_element_type | solution.py:459
  53.0 7.0 %all-to-all-done.2 = bf16[8,32,896]{2,1,0:T(8,128)(2,1)} async-done(((bf16[8,32,896]{2,1,0:T(8,128)(2,1)}), bf16[8,32,896]{2,1,0:T(8,128)(2,1)}, u32[]{:S(2)}, u32[]{:S(2)}) %all-to-all-start.2) | async-done | bytes 458784 | tf_op jit(solution)/shard_map/all_to_all | solution.py:458
  60.0 3.5 %all-to-all-start.3 = ((bf16[8,16,2304]{2,1,0:T(8,128)(2,1)}), bf16[8,16,2304]{2,1,0:T(8,128)(2,1)S(1)}, u32[]{:S(2)}, u32[]{:S(2)}) async-start(bf16[8,16,2304]{2,1,0:T(8,128)(2,1)} %add_convert_fusion), calls=%async_computation.3 | async-start | bytes 1179648 | tf_op jit(solution)/shard_map/all_to_all | solution.py:461
  64.8 2.8 %collective-permute-start.1 = (bf16[1,16,896]{2,1,0:T(8,128)(2,1)S(1)}, bf16[1,16,896]{2,1,0:T(8,128)(2,1)S(1)}, u32[]{:S(2)}, u32[]{:S(2)}) collective-permute-start(bf16[1,16,896]{2,1,0:T(8,128)(2,1)S(1)} %dynamic-slice_bitcast_fusion), channel_id=1, source_target_pairs={{0,256},{256,0},{1,257},{257,1},{2,258},{258,2},{3,259},{259,3},{4... | collective-permute-start | bytes 86024 | tf_op jit(solution)/shard_map/ppermute | solution.py:46
  67.5 2.6 %pad_maximum_fusion.weights = bf16[2,512,896]{2,1,0:T(8,128)(2,1)} fusion(bf16[1,512,896]{2,1,0:T(8,128)(2,1)} %bitcast.69, bf16[1,512,896]{2,1,0:T(8,128)(2,1)S(1)} %bitcast.59), kind=kLoop, calls=%fused_computation | loop fusion | flops 917504 | bytes 3670016 | tf_op jit(solution)/shard_map/stack | solution.py:433
  70.5 12.3 %all-to-all-done.3.left_parts = bf16[8,16,2304]{2,1,0:T(8,128)(2,1)S(1)} async-done(((bf16[8,16,2304]{2,1,0:T(8,128)(2,1)}), bf16[8,16,2304]{2,1,0:T(8,128)(2,1)S(1)}, u32[]{:S(2)}, u32[]{:S(2)}) %all-to-all-start.3) | async-done | bytes 589856 | tf_op jit(solution)/shard_map/all_to_all | solution.py:461
  83.8 3.5 %all-to-all-start.4 = ((bf16[8,16,2304]{2,1,0:T(8,128)(2,1)}), bf16[8,16,2304]{2,1,0:T(8,128)(2,1)S(1)}, u32[]{:S(2)}, u32[]{:S(2)}) async-start(bf16[8,16,2304]{2,1,0:T(8,128)(2,1)} %get-tuple-element.41), calls=%async_computation.4 | async-start | bytes 1179648 | tf_op jit(solution)/shard_map/all_to_all | solution.py:468
  87.5 2.8 %collective-permute-start.2 = (bf16[16,896]{1,0:T(8,128)(2,1)S(1)}, bf16[16,896]{1,0:T(8,128)(2,1)S(1)}, u32[]{:S(2)}, u32[]{:S(2)}) collective-permute-start(bf16[16,896]{1,0:T(8,128)(2,1)S(1)} %get-tuple-element.42.own), channel_id=1, source_target_pairs={{0,256},{256,0},{1,257},{257,1},{2,258},{258,2},{3,259},{259,3},{4... | collective-permute-start | bytes 86024 | tf_op jit(solution)/shard_map/ppermute | solution.py:46
  90.3 2.9 %collective-permute-done.2.other = bf16[16,896]{1,0:T(8,128)(2,1)S(1)} collective-permute-done((bf16[16,896]{1,0:T(8,128)(2,1)S(1)}, bf16[16,896]{1,0:T(8,128)(2,1)S(1)}, u32[]{:S(2)}, u32[]{:S(2)}) %collective-permute-start.2) | collective-permute-done | bytes 28704 | tf_op jit(solution)/shard_map/ppermute | solution.py:46
  94.1 12.6 %all-to-all-done.4 = bf16[8,16,2304]{2,1,0:T(8,128)(2,1)S(1)} async-done(((bf16[8,16,2304]{2,1,0:T(8,128)(2,1)}), bf16[8,16,2304]{2,1,0:T(8,128)(2,1)S(1)}, u32[]{:S(2)}, u32[]{:S(2)}) %all-to-all-start.4) | async-done | bytes 589856 | tf_op jit(solution)/shard_map/all_to_all | solution.py:468
  106.7 2.8 %collective-permute-start.3 = (bf16[8,16,2304]{2,1,0:T(8,128)(2,1)S(1)}, bf16[8,16,2304]{2,1,0:T(8,128)(2,1)}, u32[]{:S(2)}, u32[]{:S(2)}) collective-permute-start(bf16[8,16,2304]{2,1,0:T(8,128)(2,1)S(1)} %all-to-all-done.4), channel_id=1, source_target_pairs={{0,256},{256,0},{1,257},{257,1},{2,258},{258,2},{3,259},{259,3},{4... | collective-permute-start | bytes 1769480 | tf_op jit(solution)/shard_map/ppermute | solution.py:46
  109.4 3.5 %all-to-all-start.5 = ((bf16[8,32,896]{2,1,0:T(8,128)(2,1)}), bf16[8,32,896]{2,1,0:T(8,128)(2,1)S(1)}, u32[]{:S(2)}, u32[]{:S(2)}) async-start(bf16[8,32,896]{2,1,0:T(8,128)(2,1)} %shard_map.235), calls=%async_computation.5 | async-start | bytes 917504 | tf_op jit(solution)/shard_map/all_to_all | solution.py:472
  112.9 11.0 %collective-permute-done.3 = bf16[8,16,2304]{2,1,0:T(8,128)(2,1)} collective-permute-done((bf16[8,16,2304]{2,1,0:T(8,128)(2,1)S(1)}, bf16[8,16,2304]{2,1,0:T(8,128)(2,1)}, u32[]{:S(2)}, u32[]{:S(2)}) %collective-permute-start.3) | collective-permute-done | bytes 589856 | tf_op jit(solution)/shard_map/ppermute | solution.py:46
  125.3 3.8 %all-to-all-done.5 = bf16[8,32,896]{2,1,0:T(8,128)(2,1)S(1)} async-done(((bf16[8,32,896]{2,1,0:T(8,128)(2,1)}), bf16[8,32,896]{2,1,0:T(8,128)(2,1)S(1)}, u32[]{:S(2)}, u32[]{:S(2)}) %all-to-all-start.5) | async-done | bytes 458784 | tf_op jit(solution)/shard_map/all_to_all | solution.py:472
  130.6 6.2 %shard_map.236 = (bf16[2,128,1408]{2,1,0:T(8,128)(2,1)S(1)}, f32[64,896]{1,0:T(8,128)}, f32[64,896]{1,0:T(8,128)}, f32[64,896]{1,0:T(8,128)}) custom-call(bf16[256,2304]{1,0:T(8,128)(2,1)S(1)} %bitcast.57, bf16[256,896]{1,0:T(8,128)(2,1)S(1)} %bitcast.60, bf16[2,512,896]{2,1,0:T(8,128)(2,1)S(1)} %copy-done.1, ...), custom_call_target="tpu_custom_call" | custom-call | flops 1379926016 | bytes 3670016 | tf_op jit(solution)/shard_map/pallas_call | solution.py:181
  136.8 4.3 %all_to_all.46.arrived = bf16[2,128,1408]{2,1,0:T(8,128)(2,1)S(1)} all-to-all(bf16[2,128,1408]{2,1,0:T(8,128)(2,1)S(1)} %get-tuple-element.48), channel_id=1, replica_groups=mesh['zl'=2,'y'=8,'zh'=4,'x'=4,'core'=2] {'core'}, dimensions={0} | all-to-all | bytes 1441792 | tf_op jit(solution)/shard_map/all_to_all | solution.py:477
  141.3 21.0 %all_to_all.47.parts = bf16[16,8,1792]{2,1,0:T(8,128)(2,1)S(1)} all-to-all(bf16[16,8,1792]{2,1,0:T(8,128)(2,1)S(1)} %shard_map.237), channel_id=1, replica_groups=mesh['zl'=2,'y'=8,'zh'=4,'x'=4,'core'=2] {'zh','x'}, dimensions={0} | all-to-all | bytes 917504 | tf_op jit(solution)/shard_map/all_to_all | solution.py:479
  162.9 11.1 %all_to_all.48.q_parts = bf16[8,8,768]{2,1,0:T(8,128)(2,1)S(1)} all-to-all(bf16[8,8,768]{2,1,0:T(8,128)(2,1)S(1)} %get-tuple-element.51), channel_id=1, replica_groups=mesh['zl'=2,'y'=8,'zh'=4,'x'=4,'core'=2] {'y'}, dimensions={0} | all-to-all | bytes 196608 | tf_op jit(solution)/shard_map/all_to_all | solution.py:481
  (59 shorter events, 12.2 us)
Async XLA Ops:
  2.1 29.0 %copy-start.16 = (f32[512]{0:T(512)S(1)}, f32[512]{0:T(512)}, u32[]{:S(2)}) copy-start(f32[512]{0:T(512)} %param.19) | copy-start | bytes 6148
  2.1 24.6 %all-to-all-start = ((bf16[16,8,1024]{2,1,0:T(8,128)(2,1)}), bf16[16,8,1024]{2,1,0:T(8,128)(2,1)S(1)}, u32[]{:S(2)}, u32[]{:S(2)}) async-start(bf16[16,8,1024]{2,1,0:T(8,128)(2,1)} %broadcast_in_dim.15), calls=%async_computation | async-start | bytes 524288 | tf_op jit(solution)/shard_map/all_to_all | solution.py:36
  26.7 4.5 %copy-start.9 = (bf16[512,896]{1,0:T(8,128)(2,1)S(1)}, bf16[512,896]{1,0:T(8,128)(2,1)}, u32[]{:S(2)}) copy-start(bf16[512,896]{1,0:T(8,128)(2,1)} %param.22) | copy-start | bytes 2752516
  26.7 5.7 %copy-start.8 = (bf16[64,512]{1,0:T(8,128)(2,1)S(1)}, bf16[64,512]{1,0:T(8,128)(2,1)}, u32[]{:S(2)}) copy-start(bf16[64,512]{1,0:T(8,128)(2,1)} %dbd.1) | copy-start | bytes 196612
  31.0 1.5 copy-start.3
  31.0 1.5 copy-start.4
  31.0 1.5 copy-start.5
  31.1 1.5 copy-start.6
  31.1 1.6 copy-start.7
  33.6 17.4 %collective-permute-start = (bf16[8,16,2304]{2,1,0:T(8,128)(2,1)S(1)}, bf16[8,16,2304]{2,1,0:T(8,128)(2,1)}, u32[]{:S(2)}, u32[]{:S(2)}) collective-permute-start(bf16[8,16,2304]{2,1,0:T(8,128)(2,1)S(1)} %get-tuple-element.35), channel_id=1, source_target_pairs={{0,256},{256,0},{1,257},{257,1},{2,258},{258,2},{3,259},{259,3},{4... | collective-permute-start | bytes 1769480 | tf_op jit(solution)/shard_map/ppermute | solution.py:46
  36.7 23.4 %all-to-all-start.2 = ((bf16[8,32,896]{2,1,0:T(8,128)(2,1)}), bf16[8,32,896]{2,1,0:T(8,128)(2,1)}, u32[]{:S(2)}, u32[]{:S(2)}) async-start(bf16[8,32,896]{2,1,0:T(8,128)(2,1)} %bitcast.70), calls=%async_computation.2 | async-start | bytes 917504 | tf_op jit(solution)/shard_map/all_to_all | solution.py:458
  51.0 12.6 %copy-start.10 = (bf16[64,896]{1,0:T(8,128)(2,1)S(1)}, bf16[64,896]{1,0:T(8,128)(2,1)}, u32[]{:S(2)}) copy-start(bf16[64,896]{1,0:T(8,128)(2,1)} %param.25) | copy-start | bytes 344068
  51.0 12.6 %copy-start.11 = (bf16[64,896]{1,0:T(8,128)(2,1)S(1)}, bf16[64,896]{1,0:T(8,128)(2,1)}, u32[]{:S(2)}) copy-start(bf16[64,896]{1,0:T(8,128)(2,1)} %param.31) | copy-start | bytes 344068
  60.0 22.8 %all-to-all-start.3 = ((bf16[8,16,2304]{2,1,0:T(8,128)(2,1)}), bf16[8,16,2304]{2,1,0:T(8,128)(2,1)S(1)}, u32[]{:S(2)}, u32[]{:S(2)}) async-start(bf16[8,16,2304]{2,1,0:T(8,128)(2,1)} %add_convert_fusion), calls=%async_computation.3 | async-start | bytes 1179648 | tf_op jit(solution)/shard_map/all_to_all | solution.py:461
  64.8 5.8 %collective-permute-start.1 = (bf16[1,16,896]{2,1,0:T(8,128)(2,1)S(1)}, bf16[1,16,896]{2,1,0:T(8,128)(2,1)S(1)}, u32[]{:S(2)}, u32[]{:S(2)}) collective-permute-start(bf16[1,16,896]{2,1,0:T(8,128)(2,1)S(1)} %dynamic-slice_bitcast_fusion), channel_id=1, source_target_pairs={{0,256},{256,0},{1,257},{257,1},{2,258},{258,2},{3,259},{259,3},{4... | collective-permute-start | bytes 86024 | tf_op jit(solution)/shard_map/ppermute | solution.py:46
  70.2 17.2 %copy-start.12 = (bf16[64,896]{1,0:T(8,128)(2,1)S(1)}, bf16[64,896]{1,0:T(8,128)(2,1)}, u32[]{:S(2)}) copy-start(bf16[64,896]{1,0:T(8,128)(2,1)} %param.27) | copy-start | bytes 344068
  70.2 17.2 %copy-start.13 = (bf16[64,896]{1,0:T(8,128)(2,1)S(1)}, bf16[64,896]{1,0:T(8,128)(2,1)}, u32[]{:S(2)}) copy-start(bf16[64,896]{1,0:T(8,128)(2,1)} %param.33) | copy-start | bytes 344068
  70.2 17.3 %copy-start.14 = (bf16[896,64]{0,1:T(8,128)(2,1)S(1)}, bf16[896,64]{0,1:T(8,128)(2,1)}, u32[]{:S(2)}) copy-start(bf16[896,64]{0,1:T(8,128)(2,1)} %param.28) | copy-start | bytes 344068
  70.5 16.9 %copy-start.15 = (bf16[896,64]{0,1:T(8,128)(2,1)S(1)}, bf16[896,64]{0,1:T(8,128)(2,1)}, u32[]{:S(2)}) copy-start(bf16[896,64]{0,1:T(8,128)(2,1)} %param.34) | copy-start | bytes 344068
  83.8 22.8 %all-to-all-start.4 = ((bf16[8,16,2304]{2,1,0:T(8,128)(2,1)}), bf16[8,16,2304]{2,1,0:T(8,128)(2,1)S(1)}, u32[]{:S(2)}, u32[]{:S(2)}) async-start(bf16[8,16,2304]{2,1,0:T(8,128)(2,1)} %get-tuple-element.41), calls=%async_computation.4 | async-start | bytes 1179648 | tf_op jit(solution)/shard_map/all_to_all | solution.py:468
  87.5 5.8 %collective-permute-start.2 = (bf16[16,896]{1,0:T(8,128)(2,1)S(1)}, bf16[16,896]{1,0:T(8,128)(2,1)S(1)}, u32[]{:S(2)}, u32[]{:S(2)}) collective-permute-start(bf16[16,896]{1,0:T(8,128)(2,1)S(1)} %get-tuple-element.42.own), channel_id=1, source_target_pairs={{0,256},{256,0},{1,257},{257,1},{2,258},{258,2},{3,259},{259,3},{4... | collective-permute-start | bytes 86024 | tf_op jit(solution)/shard_map/ppermute | solution.py:46
  106.7 17.2 %collective-permute-start.3 = (bf16[8,16,2304]{2,1,0:T(8,128)(2,1)S(1)}, bf16[8,16,2304]{2,1,0:T(8,128)(2,1)}, u32[]{:S(2)}, u32[]{:S(2)}) collective-permute-start(bf16[8,16,2304]{2,1,0:T(8,128)(2,1)S(1)} %all-to-all-done.4), channel_id=1, source_target_pairs={{0,256},{256,0},{1,257},{257,1},{2,258},{258,2},{3,259},{259,3},{4... | collective-permute-start | bytes 1769480 | tf_op jit(solution)/shard_map/ppermute | solution.py:46
  109.4 19.7 %all-to-all-start.5 = ((bf16[8,32,896]{2,1,0:T(8,128)(2,1)}), bf16[8,32,896]{2,1,0:T(8,128)(2,1)S(1)}, u32[]{:S(2)}, u32[]{:S(2)}) async-start(bf16[8,32,896]{2,1,0:T(8,128)(2,1)} %shard_map.235), calls=%async_computation.5 | async-start | bytes 917504 | tf_op jit(solution)/shard_map/all_to_all | solution.py:472
  129.1 1.5 copy-start.1
  (2 other events, 2.8 us)
